TPU v7x, 32 devices: a whole 2x2x4 slice. The times are simulated.
32 devices in a mesh: pw: 4 (over y, core), band: 8 (over z, x).
Axes of the slice: x: 2, y: 2, z: 4, core: 2. Of those that a mesh axis runs over, the one named last changes fastest.
Arguments:
- psi: bfloat16 [2, 8, 24576], P(None, 'band', 'pw'), may hold values from -9 to 9
- gvec_index: int32 [24576], P('pw'), may hold values from 0 to 1769471, as said below
- vloc: float32 [192, 192, 192], P(None, 'pw'), may hold values from -3 to 1
- beta: bfloat16 [2, 72, 24576], P(None, None, 'pw'), may hold values from -0.15625 to 0.15625
- dmat: float32 [4, 18, 18], replicated, may hold values from -1 to 3
- qmat: float32 [4, 18, 18], replicated, may hold values from -1 to 2
Outputs:
- hpsi: bfloat16 [2, 8, 24576], P(None, 'band', 'pw')
- spsi: bfloat16 [2, 8, 24576], P(None, 'band', 'pw')
- gram: float32 [2, 8, 8], P(None, 'band')
Inputs may be any that keep to these rules, and one draw needn't show every extreme that they name: `gvec_index`: each entry is (x - k * 48) * 192 * 192 + y * 192 + z for the grid cell (x, y, z) of its plane wave, where k is the entry's block of 6144 plane waves and x lies in k * 48 .. (k + 1) * 48 - 1; no cell appears twice.
All inputs are finite; a program needn't handle non-finite values.
Results may differ from a plain program's by a relative error of at most 0.0069.
Values may be sent and summed in bfloat16 or wider, within the bound.
No kernel may reach another device: no remote copies, remote signals or barrier semaphores. Data moves between devices by JAX's collectives and lax.ppermute only.
A program may use at most 128 MiB of HBM per device.

v0:
```python
import functools

import jax
import jax.numpy as jnp
import ml_dtypes
import numpy as np
from jax import lax
from jax.experimental import pallas as pl
from jax.experimental.pallas import tpu as pltpu
from jax.sharding import PartitionSpec as P

LANES = 128
VMEM_LIMIT = 60 * 1024 * 1024


def round_up(value, unit):
    return -(-value // unit) * unit


def dft_parts(length):
    counter = np.arange(length)
    phase = counter[:, None] * counter[None, :] % length
    angle = phase.astype(np.float32) * np.float32(2.0 * np.pi / length)
    factor = np.float32(1.0) / np.sqrt(np.float32(length))
    return (np.cos(angle) * factor).astype(np.float32), (np.sin(angle) * factor).astype(np.float32)


def as_bf16(array):
    return np.asarray(array).astype(ml_dtypes.bfloat16)


def tables_of(length, planes, blocks):
    half = length // 2
    cosine, sine = dft_parts(length)
    rows = round_up(planes, 8)
    own = np.zeros((blocks, 2 * rows, length), np.float32)
    for block in range(blocks):
        span = slice(block * planes, (block + 1) * planes)
        own[block, :planes] = cosine[span]
        own[block, rows : rows + planes] = sine[span]
    along_z = np.stack([cosine, sine])

    def square(c, s):
        return np.block([[c, -s], [s, c]])

    along_x = np.stack(
        [
            square(cosine[:half, 0::2], sine[:half, 0::2]),
            square(cosine[:half, 1::2], sine[:half, 1::2]),
            square(cosine[0::2, :half], -sine[0::2, :half]),
            square(cosine[1::2, :half], -sine[1::2, :half]),
        ]
    )
    return as_bf16(own), as_bf16(along_z), as_bf16(along_x)


def cell_parts(index, length):
    cell = index.astype(jnp.float32)
    x = jnp.floor((cell + 0.5) * (1.0 / (length * length)))
    rest = cell - x * (length * length)
    y = jnp.floor((rest + 0.5) * (1.0 / length))
    return x, y, rest - y * length


def iota(shape, dim):
    return lax.broadcasted_iota(jnp.int32, shape, dim).astype(jnp.float32)


def where_bf16(mask, value):
    return jnp.where(mask, value, 0.0).astype(jnp.bfloat16)


def dot(left, right):
    return jnp.dot(left, right, preferred_element_type=jnp.float32)


def dot_lanes(left, right):
    return lax.dot_general(left, right, (((1,), (1,)), ((), ())), preferred_element_type=jnp.float32)


def group_kernel(length, planes, chunks, gvec_ref, psi_ref, pay_ref, slot_ref, hot, counts, spread, pick):
    waves = gvec_ref.shape[1]
    tiles = waves // LANES
    rows = round_up(planes, 16)
    x, y, z = cell_parts(gvec_ref[...], length)
    psi = psi_ref[...].astype(jnp.float32)
    plane = iota((rows, LANES), 0)
    for tile in range(tiles):
        span = slice(tile * LANES, (tile + 1) * LANES)
        hot[tile * rows : (tile + 1) * rows, :] = where_bf16(plane == x[:, span], 1.0)
    upto = jnp.where(iota((LANES, LANES), 0) <= iota((LANES, LANES), 1), 1.0, 0.0)
    upto = jnp.concatenate([upto, jnp.ones((LANES, LANES), jnp.float32)], axis=1)
    counts[...] = dot(hot[...], upto.astype(jnp.bfloat16))
    total = jnp.zeros((rows, LANES), jnp.float32)
    for tile in range(tiles):
        total = total + counts[tile * rows : (tile + 1) * rows, LANES:]
    need = jnp.maximum(jnp.floor((total + (LANES - 0.5)) * (1.0 / LANES)), 1.0)
    need = jnp.where(plane < planes, need, 0.0)
    below = where_bf16(iota((rows, rows), 1) < iota((rows, rows), 0), 1.0)
    first = dot(below, need.astype(jnp.bfloat16))
    ends = jnp.where((plane < planes) & (iota((rows, LANES), 1) >= first + need), 1.0, 0.0)
    chunk_plane = jnp.sum(ends, axis=0, keepdims=True)
    running = first * LANES - 1.0
    upper = iota((chunks, LANES), 0)
    lower = iota((LANES, LANES), 0)
    for tile in range(tiles):
        span = slice(tile * LANES, (tile + 1) * LANES)
        part = slice(tile * rows, (tile + 1) * rows)
        mine = plane == x[:, span]
        slot = jnp.where(mine, counts[part, :LANES] + running, 0.0)
        slot = jnp.sum(slot, axis=0, keepdims=True)
        running = running + counts[part, LANES:]
        slot_ref[:, span] = slot
        high = jnp.floor((slot + 0.5) * (1.0 / LANES))
        at_high = upper == high
        spread[0:chunks, span] = where_bf16(at_high, psi[0:1, span])
        spread[chunks : 2 * chunks, span] = where_bf16(at_high, psi[1:2, span])
        spread[2 * chunks : 3 * chunks, span] = where_bf16(at_high, y[:, span])
        spread[3 * chunks : 4 * chunks, span] = where_bf16(at_high, z[:, span])
        pick[:, span] = where_bf16(lower == slot - high * LANES, 1.0)
    pay_ref[0 : 4 * chunks, :] = dot_lanes(spread[...], pick[...]).astype(jnp.bfloat16)
    pay_ref[4 * chunks :, :] = jnp.broadcast_to(chunk_plane, (16, LANES)).astype(jnp.bfloat16)


def group_waves(index, psi, length, planes, chunks):
    waves = index.shape[1]
    rows = round_up(planes, 16)
    tiles = waves // LANES
    return pl.pallas_call(
        functools.partial(group_kernel, length, planes, chunks),
        out_shape=(
            jax.ShapeDtypeStruct((4 * chunks + 16, LANES), jnp.bfloat16),
            jax.ShapeDtypeStruct((1, waves), jnp.float32),
        ),
        scratch_shapes=[
            pltpu.VMEM((tiles * rows, LANES), jnp.bfloat16),
            pltpu.VMEM((tiles * rows, 2 * LANES), jnp.float32),
            pltpu.VMEM((4 * chunks, waves), jnp.bfloat16),
            pltpu.VMEM((LANES, waves), jnp.bfloat16),
        ],
        compiler_params=pltpu.CompilerParams(vmem_limit_bytes=VMEM_LIMIT),
        name="group_waves",
    )(index, psi)


def lattice_kernel(length, planes, chunks, blocks, *refs):
    pays = refs[:blocks]
    vloc_hbm, own_ref, along_z, along_x = refs[blocks : blocks + 4]
    outs = refs[blocks + 4 : 2 * blocks + 4]
    wide, cells_a, cells_b, phases, vloc, vloc_a, vloc_b, result, maps, maps_s, sems = refs[2 * blocks + 4 :]
    half = length // 2
    rows = round_up(planes, 8)
    both = 2 * rows
    spare = blocks * planes
    tail = length - LANES
    me = lax.axis_index("pw")
    load = pltpu.make_async_copy(vloc_hbm, vloc, sems.at[0])
    load.start()
    for s in range(blocks):
        maps[s * 8 : (s + 1) * 8, :] = pays[s][4 * chunks : 4 * chunks + 16, :].astype(jnp.int32)[:8]
    fetch = pltpu.make_async_copy(maps, maps_s, sems.at[1])
    fetch.start()
    for s in range(blocks):
        wide[s * 4 * chunks : (s + 1) * 4 * chunks, :] = pays[s][0 : 4 * chunks, :].astype(jnp.float32)
    own = own_ref[me]
    fetch.wait()
    used = jnp.int32(0)
    for s in range(blocks):
        used = jnp.maximum(used, lax.fori_loop(
            0, chunks, lambda c, n: n + jnp.where(maps_s[s * 8, c] < planes, 1, 0), jnp.int32(0)))
    level = iota((length, LANES), 0)
    group = 4 if blocks % 4 == 0 else 1

    def place(s, c):
        at = maps_s[s * 8, c]
        return jnp.where(at < planes, (me ^ s) * planes + at, spare)

    def row(s, part, c):
        return wide[pl.ds((s * 4 + part) * chunks + c, 1), :]

    def forward(c, _):
        for base in range(0, blocks, group):
            found = []
            for s in range(base, base + group):
                pick_y = where_bf16(level == row(s, 2, c), 1.0)
                phase = dot(own, pick_y)
                phases[s * chunks + c] = phase.astype(jnp.bfloat16)
                re, im = row(s, 0, c), row(s, 1, c)
                cos, sin = phase[:rows], phase[rows:]
                mixed = jnp.concatenate([re * cos - im * sin, re * sin + im * cos], axis=0)
                pick_z = where_bf16(level == row(s, 3, c), 1.0)
                part = dot_lanes(mixed.astype(jnp.bfloat16), pick_z)
                at = place(s, c)
                before = place(s, jnp.maximum(c - 1, 0))
                fresh = (c == 0) | (at != before)
                span = pl.ds(pl.multiple_of(at * both, 8), both)
                near = part[:, :LANES] + jnp.where(fresh, 0.0, cells_a[span, :])
                far = part[:, LANES:] + jnp.where(fresh, 0.0, cells_b[span, :tail])
                found.append((span, near, far))
            for span, near, far in found:
                cells_a[span, :] = near
                cells_b[span, :tail] = far
        return 0

    lax.fori_loop(0, used, forward, 0)
    load.wait()
    vloc_a[...] = vloc[:, :LANES]
    vloc_b[:, :tail] = vloc[:, LANES:]

    def strided(first, second, start, stride):
        span = pl.ds(start, half, stride=stride)
        return jnp.concatenate([first[span, :], second[span, :][:, :tail]], axis=1)

    def push(start, value):
        span = pl.ds(start, half, stride=2 * both)
        cells_a[span, :] = value[:, :LANES]
        cells_b[span, :] = jnp.concatenate([value[:, LANES:], jnp.zeros((half, LANES - tail), jnp.float32)], axis=1)

    def middle(k, _):
        def pull(start):
            return strided(cells_a, cells_b, start, 2 * both)

        re = jnp.concatenate([pull(k), pull(k + both)], axis=0).astype(jnp.bfloat16)
        im = jnp.concatenate([pull(k + rows), pull(k + rows + both)], axis=0).astype(jnp.bfloat16)
        cos, sin = along_z[0], along_z[1]
        zre = (dot(re, cos) - dot(im, sin)).astype(jnp.bfloat16)
        zim = (dot(re, sin) + dot(im, cos)).astype(jnp.bfloat16)
        even = dot(along_x[0], jnp.concatenate([zre[:half], zim[:half]], axis=0))
        odd = dot(along_x[1], jnp.concatenate([zre[half:], zim[half:]], axis=0))
        near = strided(vloc_a, vloc_b, k, planes)
        far = strided(vloc_a, vloc_b, k + half * planes, planes)
        first = (even + odd) * jnp.concatenate([near, near], axis=0)
        second = (even - odd) * jnp.concatenate([far, far], axis=0)
        even = dot(along_x[2], (first + second).astype(jnp.bfloat16)).astype(jnp.bfloat16)
        odd = dot(along_x[3], (first - second).astype(jnp.bfloat16)).astype(jnp.bfloat16)
        re = jnp.concatenate([even[:half], odd[:half]], axis=0)
        im = jnp.concatenate([even[half:], odd[half:]], axis=0)
        zre = dot(re, cos) + dot(im, sin)
        zim = dot(im, cos) - dot(re, sin)
        push(k, zre[:half])
        push(k + both, zre[half:])
        push(k + rows, zim[:half])
        push(k + rows + both, zim[half:])
        return 0

    lax.fori_loop(0, planes, middle, 0)

    def backward(c, _):
        for base in range(0, blocks, group):
            found = []
            for s in range(base, base + group):
                at = place(s, c)
                span = pl.ds(pl.multiple_of(at * both, 8), both)
                pick_z = where_bf16(level == row(s, 3, c), 1.0)
                part = jnp.concatenate([cells_a[span, :], cells_b[span, :tail]], axis=1)
                part = dot(part.astype(jnp.bfloat16), pick_z)
                phase = phases[s * chunks + c].astype(jnp.float32)
                re, im = part[:rows], part[rows:]
                cos, sin = phase[:rows], phase[rows:]
                found.append((jnp.sum(re * cos + im * sin, axis=0, keepdims=True),
                              jnp.sum(im * cos - re * sin, axis=0, keepdims=True)))
            for s, (re, im) in zip(range(base, base + group), found):
                result[pl.ds(s * 2 * chunks + c, 1), :] = re
                result[pl.ds((s * 2 + 1) * chunks + c, 1), :] = im
        return 0

    cells_a[spare * both :, :] = jnp.zeros((both, LANES), jnp.float32)
    cells_b[spare * both :, :] = jnp.zeros((both, LANES), jnp.float32)
    result[...] = jnp.zeros_like(result)
    lax.fori_loop(0, used, backward, 0)
    for s in range(blocks):
        outs[s][...] = result[s * 2 * chunks : (s + 1) * 2 * chunks, :].astype(jnp.bfloat16)


def lattice(pays, vloc, length, planes, chunks):
    blocks = len(pays)
    rows = round_up(planes, 8)
    own, along_z, along_x = tables_of(length, planes, blocks)
    vmem = pl.BlockSpec(memory_space=pltpu.VMEM)
    return pl.pallas_call(
        functools.partial(lattice_kernel, length, planes, chunks, blocks),
        out_shape=[jax.ShapeDtypeStruct((2 * chunks, LANES), jnp.bfloat16)] * blocks,
        in_specs=[vmem] * blocks + [pl.BlockSpec(memory_space=pl.ANY)] + [vmem] * 3,
        out_specs=[vmem] * blocks,
        scratch_shapes=[
            pltpu.VMEM((blocks * 4 * chunks, LANES), jnp.float32),
            pltpu.VMEM(((blocks * planes + 1) * 2 * rows, LANES), jnp.float32),
            pltpu.VMEM(((blocks * planes + 1) * 2 * rows, LANES), jnp.float32),
            pltpu.VMEM((blocks * chunks, 2 * rows, LANES), jnp.bfloat16),
            pltpu.VMEM((length * planes, length), jnp.float32),
            pltpu.VMEM((length * planes, LANES), jnp.float32),
            pltpu.VMEM((length * planes, LANES), jnp.float32),
            pltpu.VMEM((blocks * 2 * chunks, LANES), jnp.float32),
            pltpu.VMEM((blocks * 8, LANES), jnp.int32),
            pltpu.SMEM((blocks * 8, LANES), jnp.int32),
            pltpu.SemaphoreType.DMA((2,)),
        ],
        compiler_params=pltpu.CompilerParams(vmem_limit_bytes=VMEM_LIMIT),
        name="lattice",
    )(*pays, vloc.reshape(length * planes, length), own, along_z, along_x)


def finish_kernel(length, planes, chunks, blocks, *refs):
    parts = refs[:blocks]
    slot_ref, gvec_ref, psi_ref, extra_ref, out_ref = refs[blocks:]
    waves = slot_ref.shape[1]
    local = parts[0][...].astype(jnp.float32)
    for part in parts[1:]:
        local = local + part[...].astype(jnp.float32)
    turned = jnp.concatenate([local[:chunks].T, local[chunks:].T], axis=0).astype(jnp.bfloat16)
    x, y, z = cell_parts(gvec_ref[...], length)
    x = x + (lax.axis_index("pw") * planes).astype(jnp.float32)

    def fold(level):
        return jnp.where(level < length // 2, level, level - length)

    x, y, z = fold(x), fold(y), fold(z)
    kinetic = 4.0 * (x * x + y * y + z * z) / (length * length)
    slot = slot_ref[...]
    high = jnp.floor((slot + 0.5) * (1.0 / LANES))
    low = slot - high * LANES
    for tile in range(waves // LANES):
        span = slice(tile * LANES, (tile + 1) * LANES)
        at_high = where_bf16(iota((chunks, LANES), 0) == high[:, span], 1.0)
        rows = dot(turned, at_high)
        mine = iota((LANES, LANES), 0) == low[:, span]
        re = jnp.sum(jnp.where(mine, rows[:LANES], 0.0), axis=0, keepdims=True)
        im = jnp.sum(jnp.where(mine, rows[LANES:], 0.0), axis=0, keepdims=True)
        both = jnp.concatenate([re, im], axis=0)
        psi = psi_ref[:, span].astype(jnp.float32)
        out_ref[:, span] = (both + kinetic[:, span] * psi + extra_ref[:, span]).astype(jnp.bfloat16)


def finish(parts, slot, index, psi, extra, length, planes, chunks):
    blocks = len(parts)
    return pl.pallas_call(
        functools.partial(finish_kernel, length, planes, chunks, blocks),
        out_shape=jax.ShapeDtypeStruct(psi.shape, jnp.bfloat16),
        compiler_params=pltpu.CompilerParams(vmem_limit_bytes=VMEM_LIMIT),
        name="finish",
    )(*parts, slot, index, psi, extra)


def pair_dot(left, right):
    return jnp.einsum("bg,cg->bc", left, right, preferred_element_type=jnp.float32)


def swap(value, axis, step):
    size = lax.axis_size(axis)
    return lax.ppermute(value, axis, [(k, k ^ step) for k in range(size)])


def from_all(value, axis):
    size = lax.axis_size(axis)
    return [value] + [lax.ppermute(value, axis, [(k, (k + s) % size) for k in range(size)]) for s in range(1, size)]


def on_device(psi, gvec_index, vloc, beta, dmat, qmat):
    length = vloc.shape[0]
    planes = vloc.shape[1]
    width = psi.shape[2]
    blocks = lax.axis_size("pw")
    bands = lax.axis_size("band")
    chunks = round_up(width // LANES + planes, 16)
    waves = width * blocks
    atoms, each = dmat.shape[0], dmat.shape[1]
    index = gvec_index.reshape(1, width)
    mine = psi.reshape(2, width)
    pay, slot = group_waves(index, mine, length, planes, chunks)
    pays = [pay] + [swap(pay, "pw", s) for s in range(1, blocks)]
    every = jnp.stack(from_all(mine, "band"), axis=1)
    outs = lattice(pays, vloc, length, planes, chunks)
    parts = [outs[0]] + [swap(outs[s], "pw", s) for s in range(1, blocks)]

    proj_re = pair_dot(every[0], beta[0]) + pair_dot(every[1], beta[1])
    proj_im = pair_dot(every[1], beta[0]) - pair_dot(every[0], beta[1])
    over_re = pair_dot(every[0], mine[:1]) + pair_dot(every[1], mine[1:])
    over_im = pair_dot(every[1], mine[:1]) - pair_dot(every[0], mine[1:])
    partial = jnp.stack([jnp.concatenate([proj_re, over_re], 1), jnp.concatenate([proj_im, over_im], 1)])
    coef = functools.reduce(jnp.add, from_all(partial, "pw"))
    over = coef[:, :, -1]
    coef = coef[:, :, :-1]
    split = coef.reshape(2, bands, atoms, each)
    d_coef = jnp.einsum("aij,caj->cai", dmat, split[:, 0], precision=lax.Precision.HIGHEST)
    q_coef = jnp.einsum("aij,cbaj->cbai", qmat, split, precision=lax.Precision.HIGHEST)
    d_coef = d_coef.reshape(2, 1, atoms * each).astype(jnp.bfloat16)
    q_coef = q_coef.reshape(2, bands, atoms * each).astype(jnp.bfloat16)
    stacked = jnp.concatenate([d_coef, q_coef[:, :1]], axis=1)
    added_re = jnp.dot(stacked[0], beta[0], preferred_element_type=jnp.float32) - jnp.dot(stacked[1], beta[1], preferred_element_type=jnp.float32)
    added_im = jnp.dot(stacked[0], beta[1], preferred_element_type=jnp.float32) + jnp.dot(stacked[1], beta[0], preferred_element_type=jnp.float32)
    extra = jnp.stack([added_re[0], added_im[0]])
    spsi = mine.astype(jnp.float32) + jnp.stack([added_re[1], added_im[1]])
    spsi = spsi.astype(jnp.bfloat16).reshape(2, 1, width)
    wide = q_coef.astype(jnp.float32)
    own_re, own_im = coef[0, :1], coef[1, :1]
    gram_re = over[0] + jnp.sum(own_re * wide[0] + own_im * wide[1], axis=1)
    gram_im = over[1] + jnp.sum(own_re * wide[1] - own_im * wide[0], axis=1)
    gram = jnp.stack([gram_re, gram_im]) / waves
    order = (lax.axis_index("band") - jnp.arange(bands)) % bands
    gram = jnp.sum(jnp.where(order[None, :, None] == jnp.arange(bands)[None, None, :], gram[:, :, None], 0.0), axis=1)
    hpsi = finish(parts, slot, index, mine, extra, length, planes, chunks)
    return (hpsi.reshape(2, 1, width), spsi, gram.reshape(2, 1, bands))


def solution(mesh):
    in_specs = (P(None, "band", "pw"), P("pw"), P(None, "pw", None), P(None, None, "pw"), P(), P())
    out_specs = (P(None, "band", "pw"), P(None, "band", "pw"), P(None, "band", None))
    return jax.shard_map(
        on_device, mesh=mesh, in_specs=in_specs, out_specs=out_specs, check_vma=False
    )
```

profile of v0, /device:TPU:0, one launch (start us, length us, event | category | flops | bytes accessed | tf_op | source)
XLA Modules:
  0.0 167.5 jit_solution(11898327302930604729)
XLA Ops:
  0.7 3.0 %collective-permute-start.6 = (bf16[2,6144]{1,0:T(2,128)(2,1)}, bf16[2,6144]{1,0:T(2,128)(2,1)S(1)}, u32[]{:S(2)}, u32[]{:S(2)}) collective-permute-start(bf16[2,6144]{1,0:T(2,128)(2,1)} %bitcast.136), channel_id=1, source_target_pairs={{0,1},{1,2},{2,3},{3,4},{4,5},{5,6},{6,7},{7,0},{8,9},{9,10},{10,1... | collective-permute-start | bytes 73736 | tf_op jit(solution)/shard_map/ppermute | solution.py:355
  3.7 1.6 collective-permute-start.7
  5.2 2.6 %collective-permute-start.8 = (bf16[2,6144]{1,0:T(2,128)(2,1)}, bf16[2,6144]{1,0:T(2,128)(2,1)S(1)}, u32[]{:S(2)}, u32[]{:S(2)}) collective-permute-start(bf16[2,6144]{1,0:T(2,128)(2,1)} %bitcast.138), channel_id=1, source_target_pairs={{0,3},{1,4},{2,5},{3,6},{4,7},{5,0},{6,1},{7,2},{8,11},{9,12},{10,... | collective-permute-start | bytes 73736 | tf_op jit(solution)/shard_map/ppermute | solution.py:355
  7.8 1.2 collective-permute-start.9
  9.0 2.6 %collective-permute-start.10 = (bf16[2,6144]{1,0:T(2,128)(2,1)}, bf16[2,6144]{1,0:T(2,128)(2,1)S(1)}, u32[]{:S(2)}, u32[]{:S(2)}) collective-permute-start(bf16[2,6144]{1,0:T(2,128)(2,1)} %bitcast.140), channel_id=1, source_target_pairs={{0,5},{1,6},{2,7},{3,0},{4,1},{5,2},{6,3},{7,4},{8,13},{9,14},{10,... | collective-permute-start | bytes 73736 | tf_op jit(solution)/shard_map/ppermute | solution.py:355
  11.7 0.8 constant_dynamic-update-slice_fusion
  12.5 4.8 %group_waves.1 = (bf16[400,128]{1,0:T(8,128)(2,1)}, f32[1,6144]{1,0:T(1,128)}) custom-call(s32[1,6144]{1,0:T(1,128)} %bitcast.145, bf16[2,6144]{1,0:T(2,128)(2,1)} %bitcast.141), custom_call_target="tpu_custom_call" | custom-call | tf_op jit(solution)/shard_map/group_waves/pallas_call | solution.py:129
  17.2 1.3 collective-permute-start.11
  18.6 1.5 collective-permute-start.12
  20.3 1.6 collective-permute-start.1
  22.0 0.7 collective-permute-done.12
  23.3 0.3 fusion.16
  23.7 0.3 fusion.14
  24.2 0.3 convolution_subtract_fusion.1
  24.8 0.4 convolution_add_fusion.1
  25.5 1.6 collective-permute-start.14
  27.1 1.4 collective-permute-start.15
  28.6 0.6 collective-permute-done.14
  29.2 0.6 collective-permute-done.15
  30.6 0.3 fusion.12
  31.5 0.3 convolution_subtract_fusion
  32.4 0.7 fusion.34
  33.0 0.7 pad_maximum_fusion.refs_7_
  33.8 0.6 copy-done.4
  34.4 123.5 %lattice.1 = (bf16[192,128]{1,0:T(8,128)(2,1)}, bf16[192,128]{1,0:T(8,128)(2,1)}, bf16[192,128]{1,0:T(8,128)(2,1)}, bf16[192,128]{1,0:T(8,128)(2,1)}) custom-call(bf16[400,128]{1,0:T(8,128)(2,1)} %get-tuple-element.9.refs_0_, bf16[400,128]{1,0:T(8,128)(2,1)} %copy-done.4, bf16[400,128]{1,0:T(8,128)(2,1)} %copy-done.5, bf16[400,128]{1,0:T(8,128)(2,1)} %copy-done.6, ...), custom_call_target="tpu_custom_call" | custom-call | tf_op jit(solution)/shard_map/lattice/pallas_call | solution.py:280
  157.9 0.6 collective-permute-start.3
  158.5 1.5 collective-permute-start.4
  160.1 0.6 select_reduce_fusion
  160.7 2.1 %collective-permute-done.4.refs_2_ = bf16[192,128]{1,0:T(8,128)(2,1)S(1)} collective-permute-done((bf16[192,128]{1,0:T(8,128)(2,1)}, bf16[192,128]{1,0:T(8,128)(2,1)S(1)}, u32[]{:S(2)}, u32[]{:S(2)}) %collective-permute-start.4) | collective-permute-done | bytes 49184 | tf_op jit(solution)/shard_map/ppermute | solution.py:350
  162.8 1.4 collective-permute-done.5.refs_3_
  164.3 0.6 copy-done.10
  164.9 2.6 %finish.1 = bf16[2,6144]{1,0:T(2,128)(2,1)} custom-call(bf16[192,128]{1,0:T(8,128)(2,1)} %get-tuple-element.10.refs_0_, bf16[192,128]{1,0:T(8,128)(2,1)} %copy-done.8, bf16[192,128]{1,0:T(8,128)(2,1)} %copy-done.9, bf16[192,128]{1,0:T(8,128)(2,1)} %copy-done.10, f32[1,6144]{1,0:T(1,128)} %get-tuple-element.14.refs_4_, s32[1,6144]{1,0:T(1,128)} %bitcast.146, ...), custom_call_target="tpu_custom_call" | custom-call | tf_op jit(solution)/shard_map/finish/pallas_call | solution.py:336
  (79 shorter events, 3.8 us)
Async XLA Ops:
  0.6 29.3 %copy-start = (f32[4,18,18]{2,0,1:T(4,128)S(1)}, f32[4,18,18]{2,0,1:T(4,128)}, u32[]{:S(2)}) copy-start(f32[4,18,18]{2,0,1:T(4,128)} %param.14) | copy-start | bytes 15556
  0.6 22.5 %copy-start.2 = (bf16[2,1,6144]{2,0,1:T(2,128)(2,1)S(1)}, bf16[2,1,6144]{2,0,1:T(2,128)(2,1)}, u32[]{:S(2)}) copy-start(bf16[2,1,6144]{2,0,1:T(2,128)(2,1)} %param.9) | copy-start | bytes 73732
  0.7 22.7 %copy-start.1 = (bf16[2,72,6144]{2,1,0:T(8,128)(2,1)S(1)}, bf16[2,72,6144]{2,1,0:T(8,128)(2,1)}, u32[]{:S(2)}) copy-start(bf16[2,72,6144]{2,1,0:T(8,128)(2,1)} %param.12) | copy-start | bytes 5308420
  0.7 16.6 %collective-permute-start.6 = (bf16[2,6144]{1,0:T(2,128)(2,1)}, bf16[2,6144]{1,0:T(2,128)(2,1)S(1)}, u32[]{:S(2)}, u32[]{:S(2)}) collective-permute-start(bf16[2,6144]{1,0:T(2,128)(2,1)} %bitcast.136), channel_id=1, source_target_pairs={{0,1},{1,2},{2,3},{3,4},{4,5},{5,6},{6,7},{7,0},{8,9},{9,10},{10,1... | collective-permute-start | bytes 73736 | tf_op jit(solution)/shard_map/ppermute | solution.py:355
  3.7 15.0 %collective-permute-start.7 = (bf16[2,6144]{1,0:T(2,128)(2,1)}, bf16[2,6144]{1,0:T(2,128)(2,1)S(1)}, u32[]{:S(2)}, u32[]{:S(2)}) collective-permute-start(bf16[2,6144]{1,0:T(2,128)(2,1)} %bitcast.137), channel_id=1, source_target_pairs={{0,2},{1,3},{2,4},{3,5},{4,6},{5,7},{6,0},{7,1},{8,10},{9,11},{10,... | collective-permute-start | bytes 73736 | tf_op jit(solution)/shard_map/ppermute | solution.py:355
  5.2 14.9 %collective-permute-start.8 = (bf16[2,6144]{1,0:T(2,128)(2,1)}, bf16[2,6144]{1,0:T(2,128)(2,1)S(1)}, u32[]{:S(2)}, u32[]{:S(2)}) collective-permute-start(bf16[2,6144]{1,0:T(2,128)(2,1)} %bitcast.138), channel_id=1, source_target_pairs={{0,3},{1,4},{2,5},{3,6},{4,7},{5,0},{6,1},{7,2},{8,11},{9,12},{10,... | collective-permute-start | bytes 73736 | tf_op jit(solution)/shard_map/ppermute | solution.py:355
  7.8 12.5 %collective-permute-start.9 = (bf16[2,6144]{1,0:T(2,128)(2,1)}, bf16[2,6144]{1,0:T(2,128)(2,1)S(1)}, u32[]{:S(2)}, u32[]{:S(2)}) collective-permute-start(bf16[2,6144]{1,0:T(2,128)(2,1)} %bitcast.139), channel_id=1, source_target_pairs={{0,4},{1,5},{2,6},{3,7},{4,0},{5,1},{6,2},{7,3},{8,12},{9,13},{10,... | collective-permute-start | bytes 73736 | tf_op jit(solution)/shard_map/ppermute | solution.py:355
  9.0 12.9 %collective-permute-start.10 = (bf16[2,6144]{1,0:T(2,128)(2,1)}, bf16[2,6144]{1,0:T(2,128)(2,1)S(1)}, u32[]{:S(2)}, u32[]{:S(2)}) collective-permute-start(bf16[2,6144]{1,0:T(2,128)(2,1)} %bitcast.140), channel_id=1, source_target_pairs={{0,5},{1,6},{2,7},{3,0},{4,1},{5,2},{6,3},{7,4},{8,13},{9,14},{10,... | collective-permute-start | bytes 73736 | tf_op jit(solution)/shard_map/ppermute | solution.py:355
  17.2 4.7 %collective-permute-start.11 = (bf16[2,6144]{1,0:T(2,128)(2,1)}, bf16[2,6144]{1,0:T(2,128)(2,1)S(1)}, u32[]{:S(2)}, u32[]{:S(2)}) collective-permute-start(bf16[2,6144]{1,0:T(2,128)(2,1)} %bitcast.142), channel_id=1, source_target_pairs={{0,6},{1,7},{2,0},{3,1},{4,2},{5,3},{6,4},{7,5},{8,14},{9,15},{10,... | collective-permute-start | bytes 73736 | tf_op jit(solution)/shard_map/ppermute | solution.py:355
  18.6 4.1 %collective-permute-start.12 = (bf16[2,6144]{1,0:T(2,128)(2,1)}, bf16[2,6144]{1,0:T(2,128)(2,1)S(1)}, u32[]{:S(2)}, u32[]{:S(2)}) collective-permute-start(bf16[2,6144]{1,0:T(2,128)(2,1)} %bitcast.143), channel_id=1, source_target_pairs={{0,7},{1,0},{2,1},{3,2},{4,3},{5,4},{6,5},{7,6},{8,15},{9,8},{10,9... | collective-permute-start | bytes 73736 | tf_op jit(solution)/shard_map/ppermute | solution.py:355
  20.2 13.6 %collective-permute-start = (bf16[400,128]{1,0:T(8,128)(2,1)}, bf16[400,128]{1,0:T(8,128)(2,1)S(1)}, u32[]{:S(2)}, u32[]{:S(2)}) collective-permute-start(bf16[400,128]{1,0:T(8,128)(2,1)} %get-tuple-element.9.refs_0_), channel_id=1, source_target_pairs={{0,8},{8,0},{16,24},{24,16},{1,9},{9,1},{17,25},{25,17},{2,10},{10... | collective-permute-start | bytes 307208 | tf_op jit(solution)/shard_map/ppermute | solution.py:350
  20.3 13.4 %collective-permute-start.1 = (bf16[400,128]{1,0:T(8,128)(2,1)}, bf16[400,128]{1,0:T(8,128)(2,1)S(1)}, u32[]{:S(2)}, u32[]{:S(2)}) collective-permute-start(bf16[400,128]{1,0:T(8,128)(2,1)} %get-tuple-element.9.refs_0_), channel_id=1, source_target_pairs={{0,16},{8,24},{16,0},{24,8},{1,17},{9,25},{17,1},{25,9},{2,18},{10... | collective-permute-start | bytes 307208 | tf_op jit(solution)/shard_map/ppermute | solution.py:350
  23.7 4.9 %copy-start.3 = (bf16[400,128]{1,0:T(8,128)(2,1)S(1)}, bf16[400,128]{1,0:T(8,128)(2,1)}, u32[]{:S(2)}) copy-start(bf16[400,128]{1,0:T(8,128)(2,1)} %get-tuple-element.9.refs_0_) | copy-start | bytes 307204
  23.7 6.6 %copy-start.7 = (f32[4,18,18]{2,0,1:T(4,128)S(1)}, f32[4,18,18]{2,0,1:T(4,128)}, u32[]{:S(2)}) copy-start(f32[4,18,18]{2,0,1:T(4,128)} %param.13) | copy-start | bytes 15556
  25.5 3.1 %collective-permute-start.13 = (f32[2,8,73]{2,1,0:T(8,128)S(1)}, f32[2,8,73]{2,1,0:T(8,128)S(1)}, u32[]{:S(2)}, u32[]{:S(2)}) collective-permute-start(f32[2,8,73]{2,1,0:T(8,128)S(1)} %pad_maximum_fusion.1), channel_id=1, source_target_pairs={{0,8},{8,16},{16,24},{24,0},{1,9},{9,17},{17,25},{25,1},{2,10},{10... | collective-permute-start | bytes 14024 | tf_op jit(solution)/shard_map/ppermute | solution.py:355
  25.5 3.7 %collective-permute-start.14 = (f32[2,8,73]{2,1,0:T(8,128)S(1)}, f32[2,8,73]{2,1,0:T(8,128)S(1)}, u32[]{:S(2)}, u32[]{:S(2)}) collective-permute-start(f32[2,8,73]{2,1,0:T(8,128)S(1)} %pad_maximum_fusion.1), channel_id=1, source_target_pairs={{0,16},{8,24},{16,0},{24,8},{1,17},{9,25},{17,1},{25,9},{2,18},{10... | collective-permute-start | bytes 14024 | tf_op jit(solution)/shard_map/ppermute | solution.py:355
  27.1 2.8 %collective-permute-start.15 = (f32[2,8,73]{2,1,0:T(8,128)S(1)}, f32[2,8,73]{2,1,0:T(8,128)S(1)}, u32[]{:S(2)}, u32[]{:S(2)}) collective-permute-start(f32[2,8,73]{2,1,0:T(8,128)S(1)} %pad_maximum_fusion.1), channel_id=1, source_target_pairs={{0,24},{8,0},{16,8},{24,16},{1,25},{9,1},{17,9},{25,17},{2,26},{10... | collective-permute-start | bytes 14024 | tf_op jit(solution)/shard_map/ppermute | solution.py:355
  28.6 5.2 %collective-permute-start.2 = (bf16[400,128]{1,0:T(8,128)(2,1)S(1)}, bf16[400,128]{1,0:T(8,128)(2,1)S(1)}, u32[]{:S(2)}, u32[]{:S(2)}) collective-permute-start(bf16[400,128]{1,0:T(8,128)(2,1)S(1)} %copy-done.3), channel_id=1, source_target_pairs={{0,24},{8,16},{16,8},{24,0},{1,25},{9,17},{17,9},{25,1},{2,26},{10... | collective-permute-start | bytes 307208 | tf_op jit(solution)/shard_map/ppermute | solution.py:350
  33.7 0.6 copy-start.4
  33.7 0.7 copy-start.5
  33.8 0.7 copy-start.6
  157.9 2.8 %collective-permute-start.3 = (bf16[192,128]{1,0:T(8,128)(2,1)}, bf16[192,128]{1,0:T(8,128)(2,1)S(1)}, u32[]{:S(2)}, u32[]{:S(2)}) collective-permute-start(bf16[192,128]{1,0:T(8,128)(2,1)} %get-tuple-element.11), channel_id=1, source_target_pairs={{0,8},{8,0},{16,24},{24,16},{1,9},{9,1},{17,25},{25,17},{2,10},{10... | collective-permute-start | bytes 147464 | tf_op jit(solution)/shard_map/ppermute | solution.py:350
  158.5 4.3 %collective-permute-start.4 = (bf16[192,128]{1,0:T(8,128)(2,1)}, bf16[192,128]{1,0:T(8,128)(2,1)S(1)}, u32[]{:S(2)}, u32[]{:S(2)}) collective-permute-start(bf16[192,128]{1,0:T(8,128)(2,1)} %get-tuple-element.12), channel_id=1, source_target_pairs={{0,16},{8,24},{16,0},{24,8},{1,17},{9,25},{17,1},{25,9},{2,18},{10... | collective-permute-start | bytes 147464 | tf_op jit(solution)/shard_map/ppermute | solution.py:350
  160.1 4.2 %collective-permute-start.5 = (bf16[192,128]{1,0:T(8,128)(2,1)}, bf16[192,128]{1,0:T(8,128)(2,1)S(1)}, u32[]{:S(2)}, u32[]{:S(2)}) collective-permute-start(bf16[192,128]{1,0:T(8,128)(2,1)} %get-tuple-element.13), channel_id=1, source_target_pairs={{0,24},{8,16},{16,8},{24,0},{1,25},{9,17},{17,9},{25,1},{2,26},{10... | collective-permute-start | bytes 147464 | tf_op jit(solution)/shard_map/ppermute | solution.py:350
  160.7 3.6 %copy-start.8 = (bf16[192,128]{1,0:T(8,128)(2,1)}, bf16[192,128]{1,0:T(8,128)(2,1)S(1)}, u32[]{:S(2)}) copy-start(bf16[192,128]{1,0:T(8,128)(2,1)S(1)} %collective-permute-done.3.refs_1_) | copy-start | bytes 147460
  162.8 1.5 copy-start.9
  164.3 0.6 copy-start.10
where the time goes:
time: 167 us; the launch traced here: 168 us
  Pallas kernels  131 us (78%)
  starting transfers between devices  20.7 us (12%)
  waiting for transfers between devices  5.62 us (3%)
  matrix products  3.55 us (2%)
  local copies, waits for them, and re-layouts  3.41 us (2%)
  other arithmetic  2.54 us (2%)
    pallas_call x1, Pallas kernels, lattice(): pl.pallas_call(functools.partial(lattice_kernel, length, planes, chunks,...  123 us
    ppermute x10, starting transfers between devices, from_all(): lax.ppermute(value, axis, [(k, (k + s) % size) for k in range(size)])  16.8 us
    pallas_call x1, Pallas kernels, group_waves(): pl.pallas_call(functools.partial(group_kernel, length, planes, chunks), o...  4.78 us
    ppermute x6, starting transfers between devices, swap(): return lax.ppermute(value, axis, [(k, k ^ step) for k in range(size)])  3.86 us
    ppermute x6, waiting for transfers between devices, swap(): return lax.ppermute(value, axis, [(k, k ^ step) for k in range(size)])  3.61 us
  transfers between devices with their start and end apart: 16, of which 5 were waited for; matrix products, arithmetic and copies ran while one was open for 5% of the time, Pallas kernels for 3%

commit v1 on v0

v1 whole, which is shorter than its diff:
```python
import functools

import jax
import jax.numpy as jnp
import ml_dtypes
import numpy as np
from jax import lax
from jax.experimental import pallas as pl
from jax.experimental.pallas import tpu as pltpu
from jax.sharding import PartitionSpec as P

LANES = 128
VMEM_LIMIT = 60 * 1024 * 1024


def round_up(value, unit):
    return -(-value // unit) * unit


def dft_parts(length):
    counter = np.arange(length)
    phase = counter[:, None] * counter[None, :] % length
    angle = phase.astype(np.float32) * np.float32(2.0 * np.pi / length)
    factor = np.float32(1.0) / np.sqrt(np.float32(length))
    return (np.cos(angle) * factor).astype(np.float32), (np.sin(angle) * factor).astype(np.float32)


def as_bf16(array):
    return np.asarray(array).astype(ml_dtypes.bfloat16)


def tables_of(length, planes, blocks):
    half = length // 2
    cosine, sine = dft_parts(length)
    rows = round_up(planes, 8)
    own = np.zeros((blocks, 2 * rows, length), np.float32)
    for block in range(blocks):
        span = slice(block * planes, (block + 1) * planes)
        own[block, :planes] = cosine[span]
        own[block, rows : rows + planes] = sine[span]
    def square(c, s, size):
        pad = ((0, size - half), (0, size - half))
        c, s = np.pad(c, pad), np.pad(s, pad)
        return np.block([[c, -s], [s, c]])

    first = slice(0, half)
    even, odd = slice(0, None, 2), slice(1, None, 2)
    along_z = np.stack(
        [
            square(cosine[even, first], -sine[even, first], LANES),
            square(cosine[odd, first], -sine[odd, first], LANES),
            square(cosine[first, even], sine[first, even], LANES),
            square(cosine[first, odd], sine[first, odd], LANES),
        ]
    )
    along_x = np.stack(
        [
            square(cosine[first, even], sine[first, even], half),
            square(cosine[first, odd], sine[first, odd], half),
            square(cosine[even, first], -sine[even, first], half),
            square(cosine[odd, first], -sine[odd, first], half),
        ]
    )
    return as_bf16(own), as_bf16(along_z), as_bf16(along_x)


def cell_parts(index, length):
    cell = index.astype(jnp.float32)
    x = jnp.floor((cell + 0.5) * (1.0 / (length * length)))
    rest = cell - x * (length * length)
    y = jnp.floor((rest + 0.5) * (1.0 / length))
    return x, y, rest - y * length


def iota(shape, dim):
    return lax.broadcasted_iota(jnp.int32, shape, dim).astype(jnp.float32)


def where_bf16(mask, value):
    return jnp.where(mask, value, 0.0).astype(jnp.bfloat16)


def dot(left, right):
    return jnp.dot(left, right, preferred_element_type=jnp.float32)


def dot_lanes(left, right):
    return lax.dot_general(left, right, (((1,), (1,)), ((), ())), preferred_element_type=jnp.float32)


def group_kernel(length, planes, chunks, gvec_ref, psi_ref, pay_ref, slot_ref, hot, counts, spread, pick):
    waves = gvec_ref.shape[1]
    tiles = waves // LANES
    rows = round_up(planes, 16)
    x, y, z = cell_parts(gvec_ref[...], length)
    z_half = jnp.floor(z * 0.5)
    z = z_half + (z - 2.0 * z_half) * LANES
    psi = psi_ref[...].astype(jnp.float32)
    plane = iota((rows, LANES), 0)
    for tile in range(tiles):
        span = slice(tile * LANES, (tile + 1) * LANES)
        hot[tile * rows : (tile + 1) * rows, :] = where_bf16(plane == x[:, span], 1.0)
    upto = jnp.where(iota((LANES, LANES), 0) <= iota((LANES, LANES), 1), 1.0, 0.0)
    upto = jnp.concatenate([upto, jnp.ones((LANES, LANES), jnp.float32)], axis=1)
    counts[...] = dot(hot[...], upto.astype(jnp.bfloat16))
    total = jnp.zeros((rows, LANES), jnp.float32)
    for tile in range(tiles):
        total = total + counts[tile * rows : (tile + 1) * rows, LANES:]
    need = jnp.maximum(jnp.floor((total + (LANES - 0.5)) * (1.0 / LANES)), 1.0)
    need = jnp.where(plane < planes, need, 0.0)
    below = where_bf16(iota((rows, rows), 1) < iota((rows, rows), 0), 1.0)
    first = dot(below, need.astype(jnp.bfloat16))
    ends = jnp.where((plane < planes) & (iota((rows, LANES), 1) >= first + need), 1.0, 0.0)
    chunk_plane = jnp.sum(ends, axis=0, keepdims=True)
    running = first * LANES - 1.0
    upper = iota((chunks, LANES), 0)
    lower = iota((LANES, LANES), 0)
    for tile in range(tiles):
        span = slice(tile * LANES, (tile + 1) * LANES)
        part = slice(tile * rows, (tile + 1) * rows)
        mine = plane == x[:, span]
        slot = jnp.where(mine, counts[part, :LANES] + running, 0.0)
        slot = jnp.sum(slot, axis=0, keepdims=True)
        running = running + counts[part, LANES:]
        slot_ref[:, span] = slot
        high = jnp.floor((slot + 0.5) * (1.0 / LANES))
        at_high = upper == high
        spread[0:chunks, span] = where_bf16(at_high, psi[0:1, span])
        spread[chunks : 2 * chunks, span] = where_bf16(at_high, psi[1:2, span])
        spread[2 * chunks : 3 * chunks, span] = where_bf16(at_high, y[:, span])
        spread[3 * chunks : 4 * chunks, span] = where_bf16(at_high, z[:, span])
        pick[:, span] = where_bf16(lower == slot - high * LANES, 1.0)
    pay_ref[0 : 4 * chunks, :] = dot_lanes(spread[...], pick[...]).astype(jnp.bfloat16)
    used = jnp.sum(need, axis=0, keepdims=True)
    pay_ref[4 * chunks :, :] = jnp.where(iota((16, LANES), 0) == 0.0, chunk_plane, used).astype(jnp.bfloat16)


def group_waves(index, psi, length, planes, chunks):
    waves = index.shape[1]
    rows = round_up(planes, 16)
    tiles = waves // LANES
    return pl.pallas_call(
        functools.partial(group_kernel, length, planes, chunks),
        out_shape=(
            jax.ShapeDtypeStruct((4 * chunks + 16, LANES), jnp.bfloat16),
            jax.ShapeDtypeStruct((1, waves), jnp.float32),
        ),
        scratch_shapes=[
            pltpu.VMEM((tiles * rows, LANES), jnp.bfloat16),
            pltpu.VMEM((tiles * rows, 2 * LANES), jnp.float32),
            pltpu.VMEM((4 * chunks, waves), jnp.bfloat16),
            pltpu.VMEM((LANES, waves), jnp.bfloat16),
        ],
        compiler_params=pltpu.CompilerParams(vmem_limit_bytes=VMEM_LIMIT),
        name="group_waves",
    )(index, psi)


def lattice_kernel(length, planes, chunks, blocks, *refs):
    pays = refs[:blocks]
    sums_ref, vloc_hbm, own_ref, along_z, along_x = refs[blocks : blocks + 5]
    outs = refs[blocks + 5 : 2 * blocks + 5]
    wide, cells_e, cells_o, phases, vloc, vloc_l, vloc_h, result, maps, maps_s, sems = refs[2 * blocks + 5 :]
    half = length // 2
    rows = round_up(planes, 8)
    both = 2 * rows
    pitch = both + 1
    spare = blocks * planes
    me = lax.axis_index("pw")
    load = pltpu.make_async_copy(vloc_hbm, vloc, sems.at[0])
    load.start()
    for s in range(blocks):
        maps[s * 8 : (s + 1) * 8, :] = pays[s][4 * chunks : 4 * chunks + 16, :].astype(jnp.int32)[:8]
    fetch = pltpu.make_async_copy(maps, maps_s, sems.at[1])
    fetch.start()
    for s in range(blocks):
        wide[s * 4 * chunks : (s + 1) * 4 * chunks, :] = pays[s][0 : 4 * chunks, :].astype(jnp.float32)
    own = own_ref[me]
    fetch.wait()
    used = maps_s[1, 0]
    for s in range(1, blocks):
        used = jnp.maximum(used, maps_s[s * 8 + 1, 0])
    level = iota((2 * LANES, LANES), 0)
    level_y = level[:length]
    group = 4 if blocks % 4 == 0 else 1
    ahead = 4 if blocks == group else 1
    batch = 4 if planes % 4 == 0 else 1
    turns = (used + ahead - 1) // ahead

    def place(s, c):
        at = maps_s[s * 8, c]
        x = (me ^ s) * planes + at
        return jnp.where(at < planes, x // 2 + x % 2 * half, spare)

    def row(s, part, c):
        return wide[pl.ds((s * 4 + part) * chunks + c, 1), :]

    def items(turn, base):
        return [(s, turn * ahead + j) for s in range(base, base + group) for j in range(ahead)]

    def pick_z(s, c):
        return where_bf16(level == row(s, 3, c), 1.0)

    def forward(turn, _):
        for base in range(0, blocks, group):
            todo = items(turn, base)
            found = [dot(own, where_bf16(level_y == row(s, 2, c), 1.0)) for s, c in todo]
            mixed = []
            for (s, c), phase in zip(todo, found):
                phases[s * chunks + c] = phase.astype(jnp.bfloat16)
                re, im = row(s, 0, c), row(s, 1, c)
                cos, sin = phase[:rows], phase[rows:]
                both_parts = jnp.concatenate([re * cos - im * sin, re * sin + im * cos], axis=0)
                mixed.append(both_parts.astype(jnp.bfloat16))
            found = [dot_lanes(value, pick_z(s, c)) for (s, c), value in zip(todo, mixed)]
            spans = [place(s, c) for s, c in todo]
            for n, (s, c) in enumerate(todo):
                span = pl.ds(spans[n] * pitch, both)
                if n % ahead == 0:
                    fresh = (c == 0) | (spans[n] != place(s, jnp.maximum(c - 1, 0)))
                    before_e, before_o = cells_e[span, :], cells_o[span, :]
                else:
                    fresh = spans[n] != spans[n - 1]
                    before_e, before_o = part_e, part_o
                part_e = found[n][:, :LANES] + jnp.where(fresh, 0.0, before_e)
                part_o = found[n][:, LANES:] + jnp.where(fresh, 0.0, before_o)
                cells_e[span, :] = part_e
                cells_o[span, :] = part_o
        return 0

    lax.fori_loop(0, turns, forward, 0)
    load.wait()
    step = planes + 1 - planes % 2

    def spread(x, _):
        plane = vloc[x]
        span = pl.ds(x * step, planes)
        vloc_l[span, :] = plane[:, :LANES]
        vloc_h[span, :] = jnp.concatenate([plane[:, half:], plane[:, : LANES - half]], axis=1)
        return 0

    lax.fori_loop(0, length, spread, 0, unroll=4)

    def strided(start):
        return pl.ds(start, half, stride=pitch)

    def beside(left, right):
        return jnp.concatenate([left, right], axis=1)

    def above(upper, lower):
        return jnp.concatenate([upper, lower], axis=0)

    def middle(turn, _):
        many = [turn * batch + j for j in range(batch)]
        starts = [k + odd * half * pitch for k in many for odd in range(2)]

        def pull(cells):
            return jnp.concatenate(
                [
                    beside(cells[strided(at), :], cells[strided(at + rows), :]).astype(jnp.bfloat16)
                    for at in starts
                ],
                axis=0,
            )

        even = dot(pull(cells_e), along_z[0])
        odd = dot(pull(cells_o), along_z[1])
        low, high = (even + odd).astype(jnp.bfloat16), (even - odd).astype(jnp.bfloat16)

        def stacked(n):
            part = slice(n * half, (n + 1) * half)
            return above(
                beside(low[part, :LANES], high[part, :LANES]),
                beside(low[part, LANES:], high[part, LANES:]),
            )

        sums, differences = [], []
        for j, k in enumerate(many):
            even = dot(along_x[0], stacked(2 * j))
            odd = dot(along_x[1], stacked(2 * j + 1))
            near, far = pl.ds(k, half, stride=step), pl.ds(k + half * step, half, stride=step)
            near = beside(vloc_l[near, :], vloc_h[near, :])
            far = beside(vloc_l[far, :], vloc_h[far, :])
            first = (even + odd) * above(near, near)
            second = (even - odd) * above(far, far)
            for table, value in ((along_x[2], first + second), (along_x[3], first - second)):
                back = dot(table, value.astype(jnp.bfloat16))
                total, change = back[:, :LANES] + back[:, LANES:], back[:, :LANES] - back[:, LANES:]
                sums.append(beside(total[:half], total[half:]).astype(jnp.bfloat16))
                differences.append(beside(change[:half], change[half:]).astype(jnp.bfloat16))
        even = dot(jnp.concatenate(sums, axis=0), along_z[2])
        odd = dot(jnp.concatenate(differences, axis=0), along_z[3])
        for n, at in enumerate(starts):
            part = slice(n * half, (n + 1) * half)
            cells_e[strided(at), :] = even[part, :LANES]
            cells_e[strided(at + rows), :] = even[part, LANES:]
            cells_o[strided(at), :] = odd[part, :LANES]
            cells_o[strided(at + rows), :] = odd[part, LANES:]
        return 0

    lax.fori_loop(0, planes // batch, middle, 0)

    def backward(turn, _):
        for base in range(0, blocks, group):
            todo = items(turn, base)
            found = []
            for s, c in todo:
                span = pl.ds(place(s, c) * pitch, both)
                value = beside(cells_e[span, :], cells_o[span, :]).astype(jnp.bfloat16)
                found.append(dot(value, pick_z(s, c)))
            for (s, c), part in zip(todo, found):
                phase = phases[s * chunks + c].astype(jnp.float32)
                re, im = part[:rows], part[rows:]
                cos, sin = phase[:rows], phase[rows:]
                result[pl.ds(s * 2 * chunks + c, 1), :] = jnp.sum(re * cos + im * sin, axis=0, keepdims=True)
                result[pl.ds((s * 2 + 1) * chunks + c, 1), :] = jnp.sum(im * cos - re * sin, axis=0, keepdims=True)
        return 0

    spare_span = pl.ds(spare * pitch, both)
    cells_e[spare_span, :] = jnp.zeros((both, LANES), jnp.float32)
    cells_o[spare_span, :] = jnp.zeros((both, LANES), jnp.float32)
    result[...] = jnp.zeros_like(result)
    lax.fori_loop(0, turns, backward, 0)
    rest = sums_ref[...]
    pieces = []
    for _ in range(3):
        pieces.append(rest.astype(jnp.bfloat16))
        rest = rest - pieces[-1].astype(jnp.float32)
    size = sums_ref.shape[0]
    for s in range(blocks):
        outs[s][0 : 2 * chunks, :] = result[s * 2 * chunks : (s + 1) * 2 * chunks, :].astype(jnp.bfloat16)
        for n, piece in enumerate(pieces):
            outs[s][2 * chunks + n * size : 2 * chunks + (n + 1) * size, :] = piece


def lattice(pays, sums, vloc, length, planes, chunks):
    blocks = len(pays)
    rows = round_up(planes, 8)
    own, along_z, along_x = tables_of(length, planes, blocks)
    vmem = pl.BlockSpec(memory_space=pltpu.VMEM)
    return pl.pallas_call(
        functools.partial(lattice_kernel, length, planes, chunks, blocks),
        out_shape=[jax.ShapeDtypeStruct((2 * chunks + 3 * sums.shape[0], LANES), jnp.bfloat16)] * blocks,
        in_specs=[vmem] * (blocks + 1) + [pl.BlockSpec(memory_space=pl.ANY)] + [vmem] * 3,
        out_specs=[vmem] * blocks,
        scratch_shapes=[
            pltpu.VMEM((blocks * 4 * chunks, LANES), jnp.float32),
            pltpu.VMEM((round_up((blocks * planes + 1) * (2 * rows + 1), 8), LANES), jnp.float32),
            pltpu.VMEM((round_up((blocks * planes + 1) * (2 * rows + 1), 8), LANES), jnp.float32),
            pltpu.VMEM((blocks * chunks, 2 * rows, LANES), jnp.bfloat16),
            pltpu.VMEM((length, planes, length), jnp.float32),
            pltpu.VMEM((round_up(length * (planes + 1), 8), LANES), jnp.float32),
            pltpu.VMEM((round_up(length * (planes + 1), 8), LANES), jnp.float32),
            pltpu.VMEM((blocks * 2 * chunks, LANES), jnp.float32),
            pltpu.VMEM((blocks * 8, LANES), jnp.int32),
            pltpu.SMEM((blocks * 8, LANES), jnp.int32),
            pltpu.SemaphoreType.DMA((2,)),
        ],
        compiler_params=pltpu.CompilerParams(vmem_limit_bytes=VMEM_LIMIT),
        name="lattice",
    )(*pays, sums, vloc, own, along_z, along_x)


def project_kernel(bands, *refs):
    every = [ref[...].astype(jnp.float32) for ref in refs[:bands]]
    beta_ref, out_ref = refs[bands:]
    count = beta_ref.shape[1]
    rows = out_ref.shape[0] // 2
    pad = [jnp.zeros_like(every[0][:1])] * (rows - bands)
    stack = [value[:1] for value in every] + pad + [value[1:] for value in every] + pad
    stack = jnp.concatenate(stack, axis=0).astype(jnp.bfloat16)

    def against(re, im):
        on_re, on_im = dot_lanes(stack, re), dot_lanes(stack, im)
        return jnp.concatenate([on_re[:rows] + on_im[rows:], on_re[rows:] - on_im[:rows]], axis=0)

    out_ref[...] = jnp.zeros_like(out_ref)
    out_ref[:, :count] = against(beta_ref[0], beta_ref[1])
    shape = (16, every[0].shape[1])
    own = [jnp.broadcast_to(every[0][n : n + 1], shape).astype(jnp.bfloat16) for n in range(2)]
    over = against(*own)[:, :1]
    out_ref[...] = jnp.where(iota(out_ref.shape, 1) == count, over, out_ref[...])


def project(every, beta):
    bands = len(every)
    return pl.pallas_call(
        functools.partial(project_kernel, bands),
        out_shape=jax.ShapeDtypeStruct((2 * round_up(bands, 8), LANES), jnp.float32),
        compiler_params=pltpu.CompilerParams(vmem_limit_bytes=VMEM_LIMIT),
        name="project",
    )(*every, beta)


def finish_kernel(length, planes, chunks, blocks, bands, *refs):
    parts = refs[:blocks]
    slot_ref, gvec_ref, psi_ref, beta_ref, atoms_ref, hpsi_ref, spsi_ref, gram_ref = refs[blocks:]
    waves = slot_ref.shape[1]
    count = beta_ref.shape[1]
    total = parts[0][...].astype(jnp.float32)
    for part in parts[1:]:
        total = total + part[...].astype(jnp.float32)
    size = (total.shape[0] - 2 * chunks) // 3
    half_size = size // 2
    sums = [total[2 * chunks + n * size : 2 * chunks + (n + 1) * size] for n in range(3)]
    sums = sums[0] + (sums[1] + sums[2])
    coef = jnp.dot(sums, atoms_ref[...], precision=lax.Precision.HIGHEST, preferred_element_type=jnp.float32)
    coef = coef.astype(jnp.bfloat16).astype(jnp.float32)
    d_re, d_im = coef[:1, :count], coef[half_size : half_size + 1, :count]
    q_re, q_im = coef[:1, LANES : LANES + count], coef[half_size : half_size + 1, LANES : LANES + count]
    none = jnp.zeros((4, count), jnp.float32)
    on_re = jnp.concatenate([d_re, d_im, q_re, q_im, none], axis=0).astype(jnp.bfloat16)
    on_im = jnp.concatenate([-d_im, d_re, -q_im, q_re, none], axis=0).astype(jnp.bfloat16)
    added = dot(on_re, beta_ref[0]) + dot(on_im, beta_ref[1])

    own_re, own_im = sums[:1], sums[half_size : half_size + 1]
    each_re, each_im = coef[:half_size, LANES:], coef[half_size:, LANES:]
    over = iota((half_size, LANES), 1) == count
    gram_re = own_re * each_re + own_im * each_im + jnp.where(over, sums[:half_size], 0.0)
    gram_im = own_re * each_im - own_im * each_re + jnp.where(over, sums[half_size:], 0.0)
    turn = lax.axis_index("band") - lax.broadcasted_iota(jnp.int32, (half_size, bands), 0)
    turn = jnp.where(turn < 0, turn + bands, turn)
    here = turn == lax.broadcasted_iota(jnp.int32, (half_size, bands), 1)
    here = here & (lax.broadcasted_iota(jnp.int32, (half_size, bands), 0) < bands)
    for n, value in enumerate((gram_re, gram_im)):
        value = jnp.sum(value, axis=1, keepdims=True)
        value = jnp.sum(jnp.where(here, value, 0.0), axis=0, keepdims=True)
        gram_ref[n : n + 1, :] = value * (1.0 / (waves * blocks))

    local = total[: 2 * chunks]
    turned = jnp.concatenate([local[:chunks].T, local[chunks:].T], axis=0).astype(jnp.bfloat16)
    x, y, z = cell_parts(gvec_ref[...], length)
    x = x + (lax.axis_index("pw") * planes).astype(jnp.float32)

    def fold(level):
        return jnp.where(level < length // 2, level, level - length)

    x, y, z = fold(x), fold(y), fold(z)
    kinetic = 4.0 * (x * x + y * y + z * z) / (length * length)
    slot = slot_ref[...]
    high = jnp.floor((slot + 0.5) * (1.0 / LANES))
    low = slot - high * LANES
    for tile in range(waves // LANES):
        span = slice(tile * LANES, (tile + 1) * LANES)
        at_high = where_bf16(iota((chunks, LANES), 0) == high[:, span], 1.0)
        rows = dot(turned, at_high)
        mine = iota((LANES, LANES), 0) == low[:, span]
        re = jnp.sum(jnp.where(mine, rows[:LANES], 0.0), axis=0, keepdims=True)
        im = jnp.sum(jnp.where(mine, rows[LANES:], 0.0), axis=0, keepdims=True)
        both = jnp.concatenate([re, im], axis=0)
        psi = psi_ref[:, span].astype(jnp.float32)
        hpsi_ref[:, span] = (both + kinetic[:, span] * psi + added[0:2, span]).astype(jnp.bfloat16)
        spsi_ref[:, span] = (psi + added[2:4, span]).astype(jnp.bfloat16)


def finish(parts, slot, index, psi, beta, atoms, length, planes, chunks, bands):
    blocks = len(parts)
    return pl.pallas_call(
        functools.partial(finish_kernel, length, planes, chunks, blocks, bands),
        out_shape=(
            jax.ShapeDtypeStruct(psi.shape, jnp.bfloat16),
            jax.ShapeDtypeStruct(psi.shape, jnp.bfloat16),
            jax.ShapeDtypeStruct((2, bands), jnp.float32),
        ),
        compiler_params=pltpu.CompilerParams(vmem_limit_bytes=VMEM_LIMIT),
        name="finish",
    )(*parts, slot, index, psi, beta, atoms)


def swap(value, axis, step):
    size = lax.axis_size(axis)
    return lax.ppermute(value, axis, [(k, k ^ step) for k in range(size)])


def from_all(value, axis):
    size = lax.axis_size(axis)
    return [value] + [lax.ppermute(value, axis, [(k, (k + s) % size) for k in range(size)]) for s in range(1, size)]


def atom_blocks(matrix):
    atoms, each = matrix.shape[0], matrix.shape[1]
    same = jnp.eye(atoms, dtype=matrix.dtype)[:, None, :, None]
    square = (same * jnp.transpose(matrix, (0, 2, 1))[:, :, None, :]).reshape(atoms * each, atoms * each)
    return jnp.pad(square, ((0, LANES - atoms * each), (0, LANES - atoms * each)))


def on_device(psi, gvec_index, vloc, beta, dmat, qmat):
    length = vloc.shape[0]
    planes = vloc.shape[1]
    width = psi.shape[2]
    blocks = lax.axis_size("pw")
    bands = lax.axis_size("band")
    chunks = round_up(width // LANES + planes, 16)
    index = gvec_index.reshape(1, width)
    mine = psi.reshape(2, width)
    atoms = jnp.concatenate([atom_blocks(dmat), atom_blocks(qmat)], axis=1)
    pay, slot = group_waves(index, mine, length, planes, chunks)
    pays = [pay] + [swap(pay, "pw", s) for s in range(1, blocks)]
    later, _ = lax.optimization_barrier((mine, pay))
    sums = project(from_all(later, "band"), beta)
    outs = lattice(pays, sums, vloc, length, planes, chunks)
    parts = [outs[0]] + [swap(outs[s], "pw", s) for s in range(1, blocks)]
    hpsi, spsi, gram = finish(parts, slot, index, mine, beta, atoms, length, planes, chunks, bands)
    return (hpsi.reshape(2, 1, width), spsi.reshape(2, 1, width), gram.reshape(2, 1, bands))


def solution(mesh):
    in_specs = (P(None, "band", "pw"), P("pw"), P(None, "pw", None), P(None, None, "pw"), P(), P())
    out_specs = (P(None, "band", "pw"), P(None, "band", "pw"), P(None, "band", None))
    return jax.shard_map(
        on_device, mesh=mesh, in_specs=in_specs, out_specs=out_specs, check_vma=False
    )
```

time: 167 us -> 90.1 us (0.54)
  Pallas kernels: 131 us -> 61.7 us
  matrix products: 3.55 us -> 0 us
  starting transfers between devices: 20.7 us -> 17.6 us
  other arithmetic: 2.54 us -> 0.79 us
    pallas_call x1, Pallas kernels: 123 us -> 50.1 us  [lattice(): pl.pallas_call(functools.partial(lattice_kernel, length, planes, chunks,...]
    dot_general x14 -> x0, matrix products: 3.55 us -> none  [the longest x8 2.07 us: pair_dot(): jnp.einsum('bg,cg->bc', left, right, preferred_element_type=jnp.float32)]
    pallas_call x0 -> x1, Pallas kernels: none -> 3.09 us  [project(): pl.pallas_call(functools.partial(project_kernel, bands), out_shape=jax.Sh...]
    ppermute x10 -> x7, starting transfers between devices: 16.8 us -> 13.8 us  [from_all(): lax.ppermute(value, axis, [(k, (k + s) % size) for k in range(size)])]
    transpose x0 -> x2, local copies, waits for them, and re-layouts: none -> 1.75 us  [atom_blocks(): jnp.transpose(matrix, (0, 2, 1))[:, :, None, :]]
    ppermute x10 -> x7, waiting for transfers between devices: 2.01 us -> 0.33 us  [from_all(): lax.ppermute(value, axis, [(k, (k + s) % size) for k in range(size)])]
  transfers between devices with their start and end apart: 16 -> 13, of which waited for: 5 -> 4; matrix products, arithmetic and copies ran while one was open for 5% -> 3% of each run, Pallas kernels for 3% -> 3%
where the time goes in v1:
time: 90.1 us; the launch traced here: 89.7 us
  Pallas kernels  61.7 us (68%)
  starting transfers between devices  17.6 us (20%)
  waiting for transfers between devices  4.76 us (5%)
  local copies, waits for them, and re-layouts  4.12 us (5%)
    pallas_call x1, Pallas kernels, lattice(): pl.pallas_call(functools.partial(lattice_kernel, length, planes, chunks,...  50.1 us
    ppermute x7, starting transfers between devices, from_all(): lax.ppermute(value, axis, [(k, (k + s) % size) for k in range(size)])  13.8 us
    pallas_call x1, Pallas kernels, group_waves(): pl.pallas_call(functools.partial(group_kernel, length, planes, chunks), o...  4.77 us
    ppermute x6, waiting for transfers between devices, swap(): return lax.ppermute(value, axis, [(k, k ^ step) for k in range(size)])  4.42 us
    ppermute x6, starting transfers between devices, swap(): return lax.ppermute(value, axis, [(k, k ^ step) for k in range(size)])  3.81 us
    pallas_call x1, Pallas kernels, finish(): pl.pallas_call(functools.partial(finish_kernel, length, planes, chunks, b...  3.71 us
    pallas_call x1, Pallas kernels, project(): pl.pallas_call(functools.partial(project_kernel, bands), out_shape=jax.Sh...  3.09 us
    unnamed x26, local copies, waits for them, and re-layouts  2.13 us
  transfers between devices with their start and end apart: 13, of which 4 were waited for; matrix products, arithmetic and copies ran while one was open for 3% of the time, Pallas kernels for 3%

profile of v1, /device:TPU:0, one launch (start us, length us, event | category | flops | bytes accessed | tf_op | source)
XLA Modules:
  0.0 89.7 jit_solution(17366695603305643361)
XLA Ops:
  0.6 4.8 %group_waves.1 = (bf16[400,128]{1,0:T(8,128)(2,1)}, f32[1,6144]{1,0:T(1,128)}) custom-call(s32[1,6144]{1,0:T(1,128)} %bitcast.19, bf16[2,6144]{1,0:T(2,128)(2,1)} %bitcast.9), custom_call_target="tpu_custom_call" | custom-call | tf_op jit(solution)/shard_map/group_waves/pallas_call | solution.py:142
  5.4 2.9 %collective-permute-start.3 = (bf16[2,6144]{1,0:T(2,128)(2,1)}, bf16[2,6144]{1,0:T(2,128)(2,1)S(1)}, u32[]{:S(2)}, u32[]{:S(2)}) collective-permute-start(bf16[2,6144]{1,0:T(2,128)(2,1)} %bitcast.10), channel_id=1, source_target_pairs={{0,1},{1,2},{2,3},{3,4},{4,5},{5,6},{6,7},{7,0},{8,9},{9,10},{10,1... | collective-permute-start | bytes 73736 | tf_op jit(solution)/shard_map/ppermute | solution.py:477
  8.3 1.6 %collective-permute-start.4 = (bf16[2,6144]{1,0:T(2,128)(2,1)}, bf16[2,6144]{1,0:T(2,128)(2,1)S(1)}, u32[]{:S(2)}, u32[]{:S(2)}) collective-permute-start(bf16[2,6144]{1,0:T(2,128)(2,1)} %bitcast.11), channel_id=1, source_target_pairs={{0,2},{1,3},{2,4},{3,5},{4,6},{5,7},{6,0},{7,1},{8,10},{9,11},{10,... | collective-permute-start | bytes 73736 | tf_op jit(solution)/shard_map/ppermute | solution.py:477
  9.9 2.6 %collective-permute-start.5 = (bf16[2,6144]{1,0:T(2,128)(2,1)}, bf16[2,6144]{1,0:T(2,128)(2,1)S(1)}, u32[]{:S(2)}, u32[]{:S(2)}) collective-permute-start(bf16[2,6144]{1,0:T(2,128)(2,1)} %bitcast.12), channel_id=1, source_target_pairs={{0,3},{1,4},{2,5},{3,6},{4,7},{5,0},{6,1},{7,2},{8,11},{9,12},{10,... | collective-permute-start | bytes 73736 | tf_op jit(solution)/shard_map/ppermute | solution.py:477
  12.5 1.2 %collective-permute-start.6 = (bf16[2,6144]{1,0:T(2,128)(2,1)}, bf16[2,6144]{1,0:T(2,128)(2,1)S(1)}, u32[]{:S(2)}, u32[]{:S(2)}) collective-permute-start(bf16[2,6144]{1,0:T(2,128)(2,1)} %bitcast.13), channel_id=1, source_target_pairs={{0,4},{1,5},{2,6},{3,7},{4,0},{5,1},{6,2},{7,3},{8,12},{9,13},{10,... | collective-permute-start | bytes 73736 | tf_op jit(solution)/shard_map/ppermute | solution.py:477
  13.7 2.6 %collective-permute-start.7 = (bf16[2,6144]{1,0:T(2,128)(2,1)}, bf16[2,6144]{1,0:T(2,128)(2,1)S(1)}, u32[]{:S(2)}, u32[]{:S(2)}) collective-permute-start(bf16[2,6144]{1,0:T(2,128)(2,1)} %bitcast.14), channel_id=1, source_target_pairs={{0,5},{1,6},{2,7},{3,0},{4,1},{5,2},{6,3},{7,4},{8,13},{9,14},{10,... | collective-permute-start | bytes 73736 | tf_op jit(solution)/shard_map/ppermute | solution.py:477
  16.3 0.9 copy.12
  17.2 0.9 copy.13
  18.1 0.0 collective-permute-done.3.refs_1_
  18.1 1.4 %collective-permute-start.8 = (bf16[2,6144]{1,0:T(2,128)(2,1)}, bf16[2,6144]{1,0:T(2,128)(2,1)S(1)}, u32[]{:S(2)}, u32[]{:S(2)}) collective-permute-start(bf16[2,6144]{1,0:T(2,128)(2,1)} %bitcast.15), channel_id=1, source_target_pairs={{0,6},{1,7},{2,0},{3,1},{4,2},{5,3},{6,4},{7,5},{8,14},{9,15},{10,... | collective-permute-start | bytes 73736 | tf_op jit(solution)/shard_map/ppermute | solution.py:477
  19.5 0.0 collective-permute-done.4.refs_2_
  19.5 1.4 %collective-permute-start.9 = (bf16[2,6144]{1,0:T(2,128)(2,1)}, bf16[2,6144]{1,0:T(2,128)(2,1)S(1)}, u32[]{:S(2)}, u32[]{:S(2)}) collective-permute-start(bf16[2,6144]{1,0:T(2,128)(2,1)} %bitcast.16), channel_id=1, source_target_pairs={{0,7},{1,0},{2,1},{3,2},{4,3},{5,4},{6,5},{7,6},{8,15},{9,8},{10,9... | collective-permute-start | bytes 73736 | tf_op jit(solution)/shard_map/ppermute | solution.py:477
  21.0 1.6 %collective-permute-start.1 = (bf16[400,128]{1,0:T(8,128)(2,1)}, bf16[400,128]{1,0:T(8,128)(2,1)S(1)}, u32[]{:S(2)}, u32[]{:S(2)}) collective-permute-start(bf16[400,128]{1,0:T(8,128)(2,1)} %get-tuple-element.13.refs_0_), channel_id=1, source_target_pairs={{0,16},{8,24},{16,0},{24,8},{1,17},{9,25},{17,1},{25,9},{2,18},{10... | collective-permute-start | bytes 307208 | tf_op jit(solution)/shard_map/ppermute | solution.py:472
  22.6 0.3 collective-permute-start.2
  22.8 0.1 broadcast_multiply_fusion.1
  22.9 0.1 mul.37
  23.1 0.1 mul.40
  23.2 0.3 collective-permute-done.9.refs_7_
  23.6 0.2 copy-done.11
  23.8 0.6 copy-done.12
  24.4 3.1 %project.1.refs_4_ = f32[16,128]{1,0:T(8,128)} custom-call(bf16[2,6144]{1,0:T(2,128)(2,1)} %bitcast.17, bf16[2,6144]{1,0:T(2,128)(2,1)} %copy-done.6, bf16[2,6144]{1,0:T(2,128)(2,1)} %copy-done.7, bf16[2,6144]{1,0:T(2,128)(2,1)} %copy-done.8, bf16[2,6144]{1,0:T(2,128)(2,1)} %copy-done.9, bf16[2,6144]{1,0:T(2,128)(2,1)} %copy-done.10, ...), custom_call_target="tpu_custom_call" | custom-call | tf_op jit(solution)/shard_map/project/pallas_call | solution.py:387
  27.5 0.7 collective-permute-done.2.refs_3_
  28.2 0.6 copy-done.2
  28.8 50.1 %lattice.1 = (bf16[240,128]{1,0:T(8,128)(2,1)}, bf16[240,128]{1,0:T(8,128)(2,1)}, bf16[240,128]{1,0:T(8,128)(2,1)}, bf16[240,128]{1,0:T(8,128)(2,1)}) custom-call(bf16[400,128]{1,0:T(8,128)(2,1)} %get-tuple-element.13.refs_0_, bf16[400,128]{1,0:T(8,128)(2,1)} %copy-done, bf16[400,128]{1,0:T(8,128)(2,1)} %copy-done.1, bf16[400,128]{1,0:T(8,128)(2,1)} %copy-done.2, ...), custom_call_target="tpu_custom_call" | custom-call | tf_op jit(solution)/shard_map/lattice/pallas_call | solution.py:341
  79.0 0.4 collective-permute-start.10
  79.4 1.5 %collective-permute-start.11 = (bf16[240,128]{1,0:T(8,128)(2,1)}, bf16[240,128]{1,0:T(8,128)(2,1)S(1)}, u32[]{:S(2)}, u32[]{:S(2)}) collective-permute-start(bf16[240,128]{1,0:T(8,128)(2,1)} %get-tuple-element.17), channel_id=1, source_target_pairs={{0,16},{8,24},{16,0},{24,8},{1,17},{9,25},{17,1},{25,9},{2,18},{10... | collective-permute-start | bytes 184328 | tf_op jit(solution)/shard_map/ppermute | solution.py:472
  80.9 0.0 collective-permute-start.12
  80.9 0.7 select_maximum_fusion.refs_8_
  81.6 2.2 %collective-permute-done.11.refs_2_ = bf16[240,128]{1,0:T(8,128)(2,1)S(1)} collective-permute-done((bf16[240,128]{1,0:T(8,128)(2,1)}, bf16[240,128]{1,0:T(8,128)(2,1)S(1)}, u32[]{:S(2)}, u32[]{:S(2)}) %collective-permute-start.11) | collective-permute-done | bytes 61472 | tf_op jit(solution)/shard_map/ppermute | solution.py:472
  83.8 1.6 %collective-permute-done.12.refs_3_ = bf16[240,128]{1,0:T(8,128)(2,1)S(1)} collective-permute-done((bf16[240,128]{1,0:T(8,128)(2,1)}, bf16[240,128]{1,0:T(8,128)(2,1)S(1)}, u32[]{:S(2)}, u32[]{:S(2)}) %collective-permute-start.12) | collective-permute-done | bytes 61472 | tf_op jit(solution)/shard_map/ppermute | solution.py:472
  85.4 0.6 copy-done.5
  86.0 3.7 %finish.1 = (bf16[2,6144]{1,0:T(2,128)(2,1)}, bf16[2,6144]{1,0:T(2,128)(2,1)}, f32[2,8]{1,0:T(2,128)}) custom-call(bf16[240,128]{1,0:T(8,128)(2,1)} %get-tuple-element.15.refs_0_, bf16[240,128]{1,0:T(8,128)(2,1)} %copy-done.3, bf16[240,128]{1,0:T(8,128)(2,1)} %copy-done.4, bf16[240,128]{1,0:T(8,128)(2,1)} %copy-done.5, f32[1,6144]{1,0:T(1,128)} %get-tuple-element.19.refs_4_, ...), custom_call_target="tpu_custom_call" | custom-call | tf_op jit(solution)/shard_map/finish/pallas_call | solution.py:458
  (31 shorter events, 0.1 us)
Async XLA Ops:
  5.4 12.7 %collective-permute-start.3 = (bf16[2,6144]{1,0:T(2,128)(2,1)}, bf16[2,6144]{1,0:T(2,128)(2,1)S(1)}, u32[]{:S(2)}, u32[]{:S(2)}) collective-permute-start(bf16[2,6144]{1,0:T(2,128)(2,1)} %bitcast.10), channel_id=1, source_target_pairs={{0,1},{1,2},{2,3},{3,4},{4,5},{5,6},{6,7},{7,0},{8,9},{9,10},{10,1... | collective-permute-start | bytes 73736 | tf_op jit(solution)/shard_map/ppermute | solution.py:477
  8.3 11.2 %collective-permute-start.4 = (bf16[2,6144]{1,0:T(2,128)(2,1)}, bf16[2,6144]{1,0:T(2,128)(2,1)S(1)}, u32[]{:S(2)}, u32[]{:S(2)}) collective-permute-start(bf16[2,6144]{1,0:T(2,128)(2,1)} %bitcast.11), channel_id=1, source_target_pairs={{0,2},{1,3},{2,4},{3,5},{4,6},{5,7},{6,0},{7,1},{8,10},{9,11},{10,... | collective-permute-start | bytes 73736 | tf_op jit(solution)/shard_map/ppermute | solution.py:477
  9.9 11.0 %collective-permute-start.5 = (bf16[2,6144]{1,0:T(2,128)(2,1)}, bf16[2,6144]{1,0:T(2,128)(2,1)S(1)}, u32[]{:S(2)}, u32[]{:S(2)}) collective-permute-start(bf16[2,6144]{1,0:T(2,128)(2,1)} %bitcast.12), channel_id=1, source_target_pairs={{0,3},{1,4},{2,5},{3,6},{4,7},{5,0},{6,1},{7,2},{8,11},{9,12},{10,... | collective-permute-start | bytes 73736 | tf_op jit(solution)/shard_map/ppermute | solution.py:477
  12.5 8.5 %collective-permute-start.6 = (bf16[2,6144]{1,0:T(2,128)(2,1)}, bf16[2,6144]{1,0:T(2,128)(2,1)S(1)}, u32[]{:S(2)}, u32[]{:S(2)}) collective-permute-start(bf16[2,6144]{1,0:T(2,128)(2,1)} %bitcast.13), channel_id=1, source_target_pairs={{0,4},{1,5},{2,6},{3,7},{4,0},{5,1},{6,2},{7,3},{8,12},{9,13},{10,... | collective-permute-start | bytes 73736 | tf_op jit(solution)/shard_map/ppermute | solution.py:477
  13.7 8.8 %collective-permute-start.7 = (bf16[2,6144]{1,0:T(2,128)(2,1)}, bf16[2,6144]{1,0:T(2,128)(2,1)S(1)}, u32[]{:S(2)}, u32[]{:S(2)}) collective-permute-start(bf16[2,6144]{1,0:T(2,128)(2,1)} %bitcast.14), channel_id=1, source_target_pairs={{0,5},{1,6},{2,7},{3,0},{4,1},{5,2},{6,3},{7,4},{8,13},{9,14},{10,... | collective-permute-start | bytes 73736 | tf_op jit(solution)/shard_map/ppermute | solution.py:477
  18.1 5.5 %copy-start.6 = (bf16[2,6144]{1,0:T(2,128)(2,1)}, bf16[2,6144]{1,0:T(2,128)(2,1)S(1)}, u32[]{:S(2)}) copy-start(bf16[2,6144]{1,0:T(2,128)(2,1)S(1)} %collective-permute-done.3.refs_1_) | copy-start | bytes 73732
  18.1 5.1 %collective-permute-start.8 = (bf16[2,6144]{1,0:T(2,128)(2,1)}, bf16[2,6144]{1,0:T(2,128)(2,1)S(1)}, u32[]{:S(2)}, u32[]{:S(2)}) collective-permute-start(bf16[2,6144]{1,0:T(2,128)(2,1)} %bitcast.15), channel_id=1, source_target_pairs={{0,6},{1,7},{2,0},{3,1},{4,2},{5,3},{6,4},{7,5},{8,14},{9,15},{10,... | collective-permute-start | bytes 73736 | tf_op jit(solution)/shard_map/ppermute | solution.py:477
  19.5 4.0 %copy-start.7 = (bf16[2,6144]{1,0:T(2,128)(2,1)}, bf16[2,6144]{1,0:T(2,128)(2,1)S(1)}, u32[]{:S(2)}) copy-start(bf16[2,6144]{1,0:T(2,128)(2,1)S(1)} %collective-permute-done.4.refs_2_) | copy-start | bytes 73732
  19.5 4.0 %collective-permute-start.9 = (bf16[2,6144]{1,0:T(2,128)(2,1)}, bf16[2,6144]{1,0:T(2,128)(2,1)S(1)}, u32[]{:S(2)}, u32[]{:S(2)}) collective-permute-start(bf16[2,6144]{1,0:T(2,128)(2,1)} %bitcast.16), channel_id=1, source_target_pairs={{0,7},{1,0},{2,1},{3,2},{4,3},{5,4},{6,5},{7,6},{8,15},{9,8},{10,9... | collective-permute-start | bytes 73736 | tf_op jit(solution)/shard_map/ppermute | solution.py:477
  20.9 2.6 %copy-start.8 = (bf16[2,6144]{1,0:T(2,128)(2,1)}, bf16[2,6144]{1,0:T(2,128)(2,1)S(1)}, u32[]{:S(2)}) copy-start(bf16[2,6144]{1,0:T(2,128)(2,1)S(1)} %collective-permute-done.5.refs_3_) | copy-start | bytes 73732
  20.9 6.6 %collective-permute-start = (bf16[400,128]{1,0:T(8,128)(2,1)}, bf16[400,128]{1,0:T(8,128)(2,1)S(1)}, u32[]{:S(2)}, u32[]{:S(2)}) collective-permute-start(bf16[400,128]{1,0:T(8,128)(2,1)} %get-tuple-element.13.refs_0_), channel_id=1, source_target_pairs={{0,8},{8,0},{16,24},{24,16},{1,9},{9,1},{17,25},{25,17},{2,10},{10... | collective-permute-start | bytes 307208 | tf_op jit(solution)/shard_map/ppermute | solution.py:472
  21.0 2.6 %copy-start.9 = (bf16[2,6144]{1,0:T(2,128)(2,1)}, bf16[2,6144]{1,0:T(2,128)(2,1)S(1)}, u32[]{:S(2)}) copy-start(bf16[2,6144]{1,0:T(2,128)(2,1)S(1)} %collective-permute-done.6.refs_4_) | copy-start | bytes 73732
  21.0 6.5 %collective-permute-start.1 = (bf16[400,128]{1,0:T(8,128)(2,1)}, bf16[400,128]{1,0:T(8,128)(2,1)S(1)}, u32[]{:S(2)}, u32[]{:S(2)}) collective-permute-start(bf16[400,128]{1,0:T(8,128)(2,1)} %get-tuple-element.13.refs_0_), channel_id=1, source_target_pairs={{0,16},{8,24},{16,0},{24,8},{1,17},{9,25},{17,1},{25,9},{2,18},{10... | collective-permute-start | bytes 307208 | tf_op jit(solution)/shard_map/ppermute | solution.py:472
  22.6 1.0 %copy-start.10 = (bf16[2,6144]{1,0:T(2,128)(2,1)}, bf16[2,6144]{1,0:T(2,128)(2,1)S(1)}, u32[]{:S(2)}) copy-start(bf16[2,6144]{1,0:T(2,128)(2,1)S(1)} %collective-permute-done.7.refs_5_) | copy-start | bytes 73732
  22.6 5.6 %collective-permute-start.2 = (bf16[400,128]{1,0:T(8,128)(2,1)}, bf16[400,128]{1,0:T(8,128)(2,1)S(1)}, u32[]{:S(2)}, u32[]{:S(2)}) collective-permute-start(bf16[400,128]{1,0:T(8,128)(2,1)} %get-tuple-element.13.refs_0_), channel_id=1, source_target_pairs={{0,24},{8,16},{16,8},{24,0},{1,25},{9,17},{17,9},{25,1},{2,26},{10... | collective-permute-start | bytes 307208 | tf_op jit(solution)/shard_map/ppermute | solution.py:472
  23.2 0.6 copy-start.11
  23.8 0.6 copy-start.12
  27.5 0.7 copy-start
  27.5 0.7 copy-start.1
  28.2 0.6 copy-start.2
  79.0 2.6 %collective-permute-start.10 = (bf16[240,128]{1,0:T(8,128)(2,1)}, bf16[240,128]{1,0:T(8,128)(2,1)S(1)}, u32[]{:S(2)}, u32[]{:S(2)}) collective-permute-start(bf16[240,128]{1,0:T(8,128)(2,1)} %get-tuple-element.16), channel_id=1, source_target_pairs={{0,8},{8,0},{16,24},{24,16},{1,9},{9,1},{17,25},{25,17},{2,10},{10... | collective-permute-start | bytes 184328 | tf_op jit(solution)/shard_map/ppermute | solution.py:472
  79.4 4.4 %collective-permute-start.11 = (bf16[240,128]{1,0:T(8,128)(2,1)}, bf16[240,128]{1,0:T(8,128)(2,1)S(1)}, u32[]{:S(2)}, u32[]{:S(2)}) collective-permute-start(bf16[240,128]{1,0:T(8,128)(2,1)} %get-tuple-element.17), channel_id=1, source_target_pairs={{0,16},{8,24},{16,0},{24,8},{1,17},{9,25},{17,1},{25,9},{2,18},{10... | collective-permute-start | bytes 184328 | tf_op jit(solution)/shard_map/ppermute | solution.py:472
  80.9 4.5 %collective-permute-start.12 = (bf16[240,128]{1,0:T(8,128)(2,1)}, bf16[240,128]{1,0:T(8,128)(2,1)S(1)}, u32[]{:S(2)}, u32[]{:S(2)}) collective-permute-start(bf16[240,128]{1,0:T(8,128)(2,1)} %get-tuple-element.18), channel_id=1, source_target_pairs={{0,24},{8,16},{16,8},{24,0},{1,25},{9,17},{17,9},{25,1},{2,26},{10... | collective-permute-start | bytes 184328 | tf_op jit(solution)/shard_map/ppermute | solution.py:472
  81.6 3.7 %copy-start.3 = (bf16[240,128]{1,0:T(8,128)(2,1)}, bf16[240,128]{1,0:T(8,128)(2,1)S(1)}, u32[]{:S(2)}) copy-start(bf16[240,128]{1,0:T(8,128)(2,1)S(1)} %collective-permute-done.10.refs_1_) | copy-start | bytes 184324
  83.8 1.6 %copy-start.4 = (bf16[240,128]{1,0:T(8,128)(2,1)}, bf16[240,128]{1,0:T(8,128)(2,1)S(1)}, u32[]{:S(2)}) copy-start(bf16[240,128]{1,0:T(8,128)(2,1)S(1)} %collective-permute-done.11.refs_2_) | copy-start | bytes 184324
  85.4 0.6 copy-start.5

commit v2 on v1

--- a/solution.py
+++ b/solution.py
@@ -160,15 +160,19 @@
     pays = refs[:blocks]
     sums_ref, vloc_hbm, own_ref, along_z, along_x = refs[blocks : blocks + 5]
     outs = refs[blocks + 5 : 2 * blocks + 5]
-    wide, cells_e, cells_o, phases, vloc, vloc_l, vloc_h, result, maps, maps_s, sems = refs[2 * blocks + 5 :]
+    wide, cells_e, cells_o, phases, vloc, result, maps, maps_s, sems = refs[2 * blocks + 5 :]
     half = length // 2
     rows = round_up(planes, 8)
     both = 2 * rows
     pitch = both + 1
     spare = blocks * planes
     me = lax.axis_index("pw")
-    load = pltpu.make_async_copy(vloc_hbm, vloc, sems.at[0])
-    load.start()
+
+    def load(k, _):
+        pltpu.make_async_copy(vloc_hbm.at[:, k, :], vloc.at[k], sems.at[0]).start()
+        return 0
+
+    lax.fori_loop(0, planes, load, 0)
     for s in range(blocks):
         maps[s * 8 : (s + 1) * 8, :] = pays[s][4 * chunks : 4 * chunks + 16, :].astype(jnp.int32)[:8]
     fetch = pltpu.make_async_copy(maps, maps_s, sems.at[1])
@@ -183,8 +187,8 @@
     level = iota((2 * LANES, LANES), 0)
     level_y = level[:length]
     group = 4 if blocks % 4 == 0 else 1
-    ahead = 4 if blocks == group else 1
-    batch = 4 if planes % 4 == 0 else 1
+    ahead = 8 if blocks == group else 1
+    batch = 8 if planes % 8 == 0 else 1
     turns = (used + ahead - 1) // ahead
 
     def place(s, c):
@@ -201,10 +205,18 @@
     def pick_z(s, c):
         return where_bf16(level == row(s, 3, c), 1.0)
 
+    def phases_of(todo):
+        wanted = [where_bf16(level_y == row(s, 2, c), 1.0) for s, c in todo]
+        found = []
+        for n in range(0, len(todo), 2):
+            both_phases = dot(own, jnp.concatenate(wanted[n : n + 2], axis=1))
+            found += [both_phases[:, :LANES], both_phases[:, LANES:]][: len(wanted[n : n + 2])]
+        return found
+
     def forward(turn, _):
         for base in range(0, blocks, group):
             todo = items(turn, base)
-            found = [dot(own, where_bf16(level_y == row(s, 2, c), 1.0)) for s, c in todo]
+            found = phases_of(todo)
             mixed = []
             for (s, c), phase in zip(todo, found):
                 phases[s * chunks + c] = phase.astype(jnp.bfloat16)
@@ -229,17 +241,7 @@
         return 0
 
     lax.fori_loop(0, turns, forward, 0)
-    load.wait()
-    step = planes + 1 - planes % 2
-
-    def spread(x, _):
-        plane = vloc[x]
-        span = pl.ds(x * step, planes)
-        vloc_l[span, :] = plane[:, :LANES]
-        vloc_h[span, :] = jnp.concatenate([plane[:, half:], plane[:, : LANES - half]], axis=1)
-        return 0
-
-    lax.fori_loop(0, length, spread, 0, unroll=4)
+    pltpu.make_async_copy(vloc, vloc, sems.at[0]).wait()
 
     def strided(start):
         return pl.ds(start, half, stride=pitch)
@@ -278,9 +280,9 @@
         for j, k in enumerate(many):
             even = dot(along_x[0], stacked(2 * j))
             odd = dot(along_x[1], stacked(2 * j + 1))
-            near, far = pl.ds(k, half, stride=step), pl.ds(k + half * step, half, stride=step)
-            near = beside(vloc_l[near, :], vloc_h[near, :])
-            far = beside(vloc_l[far, :], vloc_h[far, :])
+            field = vloc[k]
+            field = beside(field[:, :LANES], beside(field[:, half:], field[:, : LANES - half]))
+            near, far = field[:half], field[half:]
             first = (even + odd) * above(near, near)
             second = (even - odd) * above(far, far)
             for table, value in ((along_x[2], first + second), (along_x[3], first - second)):
@@ -348,9 +350,7 @@
             pltpu.VMEM((round_up((blocks * planes + 1) * (2 * rows + 1), 8), LANES), jnp.float32),
             pltpu.VMEM((round_up((blocks * planes + 1) * (2 * rows + 1), 8), LANES), jnp.float32),
             pltpu.VMEM((blocks * chunks, 2 * rows, LANES), jnp.bfloat16),
-            pltpu.VMEM((length, planes, length), jnp.float32),
-            pltpu.VMEM((round_up(length * (planes + 1), 8), LANES), jnp.float32),
-            pltpu.VMEM((round_up(length * (planes + 1), 8), LANES), jnp.float32),
+            pltpu.VMEM((planes, length, length), jnp.float32),
             pltpu.VMEM((blocks * 2 * chunks, LANES), jnp.float32),
             pltpu.VMEM((blocks * 8, LANES), jnp.int32),
             pltpu.SMEM((blocks * 8, LANES), jnp.int32),
@@ -362,34 +362,36 @@
 
 
 def project_kernel(bands, *refs):
-    every = [ref[...].astype(jnp.float32) for ref in refs[:bands]]
-    beta_ref, out_ref = refs[bands:]
-    count = beta_ref.shape[1]
+    every = [ref[...].astype(jnp.float32) for ref in refs[:-2]]
+    beta_ref, out_ref = refs[-2:]
+    count = beta_ref.shape[0] // 2
     rows = out_ref.shape[0] // 2
-    pad = [jnp.zeros_like(every[0][:1])] * (rows - bands)
-    stack = [value[:1] for value in every] + pad + [value[1:] for value in every] + pad
-    stack = jnp.concatenate(stack, axis=0).astype(jnp.bfloat16)
-
-    def against(re, im):
-        on_re, on_im = dot_lanes(stack, re), dot_lanes(stack, im)
-        return jnp.concatenate([on_re[:rows] + on_im[rows:], on_re[rows:] - on_im[:rows]], axis=0)
-
+    pad = [jnp.zeros((rows - bands, every[0].shape[2]), jnp.float32)] if rows > bands else []
+    re = jnp.concatenate([value[0] for value in every] + pad, axis=0)
+    im = jnp.concatenate([value[1] for value in every] + pad, axis=0)
+    found = dot_lanes(beta_ref[...], jnp.concatenate([re, im], axis=0).astype(jnp.bfloat16))
+    on_re, on_im = found[:count], found[count:]
+    found = jnp.concatenate([on_re[:, :rows] + on_im[:, rows:], on_re[:, rows:] - on_im[:, :rows]], axis=1)
     out_ref[...] = jnp.zeros_like(out_ref)
-    out_ref[:, :count] = against(beta_ref[0], beta_ref[1])
-    shape = (16, every[0].shape[1])
-    own = [jnp.broadcast_to(every[0][n : n + 1], shape).astype(jnp.bfloat16) for n in range(2)]
-    over = against(*own)[:, :1]
+    out_ref[:, :count] = found.T
+    own_re, own_im = re[:1], im[:1]
+    over = jnp.concatenate(
+        [
+            jnp.sum(re * own_re + im * own_im, axis=1, keepdims=True),
+            jnp.sum(im * own_re - re * own_im, axis=1, keepdims=True),
+        ],
+        axis=0,
+    )
     out_ref[...] = jnp.where(iota(out_ref.shape, 1) == count, over, out_ref[...])
 
 
-def project(every, beta):
-    bands = len(every)
+def project(every, beta, bands):
     return pl.pallas_call(
         functools.partial(project_kernel, bands),
         out_shape=jax.ShapeDtypeStruct((2 * round_up(bands, 8), LANES), jnp.float32),
         compiler_params=pltpu.CompilerParams(vmem_limit_bytes=VMEM_LIMIT),
         name="project",
-    )(*every, beta)
+    )(*every, beta.reshape(2 * beta.shape[1], beta.shape[2]))
 
 
 def finish_kernel(length, planes, chunks, blocks, bands, *refs):
@@ -418,8 +420,12 @@
     over = iota((half_size, LANES), 1) == count
     gram_re = own_re * each_re + own_im * each_im + jnp.where(over, sums[:half_size], 0.0)
     gram_im = own_re * each_im - own_im * each_re + jnp.where(over, sums[half_size:], 0.0)
-    turn = lax.axis_index("band") - lax.broadcasted_iota(jnp.int32, (half_size, bands), 0)
-    turn = jnp.where(turn < 0, turn + bands, turn)
+    slot_at = lax.broadcasted_iota(jnp.int32, (half_size, bands), 0)
+    if doubles(bands):
+        turn = lax.axis_index("band") ^ slot_at
+    else:
+        turn = lax.axis_index("band") - slot_at
+        turn = jnp.where(turn < 0, turn + bands, turn)
     here = turn == lax.broadcasted_iota(jnp.int32, (half_size, bands), 1)
     here = here & (lax.broadcasted_iota(jnp.int32, (half_size, bands), 0) < bands)
     for n, value in enumerate((gram_re, gram_im)):
@@ -472,9 +478,32 @@
     return lax.ppermute(value, axis, [(k, k ^ step) for k in range(size)])
 
 
-def from_all(value, axis):
+def doubles(size):
+    return size & (size - 1) == 0
+
+
+def from_blocks(value, axis):
     size = lax.axis_size(axis)
-    return [value] + [lax.ppermute(value, axis, [(k, (k + s) % size) for k in range(size)]) for s in range(1, size)]
+    found = {0: value}
+    step = size // 2
+    while step:
+        found.update({s + step: swap(found[s], axis, step) for s in list(found)})
+        step //= 2
+    return [found[s] for s in range(size)]
+
+
+def from_bands(value, axis):
+    size = lax.axis_size(axis)
+    if not doubles(size):
+        pairs = [[(k, (k + s) % size) for k in range(size)] for s in range(1, size)]
+        return [value] + [lax.ppermute(value, axis, pair) for pair in pairs]
+    held = [value]
+    step = 1
+    while step < size:
+        value = jnp.concatenate(held, axis=1)
+        held = [value, swap(value, axis, step)]
+        step *= 2
+    return held
 
 
 def atom_blocks(matrix):
@@ -495,9 +524,8 @@
     mine = psi.reshape(2, width)
     atoms = jnp.concatenate([atom_blocks(dmat), atom_blocks(qmat)], axis=1)
     pay, slot = group_waves(index, mine, length, planes, chunks)
-    pays = [pay] + [swap(pay, "pw", s) for s in range(1, blocks)]
-    later, _ = lax.optimization_barrier((mine, pay))
-    sums = project(from_all(later, "band"), beta)
+    pays = from_blocks(pay, "pw")
+    sums = project(from_bands(psi, "band"), beta, bands)
     outs = lattice(pays, sums, vloc, length, planes, chunks)
     parts = [outs[0]] + [swap(outs[s], "pw", s) for s in range(1, blocks)]
     hpsi, spsi, gram = finish(parts, slot, index, mine, beta, atoms, length, planes, chunks, bands)

time: 90.1 us -> 77.8 us (0.86)
  Pallas kernels: 61.7 us -> 52.2 us
  starting transfers between devices: 17.6 us -> 10.8 us
  waiting for transfers between devices: 4.76 us -> 8.26 us
  local copies, waits for them, and re-layouts: 4.12 us -> 5.28 us
    ppermute x7 -> x0, starting transfers between devices: 13.8 us -> none  [from_all(): lax.ppermute(value, axis, [(k, (k + s) % size) for k in range(size)])]
    pallas_call x1, Pallas kernels: 50.1 us -> 40.8 us  [lattice(): pl.pallas_call(functools.partial(lattice_kernel, length, planes, chunks,...]
    ppermute x6 -> x9, starting transfers between devices: 3.81 us -> 10.8 us  [swap(): return lax.ppermute(value, axis, [(k, k ^ step) for k in range(size)])]
    ppermute x6 -> x9, waiting for transfers between devices: 4.42 us -> 8.26 us  [swap(): return lax.ppermute(value, axis, [(k, k ^ step) for k in range(size)])]
    unnamed x26 -> x17, local copies, waits for them, and re-layouts: 2.13 us -> 3.29 us
  transfers between devices with their start and end apart: 13 -> 9, of which waited for: 4 -> 4; matrix products, arithmetic and copies ran while one was open for 3% -> 4% of each run, Pallas kernels for 3% -> 10%
where the time goes in v2:
time: 77.8 us; the launch traced here: 78.3 us
  Pallas kernels  52.2 us (67%)
  starting transfers between devices  10.8 us (14%)
  waiting for transfers between devices  8.26 us (11%)
  local copies, waits for them, and re-layouts  5.28 us (7%)
  other arithmetic  1.07 us (1%)
    pallas_call x1, Pallas kernels, lattice(): pl.pallas_call(functools.partial(lattice_kernel, length, planes, chunks,...  40.8 us
    ppermute x9, starting transfers between devices, swap(): return lax.ppermute(value, axis, [(k, k ^ step) for k in range(size)])  10.8 us
    ppermute x9, waiting for transfers between devices, swap(): return lax.ppermute(value, axis, [(k, k ^ step) for k in range(size)])  8.26 us
    pallas_call x1, Pallas kernels, group_waves(): pl.pallas_call(functools.partial(group_kernel, length, planes, chunks), o...  4.78 us
    pallas_call x1, Pallas kernels, finish(): pl.pallas_call(functools.partial(finish_kernel, length, planes, chunks, b...  3.71 us
    unnamed x17, local copies, waits for them, and re-layouts  3.29 us
    pallas_call x1, Pallas kernels, project(): pl.pallas_call(functools.partial(project_kernel, bands), out_shape=jax.Sh...  2.94 us
    transpose x2, local copies, waits for them, and re-layouts, atom_blocks(): jnp.transpose(matrix, (0, 2, 1))[:, :, None, :]  1.75 us
  transfers between devices with their start and end apart: 9, of which 4 were waited for; matrix products, arithmetic and copies ran while one was open for 4% of the time, Pallas kernels for 10%

profile of v2, /device:TPU:0, one launch (start us, length us, event | category | flops | bytes accessed | tf_op | source)
XLA Modules:
  0.0 78.3 jit_solution(295068312067276204)
XLA Ops:
  0.6 0.8 copy.14
  1.4 3.0 %collective-permute-start.3 = (bf16[2,1,6144]{2,1,0:T(2,128)(2,1)S(1)}, bf16[2,1,6144]{2,1,0:T(2,128)(2,1)S(1)}, u32[]{:S(2)}, u32[]{:S(2)}) collective-permute-start(bf16[2,1,6144]{2,1,0:T(2,128)(2,1)S(1)} %copy.14), channel_id=1, source_target_pairs={{0,1},{1,0},{2,3},{3,2},{4,5},{5,4},{6,7},{7,6},{8,9},{9,8},{10,11... | collective-permute-start | bytes 73736 | tf_op jit(solution)/shard_map/ppermute | solution.py:478
  4.4 4.8 %group_waves.1 = (bf16[400,128]{1,0:T(8,128)(2,1)}, f32[1,6144]{1,0:T(1,128)}) custom-call(s32[1,6144]{1,0:T(1,128)} %bitcast.13, bf16[2,6144]{1,0:T(2,128)(2,1)} %bitcast.11), custom_call_target="tpu_custom_call" | custom-call | tf_op jit(solution)/shard_map/group_waves/pallas_call | solution.py:142
  9.2 1.5 %collective-permute-start.1 = (bf16[400,128]{1,0:T(8,128)(2,1)}, bf16[400,128]{1,0:T(8,128)(2,1)S(1)}, u32[]{:S(2)}, u32[]{:S(2)}) collective-permute-start(bf16[400,128]{1,0:T(8,128)(2,1)} %get-tuple-element.12.refs_0_), channel_id=1, source_target_pairs={{0,16},{8,24},{16,0},{24,8},{1,17},{9,25},{17,1},{25,9},{2,18},{10... | collective-permute-start | bytes 307208 | tf_op jit(solution)/shard_map/ppermute | solution.py:478
  10.7 0.0 collective-permute-start
  10.7 0.0 collective-permute-done.3
  10.7 0.1 pad_maximum_fusion.1
  10.8 1.6 %collective-permute-start.4 = (bf16[2,2,6144]{2,1,0:T(2,128)(2,1)S(1)}, bf16[2,2,6144]{2,1,0:T(2,128)(2,1)S(1)}, u32[]{:S(2)}, u32[]{:S(2)}) collective-permute-start(bf16[2,2,6144]{2,1,0:T(2,128)(2,1)S(1)} %pad_maximum_fusion.1), channel_id=1, source_target_pairs={{0,2},{1,3},{2,0},{3,1},{4,6},{5,7},{6,4},{7,5},{8,10},{9,11},{10,... | collective-permute-start | bytes 147464 | tf_op jit(solution)/shard_map/ppermute | solution.py:478
  12.5 0.9 %copy.15 = f32[4,18,18]{2,1,0:T(8,128)S(1)} copy(f32[4,18,18]{1,0,2:T(4,128)} %bitcast.15) | data formatting | bytes 10368 | tf_op jit(solution)/shard_map/transpose | solution.py:512
  13.4 0.9 %copy.16 = f32[4,18,18]{2,1,0:T(8,128)S(1)} copy(f32[4,18,18]{1,0,2:T(4,128)} %bitcast.16) | data formatting | bytes 10368 | tf_op jit(solution)/shard_map/transpose | solution.py:512
  14.2 0.8 %collective-permute-done.4 = bf16[2,2,6144]{2,1,0:T(2,128)(2,1)S(1)} collective-permute-done((bf16[2,2,6144]{2,1,0:T(2,128)(2,1)S(1)}, bf16[2,2,6144]{2,1,0:T(2,128)(2,1)S(1)}, u32[]{:S(2)}, u32[]{:S(2)}) %collective-permute-start.4) | collective-permute-done | bytes 49184 | tf_op jit(solution)/shard_map/ppermute | solution.py:478
  15.1 0.2 pad_maximum_fusion.refs_0_
  15.2 2.7 %collective-permute-start.5 = (bf16[2,4,6144]{2,1,0:T(4,128)(2,1)S(1)}, bf16[2,4,6144]{2,1,0:T(4,128)(2,1)S(1)}, u32[]{:S(2)}, u32[]{:S(2)}) collective-permute-start(bf16[2,4,6144]{2,1,0:T(4,128)(2,1)S(1)} %pad_maximum_fusion.refs_0_), channel_id=1, source_target_pairs={{0,4},{1,5},{2,6},{3,7},{4,0},{5,1},{6,2},{7,3},{8,12},{9,13},{10,... | collective-permute-start | bytes 294920 | tf_op jit(solution)/shard_map/ppermute | solution.py:478
  17.9 0.0 collective-permute-done.1.refs_2_
  17.9 0.1 broadcast_multiply_fusion.1
  18.0 0.1 mul.37
  18.2 0.1 mul.40
  18.3 4.5 %collective-permute-done.5.refs_1_ = bf16[2,4,6144]{2,1,0:T(4,128)(2,1)S(1)} collective-permute-done((bf16[2,4,6144]{2,1,0:T(4,128)(2,1)S(1)}, bf16[2,4,6144]{2,1,0:T(4,128)(2,1)S(1)}, u32[]{:S(2)}, u32[]{:S(2)}) %collective-permute-start.5) | collective-permute-done | bytes 98336 | tf_op jit(solution)/shard_map/ppermute | solution.py:478
  22.7 0.6 copy-done.4
  23.4 2.9 %project.1.refs_4_ = f32[16,128]{1,0:T(8,128)} custom-call(bf16[2,4,6144]{2,1,0:T(4,128)(2,1)} %copy-done, bf16[2,4,6144]{2,1,0:T(4,128)(2,1)} %copy-done.4, bf16[144,6144]{1,0:T(8,128)(2,1)} %bitcast.10), custom_call_target="tpu_custom_call" | custom-call | tf_op jit(solution)/shard_map/project/pallas_call | solution.py:389
  26.3 0.6 copy-done.2
  27.0 0.6 copy-done.3
  27.6 40.8 %lattice.1 = (bf16[240,128]{1,0:T(8,128)(2,1)}, bf16[240,128]{1,0:T(8,128)(2,1)}, bf16[240,128]{1,0:T(8,128)(2,1)}, bf16[240,128]{1,0:T(8,128)(2,1)}) custom-call(bf16[400,128]{1,0:T(8,128)(2,1)} %get-tuple-element.12.refs_0_, bf16[400,128]{1,0:T(8,128)(2,1)} %copy-done.2, bf16[400,128]{1,0:T(8,128)(2,1)} %copy-done.1, bf16[400,128]{1,0:T(8,128)(2,1)} %copy-done.3, ...), custom_call_target="tpu_custom_call" | custom-call | tf_op jit(solution)/shard_map/lattice/pallas_call | solution.py:343
  68.4 0.1 collective-permute-start.6
  68.4 0.6 collective-permute-start.7
  69.1 1.2 %collective-permute-start.8 = (bf16[240,128]{1,0:T(8,128)(2,1)}, bf16[240,128]{1,0:T(8,128)(2,1)S(1)}, u32[]{:S(2)}, u32[]{:S(2)}) collective-permute-start(bf16[240,128]{1,0:T(8,128)(2,1)} %get-tuple-element.16), channel_id=1, source_target_pairs={{0,24},{8,16},{16,8},{24,0},{1,25},{9,17},{17,9},{25,1},{2,26},{10... | collective-permute-start | bytes 184328 | tf_op jit(solution)/shard_map/ppermute | solution.py:478
  70.3 0.7 select_maximum_fusion.refs_8_
  71.0 2.6 %collective-permute-done.7.refs_2_ = bf16[240,128]{1,0:T(8,128)(2,1)S(1)} collective-permute-done((bf16[240,128]{1,0:T(8,128)(2,1)}, bf16[240,128]{1,0:T(8,128)(2,1)S(1)}, u32[]{:S(2)}, u32[]{:S(2)}) %collective-permute-start.7) | collective-permute-done | bytes 61472 | tf_op jit(solution)/shard_map/ppermute | solution.py:478
  73.5 0.4 collective-permute-done.8.refs_3_
  73.9 0.2 copy-done.6
  74.2 0.4 copy-done.7
  74.5 3.7 %finish.1 = (bf16[2,6144]{1,0:T(2,128)(2,1)}, bf16[2,6144]{1,0:T(2,128)(2,1)}, f32[2,8]{1,0:T(2,128)}) custom-call(bf16[240,128]{1,0:T(8,128)(2,1)} %get-tuple-element.13.refs_0_, bf16[240,128]{1,0:T(8,128)(2,1)} %copy-done.5, bf16[240,128]{1,0:T(8,128)(2,1)} %copy-done.6, bf16[240,128]{1,0:T(8,128)(2,1)} %copy-done.7, f32[1,6144]{1,0:T(1,128)} %get-tuple-element.17.refs_4_, ...), custom_call_target="tpu_custom_call" | custom-call | tf_op jit(solution)/shard_map/finish/pallas_call | solution.py:464
  (16 shorter events, 0.0 us)
Async XLA Ops:
  1.4 9.3 %collective-permute-start.3 = (bf16[2,1,6144]{2,1,0:T(2,128)(2,1)S(1)}, bf16[2,1,6144]{2,1,0:T(2,128)(2,1)S(1)}, u32[]{:S(2)}, u32[]{:S(2)}) collective-permute-start(bf16[2,1,6144]{2,1,0:T(2,128)(2,1)S(1)} %copy.14), channel_id=1, source_target_pairs={{0,1},{1,0},{2,3},{3,2},{4,5},{5,4},{6,7},{7,6},{8,9},{9,8},{10,11... | collective-permute-start | bytes 73736 | tf_op jit(solution)/shard_map/ppermute | solution.py:478
  9.2 8.7 %collective-permute-start.1 = (bf16[400,128]{1,0:T(8,128)(2,1)}, bf16[400,128]{1,0:T(8,128)(2,1)S(1)}, u32[]{:S(2)}, u32[]{:S(2)}) collective-permute-start(bf16[400,128]{1,0:T(8,128)(2,1)} %get-tuple-element.12.refs_0_), channel_id=1, source_target_pairs={{0,16},{8,24},{16,0},{24,8},{1,17},{9,25},{17,1},{25,9},{2,18},{10... | collective-permute-start | bytes 307208 | tf_op jit(solution)/shard_map/ppermute | solution.py:478
  10.7 15.6 %collective-permute-start = (bf16[400,128]{1,0:T(8,128)(2,1)}, bf16[400,128]{1,0:T(8,128)(2,1)S(1)}, u32[]{:S(2)}, u32[]{:S(2)}) collective-permute-start(bf16[400,128]{1,0:T(8,128)(2,1)} %get-tuple-element.12.refs_0_), channel_id=1, source_target_pairs={{0,8},{8,0},{16,24},{24,16},{1,9},{9,1},{17,25},{25,17},{2,10},{10... | collective-permute-start | bytes 307208 | tf_op jit(solution)/shard_map/ppermute | solution.py:478
  10.8 4.2 %collective-permute-start.4 = (bf16[2,2,6144]{2,1,0:T(2,128)(2,1)S(1)}, bf16[2,2,6144]{2,1,0:T(2,128)(2,1)S(1)}, u32[]{:S(2)}, u32[]{:S(2)}) collective-permute-start(bf16[2,2,6144]{2,1,0:T(2,128)(2,1)S(1)} %pad_maximum_fusion.1), channel_id=1, source_target_pairs={{0,2},{1,3},{2,0},{3,1},{4,6},{5,7},{6,4},{7,5},{8,10},{9,11},{10,... | collective-permute-start | bytes 147464 | tf_op jit(solution)/shard_map/ppermute | solution.py:478
  15.2 7.5 %copy-start = (bf16[2,4,6144]{2,1,0:T(4,128)(2,1)}, bf16[2,4,6144]{2,1,0:T(4,128)(2,1)S(1)}, u32[]{:S(2)}) copy-start(bf16[2,4,6144]{2,1,0:T(4,128)(2,1)S(1)} %pad_maximum_fusion.refs_0_) | copy-start | bytes 294916
  15.2 7.5 %collective-permute-start.5 = (bf16[2,4,6144]{2,1,0:T(4,128)(2,1)S(1)}, bf16[2,4,6144]{2,1,0:T(4,128)(2,1)S(1)}, u32[]{:S(2)}, u32[]{:S(2)}) collective-permute-start(bf16[2,4,6144]{2,1,0:T(4,128)(2,1)S(1)} %pad_maximum_fusion.refs_0_), channel_id=1, source_target_pairs={{0,4},{1,5},{2,6},{3,7},{4,0},{5,1},{6,2},{7,3},{8,12},{9,13},{10,... | collective-permute-start | bytes 294920 | tf_op jit(solution)/shard_map/ppermute | solution.py:478
  17.9 8.4 %copy-start.1 = (bf16[400,128]{1,0:T(8,128)(2,1)}, bf16[400,128]{1,0:T(8,128)(2,1)S(1)}, u32[]{:S(2)}) copy-start(bf16[400,128]{1,0:T(8,128)(2,1)S(1)} %collective-permute-done.1.refs_2_) | copy-start | bytes 307204
  17.9 8.4 %collective-permute-start.2 = (bf16[400,128]{1,0:T(8,128)(2,1)S(1)}, bf16[400,128]{1,0:T(8,128)(2,1)S(1)}, u32[]{:S(2)}, u32[]{:S(2)}) collective-permute-start(bf16[400,128]{1,0:T(8,128)(2,1)S(1)} %collective-permute-done.1.refs_2_), channel_id=1, source_target_pairs={{0,8},{8,0},{16,24},{24,16},{1,9},{9,1},{17,25},{25,17},{2,10},{10... | collective-permute-start | bytes 307208 | tf_op jit(solution)/shard_map/ppermute | solution.py:478
  22.7 0.6 copy-start.4
  26.3 0.6 copy-start.2
  27.0 0.6 copy-start.3
  68.4 2.6 %collective-permute-start.6 = (bf16[240,128]{1,0:T(8,128)(2,1)}, bf16[240,128]{1,0:T(8,128)(2,1)S(1)}, u32[]{:S(2)}, u32[]{:S(2)}) collective-permute-start(bf16[240,128]{1,0:T(8,128)(2,1)} %get-tuple-element.14), channel_id=1, source_target_pairs={{0,8},{8,0},{16,24},{24,16},{1,9},{9,1},{17,25},{25,17},{2,10},{10... | collective-permute-start | bytes 184328 | tf_op jit(solution)/shard_map/ppermute | solution.py:478
  68.4 5.1 %collective-permute-start.7 = (bf16[240,128]{1,0:T(8,128)(2,1)}, bf16[240,128]{1,0:T(8,128)(2,1)S(1)}, u32[]{:S(2)}, u32[]{:S(2)}) collective-permute-start(bf16[240,128]{1,0:T(8,128)(2,1)} %get-tuple-element.15), channel_id=1, source_target_pairs={{0,16},{8,24},{16,0},{24,8},{1,17},{9,25},{17,1},{25,9},{2,18},{10... | collective-permute-start | bytes 184328 | tf_op jit(solution)/shard_map/ppermute | solution.py:478
  69.1 4.9 %collective-permute-start.8 = (bf16[240,128]{1,0:T(8,128)(2,1)}, bf16[240,128]{1,0:T(8,128)(2,1)S(1)}, u32[]{:S(2)}, u32[]{:S(2)}) collective-permute-start(bf16[240,128]{1,0:T(8,128)(2,1)} %get-tuple-element.16), channel_id=1, source_target_pairs={{0,24},{8,16},{16,8},{24,0},{1,25},{9,17},{17,9},{25,1},{2,26},{10... | collective-permute-start | bytes 184328 | tf_op jit(solution)/shard_map/ppermute | solution.py:478
  71.0 3.0 %copy-start.5 = (bf16[240,128]{1,0:T(8,128)(2,1)}, bf16[240,128]{1,0:T(8,128)(2,1)S(1)}, u32[]{:S(2)}) copy-start(bf16[240,128]{1,0:T(8,128)(2,1)S(1)} %collective-permute-done.6.refs_1_) | copy-start | bytes 184324
  73.5 0.6 copy-start.6
  73.9 0.6 copy-start.7

commit v3 on v2

--- a/solution.py
+++ b/solution.py
@@ -10,7 +10,11 @@
 from jax.sharding import PartitionSpec as P
 
 LANES = 128
-VMEM_LIMIT = 60 * 1024 * 1024
+MIB = 1024 * 1024
+
+
+def cost(us):
+    return pl.CostEstimate(flops=int(us * 1e9), bytes_accessed=MIB, transcendentals=0)
 
 
 def round_up(value, unit):
@@ -61,7 +65,9 @@
             square(cosine[odd, first], -sine[odd, first], half),
         ]
     )
-    return as_bf16(own), as_bf16(along_z), as_bf16(along_x)
+    pieces = [along_z, along_x, own]
+    pieces = [np.pad(piece, ((0, 0), (0, 0), (0, 2 * LANES - piece.shape[2]))) for piece in pieces]
+    return as_bf16(np.concatenate([piece.reshape(-1, 2 * LANES) for piece in pieces]))
 
 
 def cell_parts(index, length):
@@ -88,7 +94,18 @@
     return lax.dot_general(left, right, (((1,), (1,)), ((), ())), preferred_element_type=jnp.float32)
 
 
-def group_kernel(length, planes, chunks, gvec_ref, psi_ref, pay_ref, slot_ref, hot, counts, spread, pick):
+def fetch_all(pairs, sems):
+    copies = [pltpu.make_async_copy(source, target, sems.at[n]) for n, (source, target) in enumerate(pairs)]
+    for copy in copies:
+        copy.start()
+    return copies
+
+
+def group_kernel(
+    length, planes, chunks, gvec_hbm, psi_hbm, pay_ref, slot_ref, hot, counts, spread, pick, gvec_ref, psi_ref, sems
+):
+    for copy in fetch_all(((gvec_hbm, gvec_ref), (psi_hbm, psi_ref)), sems):
+        copy.wait()
     waves = gvec_ref.shape[1]
     tiles = waves // LANES
     rows = round_up(planes, 16)
@@ -150,36 +167,48 @@
             pltpu.VMEM((tiles * rows, 2 * LANES), jnp.float32),
             pltpu.VMEM((4 * chunks, waves), jnp.bfloat16),
             pltpu.VMEM((LANES, waves), jnp.bfloat16),
+            pltpu.VMEM((1, waves), jnp.int32),
+            pltpu.VMEM((2, waves), jnp.bfloat16),
+            pltpu.SemaphoreType.DMA((2,)),
         ],
-        compiler_params=pltpu.CompilerParams(vmem_limit_bytes=VMEM_LIMIT),
+        in_specs=[pl.BlockSpec(memory_space=pl.ANY)] * 2,
+        compiler_params=pltpu.CompilerParams(vmem_limit_bytes=24 * MIB),
+        cost_estimate=cost(3.4),
         name="group_waves",
     )(index, psi)
 
 
 def lattice_kernel(length, planes, chunks, blocks, *refs):
     pays = refs[:blocks]
-    sums_ref, vloc_hbm, own_ref, along_z, along_x = refs[blocks : blocks + 5]
-    outs = refs[blocks + 5 : 2 * blocks + 5]
-    wide, cells_e, cells_o, phases, vloc, result, maps, maps_s, sems = refs[2 * blocks + 5 :]
+    sums_ref, vloc_hbm, tables = refs[blocks : blocks + 3]
+    outs = refs[blocks + 3 : 2 * blocks + 3]
+    wide, cells_e, cells_o, phases, vloc, result, maps, maps_s, sems, vloc_sem = refs[2 * blocks + 3 :]
     half = length // 2
     rows = round_up(planes, 8)
     both = 2 * rows
     pitch = both + 1
     spare = blocks * planes
     me = lax.axis_index("pw")
+    for s in range(blocks):
+        maps[s * 8 : (s + 1) * 8, :] = pays[s][4 * chunks : 4 * chunks + 16, :].astype(jnp.int32)[:8]
+    (fetch,) = fetch_all(((maps, maps_s),), sems)
 
     def load(k, _):
-        pltpu.make_async_copy(vloc_hbm.at[:, k, :], vloc.at[k], sems.at[0]).start()
+        pltpu.make_async_copy(vloc_hbm.at[:, k, :], vloc.at[k], vloc_sem).start()
         return 0
 
     lax.fori_loop(0, planes, load, 0)
     for s in range(blocks):
-        maps[s * 8 : (s + 1) * 8, :] = pays[s][4 * chunks : 4 * chunks + 16, :].astype(jnp.int32)[:8]
-    fetch = pltpu.make_async_copy(maps, maps_s, sems.at[1])
-    fetch.start()
-    for s in range(blocks):
         wide[s * 4 * chunks : (s + 1) * 4 * chunks, :] = pays[s][0 : 4 * chunks, :].astype(jnp.float32)
-    own = own_ref[me]
+    own_at = 8 * LANES + 4 * length + pl.multiple_of(me * both, 16)
+    own = tables[pl.ds(own_at, both), :][:, :length]
+
+    def along_z(n):
+        return tables[2 * LANES * n : 2 * LANES * (n + 1), :]
+
+    def along_x(n):
+        return tables[8 * LANES + length * n : 8 * LANES + length * (n + 1), :][:, :length]
+
     fetch.wait()
     used = maps_s[1, 0]
     for s in range(1, blocks):
@@ -241,7 +270,7 @@
         return 0
 
     lax.fori_loop(0, turns, forward, 0)
-    pltpu.make_async_copy(vloc, vloc, sems.at[0]).wait()
+    pltpu.make_async_copy(vloc, vloc, vloc_sem).wait()
 
     def strided(start):
         return pl.ds(start, half, stride=pitch)
@@ -265,8 +294,8 @@
                 axis=0,
             )
 
-        even = dot(pull(cells_e), along_z[0])
-        odd = dot(pull(cells_o), along_z[1])
+        even = dot(pull(cells_e), along_z(0))
+        odd = dot(pull(cells_o), along_z(1))
         low, high = (even + odd).astype(jnp.bfloat16), (even - odd).astype(jnp.bfloat16)
 
         def stacked(n):
@@ -278,20 +307,20 @@
 
         sums, differences = [], []
         for j, k in enumerate(many):
-            even = dot(along_x[0], stacked(2 * j))
-            odd = dot(along_x[1], stacked(2 * j + 1))
+            even = dot(along_x(0), stacked(2 * j))
+            odd = dot(along_x(1), stacked(2 * j + 1))
             field = vloc[k]
             field = beside(field[:, :LANES], beside(field[:, half:], field[:, : LANES - half]))
             near, far = field[:half], field[half:]
             first = (even + odd) * above(near, near)
             second = (even - odd) * above(far, far)
-            for table, value in ((along_x[2], first + second), (along_x[3], first - second)):
+            for table, value in ((along_x(2), first + second), (along_x(3), first - second)):
                 back = dot(table, value.astype(jnp.bfloat16))
                 total, change = back[:, :LANES] + back[:, LANES:], back[:, :LANES] - back[:, LANES:]
                 sums.append(beside(total[:half], total[half:]).astype(jnp.bfloat16))
                 differences.append(beside(change[:half], change[half:]).astype(jnp.bfloat16))
-        even = dot(jnp.concatenate(sums, axis=0), along_z[2])
-        odd = dot(jnp.concatenate(differences, axis=0), along_z[3])
+        even = dot(jnp.concatenate(sums, axis=0), along_z(2))
+        odd = dot(jnp.concatenate(differences, axis=0), along_z(3))
         for n, at in enumerate(starts):
             part = slice(n * half, (n + 1) * half)
             cells_e[strided(at), :] = even[part, :LANES]
@@ -338,12 +367,12 @@
 def lattice(pays, sums, vloc, length, planes, chunks):
     blocks = len(pays)
     rows = round_up(planes, 8)
-    own, along_z, along_x = tables_of(length, planes, blocks)
+    tables = tables_of(length, planes, blocks)
     vmem = pl.BlockSpec(memory_space=pltpu.VMEM)
     return pl.pallas_call(
         functools.partial(lattice_kernel, length, planes, chunks, blocks),
         out_shape=[jax.ShapeDtypeStruct((2 * chunks + 3 * sums.shape[0], LANES), jnp.bfloat16)] * blocks,
-        in_specs=[vmem] * (blocks + 1) + [pl.BlockSpec(memory_space=pl.ANY)] + [vmem] * 3,
+        in_specs=[vmem] * (blocks + 1) + [pl.BlockSpec(memory_space=pl.ANY), vmem],
         out_specs=[vmem] * blocks,
         scratch_shapes=[
             pltpu.VMEM((blocks * 4 * chunks, LANES), jnp.float32),
@@ -354,23 +383,27 @@
             pltpu.VMEM((blocks * 2 * chunks, LANES), jnp.float32),
             pltpu.VMEM((blocks * 8, LANES), jnp.int32),
             pltpu.SMEM((blocks * 8, LANES), jnp.int32),
-            pltpu.SemaphoreType.DMA((2,)),
+            pltpu.SemaphoreType.DMA((1,)),
+            pltpu.SemaphoreType.DMA,
         ],
-        compiler_params=pltpu.CompilerParams(vmem_limit_bytes=VMEM_LIMIT),
+        compiler_params=pltpu.CompilerParams(vmem_limit_bytes=48 * MIB),
+        cost_estimate=cost(36.0),
         name="lattice",
-    )(*pays, sums, vloc, own, along_z, along_x)
+    )(*pays, sums, vloc, tables)
 
 
 def project_kernel(bands, *refs):
-    every = [ref[...].astype(jnp.float32) for ref in refs[:-2]]
-    beta_ref, out_ref = refs[-2:]
-    count = beta_ref.shape[0] // 2
+    beta_hbm, out_ref, beta_ref, sems = refs[-4:]
+    (fetch,) = fetch_all(((beta_hbm, beta_ref),), sems)
+    every = [ref[...].astype(jnp.float32) for ref in refs[:-4]]
+    count = beta_ref.shape[1]
     rows = out_ref.shape[0] // 2
     pad = [jnp.zeros((rows - bands, every[0].shape[2]), jnp.float32)] if rows > bands else []
     re = jnp.concatenate([value[0] for value in every] + pad, axis=0)
     im = jnp.concatenate([value[1] for value in every] + pad, axis=0)
-    found = dot_lanes(beta_ref[...], jnp.concatenate([re, im], axis=0).astype(jnp.bfloat16))
-    on_re, on_im = found[:count], found[count:]
+    fetch.wait()
+    stack = jnp.concatenate([re, im], axis=0).astype(jnp.bfloat16)
+    on_re, on_im = dot_lanes(beta_ref[0], stack), dot_lanes(beta_ref[1], stack)
     found = jnp.concatenate([on_re[:, :rows] + on_im[:, rows:], on_re[:, rows:] - on_im[:, :rows]], axis=1)
     out_ref[...] = jnp.zeros_like(out_ref)
     out_ref[:, :count] = found.T
@@ -389,9 +422,12 @@
     return pl.pallas_call(
         functools.partial(project_kernel, bands),
         out_shape=jax.ShapeDtypeStruct((2 * round_up(bands, 8), LANES), jnp.float32),
-        compiler_params=pltpu.CompilerParams(vmem_limit_bytes=VMEM_LIMIT),
+        in_specs=[pl.BlockSpec(memory_space=pltpu.VMEM)] * len(every) + [pl.BlockSpec(memory_space=pl.ANY)],
+        scratch_shapes=[pltpu.VMEM(beta.shape, beta.dtype), pltpu.SemaphoreType.DMA((1,))],
+        compiler_params=pltpu.CompilerParams(vmem_limit_bytes=16 * MIB),
+        cost_estimate=cost(1.2),
         name="project",
-    )(*every, beta.reshape(2 * beta.shape[1], beta.shape[2]))
+    )(*every, beta)
 
 
 def finish_kernel(length, planes, chunks, blocks, bands, *refs):
@@ -468,7 +504,8 @@
             jax.ShapeDtypeStruct(psi.shape, jnp.bfloat16),
             jax.ShapeDtypeStruct((2, bands), jnp.float32),
         ),
-        compiler_params=pltpu.CompilerParams(vmem_limit_bytes=VMEM_LIMIT),
+        compiler_params=pltpu.CompilerParams(vmem_limit_bytes=16 * MIB),
+        cost_estimate=cost(2.1),
         name="finish",
     )(*parts, slot, index, psi, beta, atoms)
 
@@ -492,13 +529,16 @@
     return [found[s] for s in range(size)]
 
 
-def from_bands(value, axis):
+def from_bands(value, axis, after):
     size = lax.axis_size(axis)
     if not doubles(size):
         pairs = [[(k, (k + s) % size) for k in range(size)] for s in range(1, size)]
-        return [value] + [lax.ppermute(value, axis, pair) for pair in pairs]
-    held = [value]
-    step = 1
+        held = [value] + [lax.ppermute(value, axis, pair) for pair in pairs]
+        return [part[:, None] for part in held]
+    other = swap(value, axis, 1) if size > 1 else value
+    other, _ = lax.optimization_barrier((other, after))
+    held = [value[:, None], other[:, None]][:size]
+    step = 2
     while step < size:
         value = jnp.concatenate(held, axis=1)
         held = [value, swap(value, axis, step)]
@@ -522,11 +562,12 @@
     chunks = round_up(width // LANES + planes, 16)
     index = gvec_index.reshape(1, width)
     mine = psi.reshape(2, width)
-    atoms = jnp.concatenate([atom_blocks(dmat), atom_blocks(qmat)], axis=1)
     pay, slot = group_waves(index, mine, length, planes, chunks)
     pays = from_blocks(pay, "pw")
-    sums = project(from_bands(psi, "band"), beta, bands)
+    sums = project(from_bands(mine, "band", pay), beta, bands)
     outs = lattice(pays, sums, vloc, length, planes, chunks)
+    dmat, qmat, _ = lax.optimization_barrier((dmat, qmat, outs[0]))
+    atoms = jnp.concatenate([atom_blocks(dmat), atom_blocks(qmat)], axis=1)
     parts = [outs[0]] + [swap(outs[s], "pw", s) for s in range(1, blocks)]
     hpsi, spsi, gram = finish(parts, slot, index, mine, beta, atoms, length, planes, chunks, bands)
     return (hpsi.reshape(2, 1, width), spsi.reshape(2, 1, width), gram.reshape(2, 1, bands))

time: 77.8 us -> 67.1 us (0.86); the launches traced: 78.3 us -> 65.9 us
  Pallas kernels: 52.2 us -> 43 us
  local copies, waits for them, and re-layouts: 5.28 us -> 2.12 us
    pallas_call x1, Pallas kernels: 40.8 us -> 36.3 us  [lattice(): pl.pallas_call(functools.partial(lattice_kernel, length, planes, chunks,...]
    unnamed x17 -> x16, local copies, waits for them, and re-layouts: 3.29 us -> 1.54 us
    pallas_call x1, Pallas kernels: 2.94 us -> 1.21 us  [project(): pl.pallas_call(functools.partial(project_kernel, bands), out_shape=jax.Sh...]
    pallas_call x1, Pallas kernels: 3.71 us -> 2.12 us  [finish(): pl.pallas_call(functools.partial(finish_kernel, length, planes, chunks, b...]
    transpose x2, local copies, waits for them, and re-layouts: 1.75 us -> 0.23 us  [atom_blocks(): jnp.transpose(matrix, (0, 2, 1))[:, :, None, :]]
    pallas_call x1, Pallas kernels: 4.78 us -> 3.43 us  [group_waves(): pl.pallas_call(functools.partial(group_kernel, length, planes, chunks), o...]
  transfers between devices with their start and end apart: 9 -> 9, of which waited for: 4 -> 4; matrix products, arithmetic and copies ran while one was open for 4% -> 0% of each run, Pallas kernels for 10% -> 7%
where the time goes in v3:
time: 67.1 us; the launch traced here: 65.9 us
  Pallas kernels  43 us (64%)
  starting transfers between devices  10.8 us (16%)
  waiting for transfers between devices  8.78 us (13%)
  local copies, waits for them, and re-layouts  2.12 us (3%)
  between operations  0.83 us (1%)
    pallas_call x1, Pallas kernels, lattice(): pl.pallas_call(functools.partial(lattice_kernel, length, planes, chunks,...  36.3 us
    ppermute x9, starting transfers between devices, swap(): return lax.ppermute(value, axis, [(k, k ^ step) for k in range(size)])  10.8 us
    ppermute x9, waiting for transfers between devices, swap(): return lax.ppermute(value, axis, [(k, k ^ step) for k in range(size)])  8.78 us
    pallas_call x1, Pallas kernels, group_waves(): pl.pallas_call(functools.partial(group_kernel, length, planes, chunks), o...  3.43 us
    pallas_call x1, Pallas kernels, finish(): pl.pallas_call(functools.partial(finish_kernel, length, planes, chunks, b...  2.12 us
    unnamed x16, local copies, waits for them, and re-layouts  1.54 us
  transfers between devices with their start and end apart: 9, of which 4 were waited for; matrix products, arithmetic and copies ran while one was open for 0% of the time, Pallas kernels for 7%

profile of v3, /device:TPU:0, one launch (start us, length us, event | category | flops | bytes accessed | tf_op | source)
XLA Modules:
  0.0 65.9 jit_solution(4870030889710692775)
XLA Ops:
  0.6 3.0 %collective-permute-start.3 = (bf16[2,6144]{1,0:T(2,128)(2,1)}, bf16[2,6144]{1,0:T(2,128)(2,1)S(1)}, u32[]{:S(2)}, u32[]{:S(2)}) collective-permute-start(bf16[2,6144]{1,0:T(2,128)(2,1)} %bitcast.10), channel_id=1, source_target_pairs={{0,1},{1,0},{2,3},{3,2},{4,5},{5,4},{6,7},{7,6},{8,9},{9,8},{10,11... | collective-permute-start | bytes 73736 | tf_op jit(solution)/shard_map/ppermute | solution.py:515
  3.6 0.8 %copy-done = bf16[2,1,6144]{2,0,1:T(2,128)(2,1)S(1)} copy-done((bf16[2,1,6144]{2,0,1:T(2,128)(2,1)S(1)}, bf16[2,1,6144]{2,0,1:T(2,128)(2,1)}, u32[]{:S(2)}) %copy-start) | copy-done | bytes 24600
  4.4 0.7 %copy-done.3 = s32[6144]{0:T(1024)S(1)} copy-done((s32[6144]{0:T(1024)S(1)}, s32[6144]{0:T(1024)}, u32[]{:S(2)}) %copy-start.3) | copy-done | bytes 24600
  5.1 3.4 %group_waves.1 = (bf16[400,128]{1,0:T(8,128)(2,1)S(1)}, f32[1,6144]{1,0:T(1,128)S(1)}) custom-call(s32[1,6144]{1,0:T(1,128)S(1)} %bitcast.13, bf16[2,6144]{1,0:T(2,128)(2,1)S(1)} %bitcast.11), custom_call_target="tpu_custom_call" | custom-call | flops 3400000000 | bytes 1048576 | tf_op jit(solution)/shard_map/group_waves/pallas_call | solution.py:159
  8.6 0.1 pad_maximum_fusion.1
  8.7 1.6 %collective-permute-start.4 = (bf16[2,2,6144]{2,0,1:T(2,128)(2,1)S(1)}, bf16[2,2,6144]{2,0,1:T(2,128)(2,1)S(1)}, u32[]{:S(2)}, u32[]{:S(2)}) collective-permute-start(bf16[2,2,6144]{2,0,1:T(2,128)(2,1)S(1)} %pad_maximum_fusion.1), channel_id=1, source_target_pairs={{0,2},{1,3},{2,0},{3,1},{4,6},{5,7},{6,4},{7,5},{8,10},{9,11},{10,... | collective-permute-start | bytes 147464 | tf_op jit(solution)/shard_map/ppermute | solution.py:515
  10.3 1.5 %collective-permute-start.1 = (bf16[400,128]{1,0:T(8,128)(2,1)S(1)}, bf16[400,128]{1,0:T(8,128)(2,1)S(1)}, u32[]{:S(2)}, u32[]{:S(2)}) collective-permute-start(bf16[400,128]{1,0:T(8,128)(2,1)S(1)} %get-tuple-element.15.refs_0_), channel_id=1, source_target_pairs={{0,16},{8,24},{16,0},{24,8},{1,17},{9,25},{17,1},{25,9},{2,18},{10... | collective-permute-start | bytes 307208 | tf_op jit(solution)/shard_map/ppermute | solution.py:515
  11.8 1.0 %collective-permute-done.4 = bf16[2,2,6144]{2,0,1:T(2,128)(2,1)S(1)} collective-permute-done((bf16[2,2,6144]{2,0,1:T(2,128)(2,1)S(1)}, bf16[2,2,6144]{2,0,1:T(2,128)(2,1)S(1)}, u32[]{:S(2)}, u32[]{:S(2)}) %collective-permute-start.4) | collective-permute-done | bytes 49184 | tf_op jit(solution)/shard_map/ppermute | solution.py:515
  12.8 0.1 pad_maximum_fusion
  13.0 2.7 %collective-permute-start.5 = (bf16[2,4,6144]{2,0,1:T(2,128)(2,1)S(1)}, bf16[2,4,6144]{2,0,1:T(2,128)(2,1)S(1)}, u32[]{:S(2)}, u32[]{:S(2)}) collective-permute-start(bf16[2,4,6144]{2,0,1:T(2,128)(2,1)S(1)} %pad_maximum_fusion), channel_id=1, source_target_pairs={{0,4},{1,5},{2,6},{3,7},{4,0},{5,1},{6,2},{7,3},{8,12},{9,13},{10,... | collective-permute-start | bytes 294920 | tf_op jit(solution)/shard_map/ppermute | solution.py:515
  15.6 0.1 copy.10.refs_0_
  15.7 0.1 collective-permute-start.2
  15.8 4.4 %collective-permute-done.5 = bf16[2,4,6144]{2,0,1:T(2,128)(2,1)S(1)} collective-permute-done((bf16[2,4,6144]{2,0,1:T(2,128)(2,1)S(1)}, bf16[2,4,6144]{2,0,1:T(2,128)(2,1)S(1)}, u32[]{:S(2)}, u32[]{:S(2)}) %collective-permute-start.5) | collective-permute-done | bytes 98336 | tf_op jit(solution)/shard_map/ppermute | solution.py:515
  20.2 0.1 copy.11.refs_1_
  20.2 0.0 copy-start.5
  20.2 1.2 %project.1.refs_4_ = f32[16,128]{1,0:T(8,128)S(1)} custom-call(bf16[2,4,6144]{2,1,0:T(4,128)(2,1)S(1)} %copy.10.refs_0_, bf16[2,4,6144]{2,1,0:T(4,128)(2,1)S(1)} %copy.11.refs_1_, bf16[2,72,6144]{2,1,0:T(8,128)(2,1)S(1)} %copy-done.2), custom_call_target="tpu_custom_call" | custom-call | flops 1200000000 | bytes 1048576 | tf_op jit(solution)/shard_map/project/pallas_call | solution.py:422
  21.5 0.0 copy-start.6
  21.5 0.0 copy-start.7
  21.5 0.0 copy-start.1
  21.5 0.0 copy-start.4
  21.5 36.3 %lattice.1 = (bf16[240,128]{1,0:T(8,128)(2,1)S(1)}, bf16[240,128]{1,0:T(8,128)(2,1)S(1)}, bf16[240,128]{1,0:T(8,128)(2,1)S(1)}, bf16[240,128]{1,0:T(8,128)(2,1)S(1)}) custom-call(bf16[400,128]{1,0:T(8,128)(2,1)S(1)} %get-tuple-element.15.refs_0_, bf16[400,128]{1,0:T(8,128)(2,1)S(1)} %collective-permute-done.refs_1_, ...), custom_call_target="tpu_custom_call" | custom-call | flops 35999997952 | bytes 1048576 | tf_op jit(solution)/shard_map/lattice/pallas_call | solution.py:372
  57.8 0.1 copy.12
  57.9 0.1 copy.13
  58.0 0.1 broadcast_multiply_fusion.1
  58.2 0.1 mul.37
  58.3 0.1 mul.40
  58.4 0.1 collective-permute-start.6
  58.5 0.1 collective-permute-start.7
  58.6 1.8 %collective-permute-start.8 = (bf16[240,128]{1,0:T(8,128)(2,1)S(1)}, bf16[240,128]{1,0:T(8,128)(2,1)S(1)}, u32[]{:S(2)}, u32[]{:S(2)}) collective-permute-start(bf16[240,128]{1,0:T(8,128)(2,1)S(1)} %get-tuple-element.20), channel_id=1, source_target_pairs={{0,24},{8,16},{16,8},{24,0},{1,25},{9,17},{17,9},{25,1},{2,26},{10... | collective-permute-start | bytes 184328 | tf_op jit(solution)/shard_map/ppermute | solution.py:515
  60.4 3.0 %collective-permute-done.7.refs_2_ = bf16[240,128]{1,0:T(8,128)(2,1)S(1)} collective-permute-done((bf16[240,128]{1,0:T(8,128)(2,1)S(1)}, bf16[240,128]{1,0:T(8,128)(2,1)S(1)}, u32[]{:S(2)}, u32[]{:S(2)}) %collective-permute-start.7) | collective-permute-done | bytes 61472 | tf_op jit(solution)/shard_map/ppermute | solution.py:515
  63.4 0.4 collective-permute-done.8.refs_3_
  63.8 2.1 %finish.1 = (bf16[2,6144]{1,0:T(2,128)(2,1)}, bf16[2,6144]{1,0:T(2,128)(2,1)}, f32[2,8]{1,0:T(2,128)}) custom-call(bf16[240,128]{1,0:T(8,128)(2,1)S(1)} %get-tuple-element.17.refs_0_, bf16[240,128]{1,0:T(8,128)(2,1)S(1)} %collective-permute-done.6.refs_1_, bf16[240,128]{1,0:T(8,128)(2,1)S(1)} %collective-permute-done.7.refs_2_, ...), custom_call_target="tpu_custom_call" | custom-call | flops 2100000000 | bytes 1048576 | tf_op jit(solution)/shard_map/finish/pallas_call | solution.py:500
  (17 shorter events, 0.0 us)
Async XLA Ops:
  0.6 8.0 %collective-permute-start.3 = (bf16[2,6144]{1,0:T(2,128)(2,1)}, bf16[2,6144]{1,0:T(2,128)(2,1)S(1)}, u32[]{:S(2)}, u32[]{:S(2)}) collective-permute-start(bf16[2,6144]{1,0:T(2,128)(2,1)} %bitcast.10), channel_id=1, source_target_pairs={{0,1},{1,0},{2,3},{3,2},{4,5},{5,4},{6,7},{7,6},{8,9},{9,8},{10,11... | collective-permute-start | bytes 73736 | tf_op jit(solution)/shard_map/ppermute | solution.py:515
  3.6 0.8 %copy-start = (bf16[2,1,6144]{2,0,1:T(2,128)(2,1)S(1)}, bf16[2,1,6144]{2,0,1:T(2,128)(2,1)}, u32[]{:S(2)}) copy-start(bf16[2,1,6144]{2,0,1:T(2,128)(2,1)} %param.7) | copy-start | bytes 73732
  4.4 0.7 %copy-start.3 = (s32[6144]{0:T(1024)S(1)}, s32[6144]{0:T(1024)}, u32[]{:S(2)}) copy-start(s32[6144]{0:T(1024)} %param.8) | copy-start | bytes 73732
  5.1 15.1 %copy-start.2 = (bf16[2,72,6144]{2,1,0:T(8,128)(2,1)S(1)}, bf16[2,72,6144]{2,1,0:T(8,128)(2,1)}, u32[]{:S(2)}) copy-start(bf16[2,72,6144]{2,1,0:T(8,128)(2,1)} %refs_7_.1) | copy-start | bytes 5308420
  8.7 4.2 %collective-permute-start.4 = (bf16[2,2,6144]{2,0,1:T(2,128)(2,1)S(1)}, bf16[2,2,6144]{2,0,1:T(2,128)(2,1)S(1)}, u32[]{:S(2)}, u32[]{:S(2)}) collective-permute-start(bf16[2,2,6144]{2,0,1:T(2,128)(2,1)S(1)} %pad_maximum_fusion.1), channel_id=1, source_target_pairs={{0,2},{1,3},{2,0},{3,1},{4,6},{5,7},{6,4},{7,5},{8,10},{9,11},{10,... | collective-permute-start | bytes 147464 | tf_op jit(solution)/shard_map/ppermute | solution.py:515
  10.3 5.4 %collective-permute-start.1 = (bf16[400,128]{1,0:T(8,128)(2,1)S(1)}, bf16[400,128]{1,0:T(8,128)(2,1)S(1)}, u32[]{:S(2)}, u32[]{:S(2)}) collective-permute-start(bf16[400,128]{1,0:T(8,128)(2,1)S(1)} %get-tuple-element.15.refs_0_), channel_id=1, source_target_pairs={{0,16},{8,24},{16,0},{24,8},{1,17},{9,25},{17,1},{25,9},{2,18},{10... | collective-permute-start | bytes 307208 | tf_op jit(solution)/shard_map/ppermute | solution.py:515
  11.8 9.7 %collective-permute-start = (bf16[400,128]{1,0:T(8,128)(2,1)S(1)}, bf16[400,128]{1,0:T(8,128)(2,1)S(1)}, u32[]{:S(2)}, u32[]{:S(2)}) collective-permute-start(bf16[400,128]{1,0:T(8,128)(2,1)S(1)} %get-tuple-element.15.refs_0_), channel_id=1, source_target_pairs={{0,8},{8,0},{16,24},{24,16},{1,9},{9,1},{17,25},{25,17},{2,10},{10... | collective-permute-start | bytes 307208 | tf_op jit(solution)/shard_map/ppermute | solution.py:515
  13.0 7.2 %collective-permute-start.5 = (bf16[2,4,6144]{2,0,1:T(2,128)(2,1)S(1)}, bf16[2,4,6144]{2,0,1:T(2,128)(2,1)S(1)}, u32[]{:S(2)}, u32[]{:S(2)}) collective-permute-start(bf16[2,4,6144]{2,0,1:T(2,128)(2,1)S(1)} %pad_maximum_fusion), channel_id=1, source_target_pairs={{0,4},{1,5},{2,6},{3,7},{4,0},{5,1},{6,2},{7,3},{8,12},{9,13},{10,... | collective-permute-start | bytes 294920 | tf_op jit(solution)/shard_map/ppermute | solution.py:515
  15.7 5.8 %collective-permute-start.2 = (bf16[400,128]{1,0:T(8,128)(2,1)S(1)}, bf16[400,128]{1,0:T(8,128)(2,1)S(1)}, u32[]{:S(2)}, u32[]{:S(2)}) collective-permute-start(bf16[400,128]{1,0:T(8,128)(2,1)S(1)} %collective-permute-done.1.refs_2_), channel_id=1, source_target_pairs={{0,8},{8,0},{16,24},{24,16},{1,9},{9,1},{17,25},{25,17},{2,10},{10... | collective-permute-start | bytes 307208 | tf_op jit(solution)/shard_map/ppermute | solution.py:515
  20.2 1.3 %copy-start.5 = (bf16[2176,256]{1,0:T(8,128)(2,1)S(1)}, bf16[2176,256]{1,0:T(8,128)(2,1)}, u32[]{:S(2)}) copy-start(bf16[2176,256]{1,0:T(8,128)(2,1)} %constant.5.clone.refs_6_) | copy-start | bytes 3342340
  21.5 36.4 %copy-start.6 = (f32[4,18,18]{2,0,1:T(4,128)S(1)}, f32[4,18,18]{2,0,1:T(4,128)}, u32[]{:S(2)}) copy-start(f32[4,18,18]{2,0,1:T(4,128)} %param.11) | copy-start | bytes 15556
  21.5 36.5 %copy-start.7 = (f32[4,18,18]{2,0,1:T(4,128)S(1)}, f32[4,18,18]{2,0,1:T(4,128)}, u32[]{:S(2)}) copy-start(f32[4,18,18]{2,0,1:T(4,128)} %param.12) | copy-start | bytes 15556
  21.5 42.3 %copy-start.1 = (bf16[2,1,6144]{2,0,1:T(2,128)(2,1)S(1)}, bf16[2,1,6144]{2,0,1:T(2,128)(2,1)}, u32[]{:S(2)}) copy-start(bf16[2,1,6144]{2,0,1:T(2,128)(2,1)} %param.7) | copy-start | bytes 73732
  21.5 42.3 %copy-start.4 = (s32[6144]{0:T(1024)S(1)}, s32[6144]{0:T(1024)}, u32[]{:S(2)}) copy-start(s32[6144]{0:T(1024)} %param.8) | copy-start | bytes 73732
  58.4 2.0 %collective-permute-start.6 = (bf16[240,128]{1,0:T(8,128)(2,1)S(1)}, bf16[240,128]{1,0:T(8,128)(2,1)S(1)}, u32[]{:S(2)}, u32[]{:S(2)}) collective-permute-start(bf16[240,128]{1,0:T(8,128)(2,1)S(1)} %get-tuple-element.18), channel_id=1, source_target_pairs={{0,8},{8,0},{16,24},{24,16},{1,9},{9,1},{17,25},{25,17},{2,10},{10... | collective-permute-start | bytes 184328 | tf_op jit(solution)/shard_map/ppermute | solution.py:515
  58.5 4.9 %collective-permute-start.7 = (bf16[240,128]{1,0:T(8,128)(2,1)S(1)}, bf16[240,128]{1,0:T(8,128)(2,1)S(1)}, u32[]{:S(2)}, u32[]{:S(2)}) collective-permute-start(bf16[240,128]{1,0:T(8,128)(2,1)S(1)} %get-tuple-element.19), channel_id=1, source_target_pairs={{0,16},{8,24},{16,0},{24,8},{1,17},{9,25},{17,1},{25,9},{2,18},{10... | collective-permute-start | bytes 184328 | tf_op jit(solution)/shard_map/ppermute | solution.py:515
  58.6 5.2 %collective-permute-start.8 = (bf16[240,128]{1,0:T(8,128)(2,1)S(1)}, bf16[240,128]{1,0:T(8,128)(2,1)S(1)}, u32[]{:S(2)}, u32[]{:S(2)}) collective-permute-start(bf16[240,128]{1,0:T(8,128)(2,1)S(1)} %get-tuple-element.20), channel_id=1, source_target_pairs={{0,24},{8,16},{16,8},{24,0},{1,25},{9,17},{17,9},{25,1},{2,26},{10... | collective-permute-start | bytes 184328 | tf_op jit(solution)/shard_map/ppermute | solution.py:515

commit v4 on v3

--- a/solution.py
+++ b/solution.py
@@ -217,7 +217,7 @@
     level_y = level[:length]
     group = 4 if blocks % 4 == 0 else 1
     ahead = 8 if blocks == group else 1
-    batch = 8 if planes % 8 == 0 else 1
+    batch = 16 if planes % 16 == 0 else 1
     turns = (used + ahead - 1) // ahead
 
     def place(s, c):
@@ -458,7 +458,9 @@
     gram_im = own_re * each_im - own_im * each_re + jnp.where(over, sums[half_size:], 0.0)
     slot_at = lax.broadcasted_iota(jnp.int32, (half_size, bands), 0)
     if doubles(bands):
-        turn = lax.axis_index("band") ^ slot_at
+        turn = lax.axis_index("band")
+        for place, step in enumerate(doubling_steps(bands)):
+            turn = turn ^ (((slot_at >> place) & 1) * step)
     else:
         turn = lax.axis_index("band") - slot_at
         turn = jnp.where(turn < 0, turn + bands, turn)
@@ -519,6 +521,11 @@
     return size & (size - 1) == 0
 
 
+def doubling_steps(size):
+    steps = [1 << place for place in range(size.bit_length() - 1)]
+    return steps[:1] + steps[:0:-1]
+
+
 def from_blocks(value, axis):
     size = lax.axis_size(axis)
     found = {0: value}
@@ -535,14 +542,15 @@
         pairs = [[(k, (k + s) % size) for k in range(size)] for s in range(1, size)]
         held = [value] + [lax.ppermute(value, axis, pair) for pair in pairs]
         return [part[:, None] for part in held]
-    other = swap(value, axis, 1) if size > 1 else value
-    other, _ = lax.optimization_barrier((other, after))
-    held = [value[:, None], other[:, None]][:size]
-    step = 2
-    while step < size:
-        value = jnp.concatenate(held, axis=1)
-        held = [value, swap(value, axis, step)]
-        step *= 2
+    held = [value[:, None]]
+    for step in doubling_steps(size):
+        if len(held) == 1:
+            other = swap(value, axis, step)
+            other, _ = lax.optimization_barrier((other, after))
+            held.append(other[:, None])
+        else:
+            joined = jnp.concatenate(held, axis=1)
+            held = [joined, swap(joined, axis, step)]
     return held
 
 

time: 67.1 us -> 65.3 us (0.973); the launches traced: 65.9 us -> 66 us
  Pallas kernels: 43 us -> 44.3 us
  waiting for transfers between devices: 8.78 us -> 7.77 us
    pallas_call x1, Pallas kernels: 36.3 us -> 37.6 us  [lattice(): pl.pallas_call(functools.partial(lattice_kernel, length, planes, chunks,...]
    ppermute x9, waiting for transfers between devices: 8.78 us -> 7.77 us  [swap(): return lax.ppermute(value, axis, [(k, k ^ step) for k in range(size)])]
  transfers between devices with their start and end apart: 9 -> 9, of which waited for: 4 -> 5; matrix products, arithmetic and copies ran while one was open for 0% -> 0% of each run, Pallas kernels for 7% -> 7%
where the time goes in v4:
time: 65.3 us; the launch traced here: 66 us
  Pallas kernels  44.3 us (68%)
  starting transfers between devices  10.6 us (16%)
  waiting for transfers between devices  7.77 us (12%)
  local copies, waits for them, and re-layouts  2.12 us (3%)
  between operations  0.81 us (1%)
    pallas_call x1, Pallas kernels, lattice(): pl.pallas_call(functools.partial(lattice_kernel, length, planes, chunks,...  37.6 us
    ppermute x9, starting transfers between devices, swap(): return lax.ppermute(value, axis, [(k, k ^ step) for k in range(size)])  10.6 us
    ppermute x9, waiting for transfers between devices, swap(): return lax.ppermute(value, axis, [(k, k ^ step) for k in range(size)])  7.77 us
    pallas_call x1, Pallas kernels, group_waves(): pl.pallas_call(functools.partial(group_kernel, length, planes, chunks), o...  3.43 us
    pallas_call x1, Pallas kernels, finish(): pl.pallas_call(functools.partial(finish_kernel, length, planes, chunks, b...  2.12 us
    unnamed x16, local copies, waits for them, and re-layouts  1.54 us
  transfers between devices with their start and end apart: 9, of which 5 were waited for; matrix products, arithmetic and copies ran while one was open for 0% of the time, Pallas kernels for 7%

profile of v4, /device:TPU:0, one launch (start us, length us, event | category | flops | bytes accessed | tf_op | source)
XLA Modules:
  0.0 66.0 jit_solution(6335799187468456649)
XLA Ops:
  0.6 3.0 %collective-permute-start.3 = (bf16[2,6144]{1,0:T(2,128)(2,1)}, bf16[2,6144]{1,0:T(2,128)(2,1)S(1)}, u32[]{:S(2)}, u32[]{:S(2)}) collective-permute-start(bf16[2,6144]{1,0:T(2,128)(2,1)} %bitcast.10), channel_id=1, source_target_pairs={{0,1},{1,0},{2,3},{3,2},{4,5},{5,4},{6,7},{7,6},{8,9},{9,8},{10,11... | collective-permute-start | bytes 73736 | tf_op jit(solution)/shard_map/ppermute | solution.py:517
  3.6 0.8 %copy-done = bf16[2,1,6144]{2,0,1:T(2,128)(2,1)S(1)} copy-done((bf16[2,1,6144]{2,0,1:T(2,128)(2,1)S(1)}, bf16[2,1,6144]{2,0,1:T(2,128)(2,1)}, u32[]{:S(2)}) %copy-start) | copy-done | bytes 24600
  4.4 0.7 %copy-done.3 = s32[6144]{0:T(1024)S(1)} copy-done((s32[6144]{0:T(1024)S(1)}, s32[6144]{0:T(1024)}, u32[]{:S(2)}) %copy-start.3) | copy-done | bytes 24600
  5.1 3.4 %group_waves.1 = (bf16[400,128]{1,0:T(8,128)(2,1)S(1)}, f32[1,6144]{1,0:T(1,128)S(1)}) custom-call(s32[1,6144]{1,0:T(1,128)S(1)} %bitcast.13, bf16[2,6144]{1,0:T(2,128)(2,1)S(1)} %bitcast.11), custom_call_target="tpu_custom_call" | custom-call | flops 3400000000 | bytes 1048576 | tf_op jit(solution)/shard_map/group_waves/pallas_call | solution.py:159
  8.6 0.1 pad_maximum_fusion.1
  8.7 2.7 %collective-permute-start.4 = (bf16[2,2,6144]{2,0,1:T(2,128)(2,1)S(1)}, bf16[2,2,6144]{2,0,1:T(2,128)(2,1)S(1)}, u32[]{:S(2)}, u32[]{:S(2)}) collective-permute-start(bf16[2,2,6144]{2,0,1:T(2,128)(2,1)S(1)} %pad_maximum_fusion.1), channel_id=1, source_target_pairs={{0,4},{1,5},{2,6},{3,7},{4,0},{5,1},{6,2},{7,3},{8,12},{9,13},{10,... | collective-permute-start | bytes 147464 | tf_op jit(solution)/shard_map/ppermute | solution.py:517
  11.3 1.5 %collective-permute-start.1 = (bf16[400,128]{1,0:T(8,128)(2,1)S(1)}, bf16[400,128]{1,0:T(8,128)(2,1)S(1)}, u32[]{:S(2)}, u32[]{:S(2)}) collective-permute-start(bf16[400,128]{1,0:T(8,128)(2,1)S(1)} %get-tuple-element.15.refs_0_), channel_id=1, source_target_pairs={{0,16},{8,24},{16,0},{24,8},{1,17},{9,25},{17,1},{25,9},{2,18},{10... | collective-permute-start | bytes 307208 | tf_op jit(solution)/shard_map/ppermute | solution.py:517
  12.8 1.0 %collective-permute-done.4 = bf16[2,2,6144]{2,0,1:T(2,128)(2,1)S(1)} collective-permute-done((bf16[2,2,6144]{2,0,1:T(2,128)(2,1)S(1)}, bf16[2,2,6144]{2,0,1:T(2,128)(2,1)S(1)}, u32[]{:S(2)}, u32[]{:S(2)}) %collective-permute-start.4) | collective-permute-done | bytes 49184 | tf_op jit(solution)/shard_map/ppermute | solution.py:517
  13.8 0.1 pad_maximum_fusion
  14.0 1.5 %collective-permute-start.5 = (bf16[2,4,6144]{2,0,1:T(2,128)(2,1)S(1)}, bf16[2,4,6144]{2,0,1:T(2,128)(2,1)S(1)}, u32[]{:S(2)}, u32[]{:S(2)}) collective-permute-start(bf16[2,4,6144]{2,0,1:T(2,128)(2,1)S(1)} %pad_maximum_fusion), channel_id=1, source_target_pairs={{0,2},{1,3},{2,0},{3,1},{4,6},{5,7},{6,4},{7,5},{8,10},{9,11},{10,... | collective-permute-start | bytes 294920 | tf_op jit(solution)/shard_map/ppermute | solution.py:517
  15.5 0.1 copy.10.refs_0_
  15.6 0.4 collective-permute-done.1.refs_2_
  16.0 2.7 %collective-permute-done.5 = bf16[2,4,6144]{2,0,1:T(2,128)(2,1)S(1)} collective-permute-done((bf16[2,4,6144]{2,0,1:T(2,128)(2,1)S(1)}, bf16[2,4,6144]{2,0,1:T(2,128)(2,1)S(1)}, u32[]{:S(2)}, u32[]{:S(2)}) %collective-permute-start.5) | collective-permute-done | bytes 98336 | tf_op jit(solution)/shard_map/ppermute | solution.py:517
  18.7 0.1 copy.11.refs_1_
  18.7 0.0 copy-start.5
  18.8 1.2 %project.1.refs_4_ = f32[16,128]{1,0:T(8,128)S(1)} custom-call(bf16[2,4,6144]{2,1,0:T(4,128)(2,1)S(1)} %copy.10.refs_0_, bf16[2,4,6144]{2,1,0:T(4,128)(2,1)S(1)} %copy.11.refs_1_, bf16[2,72,6144]{2,1,0:T(8,128)(2,1)S(1)} %copy-done.2), custom_call_target="tpu_custom_call" | custom-call | flops 1200000000 | bytes 1048576 | tf_op jit(solution)/shard_map/project/pallas_call | solution.py:422
  20.0 0.0 copy-start.6
  20.0 0.0 copy-start.7
  20.0 0.0 copy-start.1
  20.0 0.0 copy-start.4
  20.0 37.6 %lattice.1 = (bf16[240,128]{1,0:T(8,128)(2,1)S(1)}, bf16[240,128]{1,0:T(8,128)(2,1)S(1)}, bf16[240,128]{1,0:T(8,128)(2,1)S(1)}, bf16[240,128]{1,0:T(8,128)(2,1)S(1)}) custom-call(bf16[400,128]{1,0:T(8,128)(2,1)S(1)} %get-tuple-element.15.refs_0_, bf16[400,128]{1,0:T(8,128)(2,1)S(1)} %collective-permute-done.refs_1_, ...), custom_call_target="tpu_custom_call" | custom-call | flops 35999997952 | bytes 1048576 | tf_op jit(solution)/shard_map/lattice/pallas_call | solution.py:372
  57.7 0.1 copy.12
  57.8 0.1 copy.13
  57.9 0.1 broadcast_multiply_fusion.1
  58.0 0.1 mul.37
  58.1 0.1 mul.40
  58.3 0.1 collective-permute-start.6
  58.3 1.6 %collective-permute-start.7 = (bf16[240,128]{1,0:T(8,128)(2,1)S(1)}, bf16[240,128]{1,0:T(8,128)(2,1)S(1)}, u32[]{:S(2)}, u32[]{:S(2)}) collective-permute-start(bf16[240,128]{1,0:T(8,128)(2,1)S(1)} %get-tuple-element.19), channel_id=1, source_target_pairs={{0,16},{8,24},{16,0},{24,8},{1,17},{9,25},{17,1},{25,9},{2,18},{10... | collective-permute-start | bytes 184328 | tf_op jit(solution)/shard_map/ppermute | solution.py:517
  59.9 0.3 collective-permute-start.8
  60.2 2.5 %collective-permute-done.7.refs_2_ = bf16[240,128]{1,0:T(8,128)(2,1)S(1)} collective-permute-done((bf16[240,128]{1,0:T(8,128)(2,1)S(1)}, bf16[240,128]{1,0:T(8,128)(2,1)S(1)}, u32[]{:S(2)}, u32[]{:S(2)}) %collective-permute-start.7) | collective-permute-done | bytes 61472 | tf_op jit(solution)/shard_map/ppermute | solution.py:517
  62.8 1.1 %collective-permute-done.8.refs_3_ = bf16[240,128]{1,0:T(8,128)(2,1)S(1)} collective-permute-done((bf16[240,128]{1,0:T(8,128)(2,1)S(1)}, bf16[240,128]{1,0:T(8,128)(2,1)S(1)}, u32[]{:S(2)}, u32[]{:S(2)}) %collective-permute-start.8) | collective-permute-done | bytes 61472 | tf_op jit(solution)/shard_map/ppermute | solution.py:517
  63.9 2.1 %finish.1 = (bf16[2,6144]{1,0:T(2,128)(2,1)}, bf16[2,6144]{1,0:T(2,128)(2,1)}, f32[2,8]{1,0:T(2,128)}) custom-call(bf16[240,128]{1,0:T(8,128)(2,1)S(1)} %get-tuple-element.17.refs_0_, bf16[240,128]{1,0:T(8,128)(2,1)S(1)} %collective-permute-done.6.refs_1_, bf16[240,128]{1,0:T(8,128)(2,1)S(1)} %collective-permute-done.7.refs_2_, ...), custom_call_target="tpu_custom_call" | custom-call | flops 2100000000 | bytes 1048576 | tf_op jit(solution)/shard_map/finish/pallas_call | solution.py:502
  (17 shorter events, 0.0 us)
Async XLA Ops:
  0.6 8.0 %collective-permute-start.3 = (bf16[2,6144]{1,0:T(2,128)(2,1)}, bf16[2,6144]{1,0:T(2,128)(2,1)S(1)}, u32[]{:S(2)}, u32[]{:S(2)}) collective-permute-start(bf16[2,6144]{1,0:T(2,128)(2,1)} %bitcast.10), channel_id=1, source_target_pairs={{0,1},{1,0},{2,3},{3,2},{4,5},{5,4},{6,7},{7,6},{8,9},{9,8},{10,11... | collective-permute-start | bytes 73736 | tf_op jit(solution)/shard_map/ppermute | solution.py:517
  3.6 0.8 %copy-start = (bf16[2,1,6144]{2,0,1:T(2,128)(2,1)S(1)}, bf16[2,1,6144]{2,0,1:T(2,128)(2,1)}, u32[]{:S(2)}) copy-start(bf16[2,1,6144]{2,0,1:T(2,128)(2,1)} %param.7) | copy-start | bytes 73732
  4.4 0.7 %copy-start.3 = (s32[6144]{0:T(1024)S(1)}, s32[6144]{0:T(1024)}, u32[]{:S(2)}) copy-start(s32[6144]{0:T(1024)} %param.8) | copy-start | bytes 73732
  5.1 13.6 %copy-start.2 = (bf16[2,72,6144]{2,1,0:T(8,128)(2,1)S(1)}, bf16[2,72,6144]{2,1,0:T(8,128)(2,1)}, u32[]{:S(2)}) copy-start(bf16[2,72,6144]{2,1,0:T(8,128)(2,1)} %refs_7_.1) | copy-start | bytes 5308420
  8.7 5.2 %collective-permute-start.4 = (bf16[2,2,6144]{2,0,1:T(2,128)(2,1)S(1)}, bf16[2,2,6144]{2,0,1:T(2,128)(2,1)S(1)}, u32[]{:S(2)}, u32[]{:S(2)}) collective-permute-start(bf16[2,2,6144]{2,0,1:T(2,128)(2,1)S(1)} %pad_maximum_fusion.1), channel_id=1, source_target_pairs={{0,4},{1,5},{2,6},{3,7},{4,0},{5,1},{6,2},{7,3},{8,12},{9,13},{10,... | collective-permute-start | bytes 147464 | tf_op jit(solution)/shard_map/ppermute | solution.py:517
  11.3 4.7 %collective-permute-start.1 = (bf16[400,128]{1,0:T(8,128)(2,1)S(1)}, bf16[400,128]{1,0:T(8,128)(2,1)S(1)}, u32[]{:S(2)}, u32[]{:S(2)}) collective-permute-start(bf16[400,128]{1,0:T(8,128)(2,1)S(1)} %get-tuple-element.15.refs_0_), channel_id=1, source_target_pairs={{0,16},{8,24},{16,0},{24,8},{1,17},{9,25},{17,1},{25,9},{2,18},{10... | collective-permute-start | bytes 307208 | tf_op jit(solution)/shard_map/ppermute | solution.py:517
  12.8 7.2 %collective-permute-start = (bf16[400,128]{1,0:T(8,128)(2,1)S(1)}, bf16[400,128]{1,0:T(8,128)(2,1)S(1)}, u32[]{:S(2)}, u32[]{:S(2)}) collective-permute-start(bf16[400,128]{1,0:T(8,128)(2,1)S(1)} %get-tuple-element.15.refs_0_), channel_id=1, source_target_pairs={{0,8},{8,0},{16,24},{24,16},{1,9},{9,1},{17,25},{25,17},{2,10},{10... | collective-permute-start | bytes 307208 | tf_op jit(solution)/shard_map/ppermute | solution.py:517
  14.0 4.7 %collective-permute-start.5 = (bf16[2,4,6144]{2,0,1:T(2,128)(2,1)S(1)}, bf16[2,4,6144]{2,0,1:T(2,128)(2,1)S(1)}, u32[]{:S(2)}, u32[]{:S(2)}) collective-permute-start(bf16[2,4,6144]{2,0,1:T(2,128)(2,1)S(1)} %pad_maximum_fusion), channel_id=1, source_target_pairs={{0,2},{1,3},{2,0},{3,1},{4,6},{5,7},{6,4},{7,5},{8,10},{9,11},{10,... | collective-permute-start | bytes 294920 | tf_op jit(solution)/shard_map/ppermute | solution.py:517
  16.0 4.0 %collective-permute-start.2 = (bf16[400,128]{1,0:T(8,128)(2,1)S(1)}, bf16[400,128]{1,0:T(8,128)(2,1)S(1)}, u32[]{:S(2)}, u32[]{:S(2)}) collective-permute-start(bf16[400,128]{1,0:T(8,128)(2,1)S(1)} %collective-permute-done.1.refs_2_), channel_id=1, source_target_pairs={{0,8},{8,0},{16,24},{24,16},{1,9},{9,1},{17,25},{25,17},{2,10},{10... | collective-permute-start | bytes 307208 | tf_op jit(solution)/shard_map/ppermute | solution.py:517
  18.7 1.3 %copy-start.5 = (bf16[2176,256]{1,0:T(8,128)(2,1)S(1)}, bf16[2176,256]{1,0:T(8,128)(2,1)}, u32[]{:S(2)}) copy-start(bf16[2176,256]{1,0:T(8,128)(2,1)} %constant.5.clone.refs_6_) | copy-start | bytes 3342340
  20.0 37.7 %copy-start.6 = (f32[4,18,18]{2,0,1:T(4,128)S(1)}, f32[4,18,18]{2,0,1:T(4,128)}, u32[]{:S(2)}) copy-start(f32[4,18,18]{2,0,1:T(4,128)} %param.11) | copy-start | bytes 15556
  20.0 37.8 %copy-start.7 = (f32[4,18,18]{2,0,1:T(4,128)S(1)}, f32[4,18,18]{2,0,1:T(4,128)}, u32[]{:S(2)}) copy-start(f32[4,18,18]{2,0,1:T(4,128)} %param.12) | copy-start | bytes 15556
  20.0 43.9 %copy-start.1 = (bf16[2,1,6144]{2,0,1:T(2,128)(2,1)S(1)}, bf16[2,1,6144]{2,0,1:T(2,128)(2,1)}, u32[]{:S(2)}) copy-start(bf16[2,1,6144]{2,0,1:T(2,128)(2,1)} %param.7) | copy-start | bytes 73732
  20.0 43.9 %copy-start.4 = (s32[6144]{0:T(1024)S(1)}, s32[6144]{0:T(1024)}, u32[]{:S(2)}) copy-start(s32[6144]{0:T(1024)} %param.8) | copy-start | bytes 73732
  58.3 2.0 %collective-permute-start.6 = (bf16[240,128]{1,0:T(8,128)(2,1)S(1)}, bf16[240,128]{1,0:T(8,128)(2,1)S(1)}, u32[]{:S(2)}, u32[]{:S(2)}) collective-permute-start(bf16[240,128]{1,0:T(8,128)(2,1)S(1)} %get-tuple-element.18), channel_id=1, source_target_pairs={{0,8},{8,0},{16,24},{24,16},{1,9},{9,1},{17,25},{25,17},{2,10},{10... | collective-permute-start | bytes 184328 | tf_op jit(solution)/shard_map/ppermute | solution.py:517
  58.3 4.4 %collective-permute-start.7 = (bf16[240,128]{1,0:T(8,128)(2,1)S(1)}, bf16[240,128]{1,0:T(8,128)(2,1)S(1)}, u32[]{:S(2)}, u32[]{:S(2)}) collective-permute-start(bf16[240,128]{1,0:T(8,128)(2,1)S(1)} %get-tuple-element.19), channel_id=1, source_target_pairs={{0,16},{8,24},{16,0},{24,8},{1,17},{9,25},{17,1},{25,9},{2,18},{10... | collective-permute-start | bytes 184328 | tf_op jit(solution)/shard_map/ppermute | solution.py:517
  59.9 4.0 %collective-permute-start.8 = (bf16[240,128]{1,0:T(8,128)(2,1)S(1)}, bf16[240,128]{1,0:T(8,128)(2,1)S(1)}, u32[]{:S(2)}, u32[]{:S(2)}) collective-permute-start(bf16[240,128]{1,0:T(8,128)(2,1)S(1)} %get-tuple-element.20), channel_id=1, source_target_pairs={{0,24},{8,16},{16,8},{24,0},{1,25},{9,17},{17,9},{25,1},{2,26},{10... | collective-permute-start | bytes 184328 | tf_op jit(solution)/shard_map/ppermute | solution.py:517

commit v5 on v4

--- a/solution.py
+++ b/solution.py
@@ -430,9 +430,9 @@
     )(*every, beta)
 
 
-def finish_kernel(length, planes, chunks, blocks, bands, *refs):
+def finish_kernel(length, planes, chunks, blocks, *refs):
     parts = refs[:blocks]
-    slot_ref, gvec_ref, psi_ref, beta_ref, atoms_ref, hpsi_ref, spsi_ref, gram_ref = refs[blocks:]
+    slot_ref, gvec_ref, psi_ref, beta_ref, atoms_ref, hpsi_ref, spsi_ref = refs[blocks:]
     waves = slot_ref.shape[1]
     count = beta_ref.shape[1]
     total = parts[0][...].astype(jnp.float32)
@@ -451,6 +451,54 @@
     on_im = jnp.concatenate([-d_im, d_re, -q_im, q_re, none], axis=0).astype(jnp.bfloat16)
     added = dot(on_re, beta_ref[0]) + dot(on_im, beta_ref[1])
 
+    local = total[: 2 * chunks]
+    turned = jnp.concatenate([local[:chunks].T, local[chunks:].T], axis=0).astype(jnp.bfloat16)
+    x, y, z = cell_parts(gvec_ref[...], length)
+    x = x + (lax.axis_index("pw") * planes).astype(jnp.float32)
+
+    def fold(level):
+        return jnp.where(level < length // 2, level, level - length)
+
+    x, y, z = fold(x), fold(y), fold(z)
+    kinetic = 4.0 * (x * x + y * y + z * z) / (length * length)
+    slot = slot_ref[...]
+    high = jnp.floor((slot + 0.5) * (1.0 / LANES))
+    low = slot - high * LANES
+    for tile in range(waves // LANES):
+        span = slice(tile * LANES, (tile + 1) * LANES)
+        at_high = where_bf16(iota((chunks, LANES), 0) == high[:, span], 1.0)
+        rows = dot(turned, at_high)
+        mine = iota((LANES, LANES), 0) == low[:, span]
+        re = jnp.sum(jnp.where(mine, rows[:LANES], 0.0), axis=0, keepdims=True)
+        im = jnp.sum(jnp.where(mine, rows[LANES:], 0.0), axis=0, keepdims=True)
+        both = jnp.concatenate([re, im], axis=0)
+        psi = psi_ref[:, span].astype(jnp.float32)
+        hpsi_ref[:, span] = (both + kinetic[:, span] * psi + added[0:2, span]).astype(jnp.bfloat16)
+        spsi_ref[:, span] = (psi + added[2:4, span]).astype(jnp.bfloat16)
+
+
+def finish(parts, slot, index, psi, beta, atoms, length, planes, chunks):
+    blocks = len(parts)
+    return pl.pallas_call(
+        functools.partial(finish_kernel, length, planes, chunks, blocks),
+        out_shape=(
+            jax.ShapeDtypeStruct(psi.shape, jnp.bfloat16),
+            jax.ShapeDtypeStruct(psi.shape, jnp.bfloat16),
+        ),
+        compiler_params=pltpu.CompilerParams(vmem_limit_bytes=16 * MIB),
+        cost_estimate=cost(2.1),
+        name="finish",
+    )(*parts, slot, index, psi, beta, atoms)
+
+
+def gram_kernel(waves, bands, count, *refs):
+    atoms_ref, gram_ref = refs[-2:]
+    sums = refs[0][...]
+    for ref in refs[1:-2]:
+        sums = sums + ref[...]
+    half_size = sums.shape[0] // 2
+    coef = jnp.dot(sums, atoms_ref[...], precision=lax.Precision.HIGHEST, preferred_element_type=jnp.float32)
+    coef = coef.astype(jnp.bfloat16).astype(jnp.float32)
     own_re, own_im = sums[:1], sums[half_size : half_size + 1]
     each_re, each_im = coef[:half_size, LANES:], coef[half_size:, LANES:]
     over = iota((half_size, LANES), 1) == count
@@ -469,47 +517,17 @@
     for n, value in enumerate((gram_re, gram_im)):
         value = jnp.sum(value, axis=1, keepdims=True)
         value = jnp.sum(jnp.where(here, value, 0.0), axis=0, keepdims=True)
-        gram_ref[n : n + 1, :] = value * (1.0 / (waves * blocks))
-
-    local = total[: 2 * chunks]
-    turned = jnp.concatenate([local[:chunks].T, local[chunks:].T], axis=0).astype(jnp.bfloat16)
-    x, y, z = cell_parts(gvec_ref[...], length)
-    x = x + (lax.axis_index("pw") * planes).astype(jnp.float32)
-
-    def fold(level):
-        return jnp.where(level < length // 2, level, level - length)
-
-    x, y, z = fold(x), fold(y), fold(z)
-    kinetic = 4.0 * (x * x + y * y + z * z) / (length * length)
-    slot = slot_ref[...]
-    high = jnp.floor((slot + 0.5) * (1.0 / LANES))
-    low = slot - high * LANES
-    for tile in range(waves // LANES):
-        span = slice(tile * LANES, (tile + 1) * LANES)
-        at_high = where_bf16(iota((chunks, LANES), 0) == high[:, span], 1.0)
-        rows = dot(turned, at_high)
-        mine = iota((LANES, LANES), 0) == low[:, span]
-        re = jnp.sum(jnp.where(mine, rows[:LANES], 0.0), axis=0, keepdims=True)
-        im = jnp.sum(jnp.where(mine, rows[LANES:], 0.0), axis=0, keepdims=True)
-        both = jnp.concatenate([re, im], axis=0)
-        psi = psi_ref[:, span].astype(jnp.float32)
-        hpsi_ref[:, span] = (both + kinetic[:, span] * psi + added[0:2, span]).astype(jnp.bfloat16)
-        spsi_ref[:, span] = (psi + added[2:4, span]).astype(jnp.bfloat16)
-
-
-def finish(parts, slot, index, psi, beta, atoms, length, planes, chunks, bands):
-    blocks = len(parts)
+        gram_ref[n : n + 1, :] = value * (1.0 / (waves))
+
+
+def gram_row(parts, atoms, waves, bands, count):
     return pl.pallas_call(
-        functools.partial(finish_kernel, length, planes, chunks, blocks, bands),
-        out_shape=(
-            jax.ShapeDtypeStruct(psi.shape, jnp.bfloat16),
-            jax.ShapeDtypeStruct(psi.shape, jnp.bfloat16),
-            jax.ShapeDtypeStruct((2, bands), jnp.float32),
-        ),
+        functools.partial(gram_kernel, waves, bands, count),
+        out_shape=jax.ShapeDtypeStruct((2, bands), jnp.float32),
         compiler_params=pltpu.CompilerParams(vmem_limit_bytes=16 * MIB),
-        cost_estimate=cost(2.1),
-        name="finish",
-    )(*parts, slot, index, psi, beta, atoms)
+        cost_estimate=cost(0.7),
+        name="gram_row",
+    )(*parts, atoms)
 
 
 def swap(value, axis, step):
@@ -536,14 +554,14 @@
     return [found[s] for s in range(size)]
 
 
-def from_bands(value, axis, after):
+def from_bands_early(value, axis, after):
     size = lax.axis_size(axis)
     if not doubles(size):
         pairs = [[(k, (k + s) % size) for k in range(size)] for s in range(1, size)]
         held = [value] + [lax.ppermute(value, axis, pair) for pair in pairs]
         return [part[:, None] for part in held]
     held = [value[:, None]]
-    for step in doubling_steps(size):
+    for step in doubling_steps(size)[:-1]:
         if len(held) == 1:
             other = swap(value, axis, step)
             other, _ = lax.optimization_barrier((other, after))
@@ -552,6 +570,14 @@
             joined = jnp.concatenate(held, axis=1)
             held = [joined, swap(joined, axis, step)]
     return held
+
+
+def from_bands_late(held, axis):
+    size = lax.axis_size(axis)
+    if size == 1 or not doubles(size):
+        return held
+    joined = jnp.concatenate(held, axis=1)
+    return [joined, swap(joined, axis, doubling_steps(size)[-1])]
 
 
 def atom_blocks(matrix):
@@ -572,12 +598,17 @@
     mine = psi.reshape(2, width)
     pay, slot = group_waves(index, mine, length, planes, chunks)
     pays = from_blocks(pay, "pw")
-    sums = project(from_bands(mine, "band", pay), beta, bands)
-    outs = lattice(pays, sums, vloc, length, planes, chunks)
-    dmat, qmat, _ = lax.optimization_barrier((dmat, qmat, outs[0]))
+    early = from_bands_early(mine, "band", pay)
+    later, _ = lax.optimization_barrier((mine, pay))
+    outs = lattice(pays, project([later[:, None]], beta, 1), vloc, length, planes, chunks)
+    parts = [outs[0]] + [swap(outs[s], "pw", s) for s in range(1, blocks)]
+    dmat, qmat, early, _ = lax.optimization_barrier((dmat, qmat, early, outs[0]))
+    every = from_bands_late(early, "band")
     atoms = jnp.concatenate([atom_blocks(dmat), atom_blocks(qmat)], axis=1)
-    parts = [outs[0]] + [swap(outs[s], "pw", s) for s in range(1, blocks)]
-    hpsi, spsi, gram = finish(parts, slot, index, mine, beta, atoms, length, planes, chunks, bands)
+    hpsi, spsi = finish(parts, slot, index, mine, beta, atoms, length, planes, chunks)
+    sums = project(every, beta, bands)
+    sums = [sums] + [swap(sums, "pw", s) for s in range(1, blocks)]
+    gram = gram_row(sums, atoms, width * blocks, bands, beta.shape[1])
     return (hpsi.reshape(2, 1, width), spsi.reshape(2, 1, width), gram.reshape(2, 1, bands))
 
 

time: 65.3 us -> 64.9 us (level); the launches traced: 66 us -> 64.6 us
  waiting for transfers between devices: 7.77 us -> 1.78 us
  starting transfers between devices: 10.6 us -> 13 us
  Pallas kernels: 44.3 us -> 46.6 us
    ppermute x9 -> x12, waiting for transfers between devices: 7.77 us -> 1.78 us  [swap(): return lax.ppermute(value, axis, [(k, k ^ step) for k in range(size)])]
    ppermute x9 -> x12, starting transfers between devices: 10.6 us -> 13 us  [swap(): return lax.ppermute(value, axis, [(k, k ^ step) for k in range(size)])]
    pallas_call x1 -> x2, Pallas kernels: 1.2 us -> 2.39 us  [project(): pl.pallas_call(functools.partial(project_kernel, bands), out_shape=jax.Sh...]
    pallas_call x0 -> x1, Pallas kernels: none -> 0.83 us  [gram_row(): pl.pallas_call(functools.partial(gram_kernel, waves, bands, count), out_s...]
    unnamed x16 -> x17, local copies, waits for them, and re-layouts: 1.54 us -> 1.54 us
  transfers between devices with their start and end apart: 9 -> 12, of which waited for: 5 -> 2; matrix products, arithmetic and copies ran while one was open for 0% -> 1% of each run, Pallas kernels for 7% -> 65%
where the time goes in v5:
time: 64.9 us; the launch traced here: 64.6 us
  Pallas kernels  46.6 us (72%)
  starting transfers between devices  13 us (20%)
  local copies, waits for them, and re-layouts  2.1 us (3%)
  waiting for transfers between devices  1.78 us (3%)
  between operations  0.84 us (1%)
    pallas_call x1, Pallas kernels, lattice(): pl.pallas_call(functools.partial(lattice_kernel, length, planes, chunks,...  37.8 us
    ppermute x12, starting transfers between devices, swap(): return lax.ppermute(value, axis, [(k, k ^ step) for k in range(size)])  13 us
    pallas_call x1, Pallas kernels, group_waves(): pl.pallas_call(functools.partial(group_kernel, length, planes, chunks), o...  3.43 us
    pallas_call x2, Pallas kernels, project(): pl.pallas_call(functools.partial(project_kernel, bands), out_shape=jax.Sh...  2.39 us
    pallas_call x1, Pallas kernels, finish(): pl.pallas_call(functools.partial(finish_kernel, length, planes, chunks, b...  2.12 us
    ppermute x12, waiting for transfers between devices, swap(): return lax.ppermute(value, axis, [(k, k ^ step) for k in range(size)])  1.78 us
    unnamed x17, local copies, waits for them, and re-layouts  1.54 us
  transfers between devices with their start and end apart: 12, of which 2 were waited for; matrix products, arithmetic and copies ran while one was open for 1% of the time, Pallas kernels for 65%

profile of v5, /device:TPU:0, one launch (start us, length us, event | category | flops | bytes accessed | tf_op | source)
XLA Modules:
  0.0 64.6 jit_solution(10463789185145875163)
XLA Ops:
  0.6 0.0 copy-start
  0.6 0.7 %copy-done = bf16[2,1,6144]{2,0,1:T(2,128)(2,1)S(1)} copy-done((bf16[2,1,6144]{2,0,1:T(2,128)(2,1)S(1)}, bf16[2,1,6144]{2,0,1:T(2,128)(2,1)}, u32[]{:S(2)}) %copy-start) | copy-done | bytes 24600
  1.4 0.7 %copy-done.3 = s32[6144]{0:T(1024)S(1)} copy-done((s32[6144]{0:T(1024)S(1)}, s32[6144]{0:T(1024)}, u32[]{:S(2)}) %copy-start.3) | copy-done | bytes 24600
  2.1 3.4 %group_waves.1 = (bf16[400,128]{1,0:T(8,128)(2,1)S(1)}, f32[1,6144]{1,0:T(1,128)S(1)}) custom-call(s32[1,6144]{1,0:T(1,128)S(1)} %bitcast.14, bf16[2,6144]{1,0:T(2,128)(2,1)S(1)} %bitcast.11), custom_call_target="tpu_custom_call" | custom-call | flops 3400000000 | bytes 1048576 | tf_op jit(solution)/shard_map/group_waves/pallas_call | solution.py:159
  5.5 3.0 %collective-permute-start.1 = (bf16[400,128]{1,0:T(8,128)(2,1)S(1)}, bf16[400,128]{1,0:T(8,128)(2,1)S(1)}, u32[]{:S(2)}, u32[]{:S(2)}) collective-permute-start(bf16[400,128]{1,0:T(8,128)(2,1)S(1)} %get-tuple-element.17.refs_0_), channel_id=1, source_target_pairs={{0,16},{8,24},{16,0},{24,8},{1,17},{9,25},{17,1},{25,9},{2,18},{10... | collective-permute-start | bytes 307208 | tf_op jit(solution)/shard_map/ppermute | solution.py:535
  8.6 1.5 %collective-permute-start.6 = (bf16[2,6144]{1,0:T(2,128)(2,1)S(1)}, bf16[2,6144]{1,0:T(2,128)(2,1)S(1)}, u32[]{:S(2)}, u32[]{:S(2)}) collective-permute-start(bf16[2,6144]{1,0:T(2,128)(2,1)S(1)} %bitcast.12), channel_id=1, source_target_pairs={{0,1},{1,0},{2,3},{3,2},{4,5},{5,4},{6,7},{7,6},{8,9},{9,8},{10,11... | collective-permute-start | bytes 73736 | tf_op jit(solution)/shard_map/ppermute | solution.py:535
  10.1 0.0 copy-start.5
  10.1 1.2 %project.2.refs_4_ = f32[16,128]{1,0:T(8,128)S(1)} custom-call(bf16[2,1,6144]{2,1,0:T(2,128)(2,1)S(1)} %copy.15.refs_0_, bf16[2,72,6144]{2,1,0:T(8,128)(2,1)S(1)} %copy-done.2), custom_call_target="tpu_custom_call" | custom-call | flops 1200000000 | bytes 1048576 | tf_op jit(solution)/shard_map/project/pallas_call | solution.py:422
  11.4 1.0 %collective-permute-done.6 = bf16[2,6144]{1,0:T(2,128)(2,1)S(1)} collective-permute-done((bf16[2,6144]{1,0:T(2,128)(2,1)S(1)}, bf16[2,6144]{1,0:T(2,128)(2,1)S(1)}, u32[]{:S(2)}, u32[]{:S(2)}) %collective-permute-start.6) | collective-permute-done | bytes 24608 | tf_op jit(solution)/shard_map/ppermute | solution.py:535
  12.5 0.1 collective-permute-start.2
  12.5 0.1 pad_maximum_fusion.1
  12.7 0.0 copy-start.6
  12.7 2.7 %collective-permute-start.7 = (bf16[2,2,6144]{2,1,0:T(2,128)(2,1)S(1)}, bf16[2,2,6144]{2,1,0:T(2,128)(2,1)S(1)}, u32[]{:S(2)}, u32[]{:S(2)}) collective-permute-start(bf16[2,2,6144]{2,1,0:T(2,128)(2,1)S(1)} %pad_maximum_fusion.1), channel_id=1, source_target_pairs={{0,4},{1,5},{2,6},{3,7},{4,0},{5,1},{6,2},{7,3},{8,12},{9,13},{10,... | collective-permute-start | bytes 147464 | tf_op jit(solution)/shard_map/ppermute | solution.py:535
  15.4 37.8 %lattice.1 = (bf16[240,128]{1,0:T(8,128)(2,1)S(1)}, bf16[240,128]{1,0:T(8,128)(2,1)S(1)}, bf16[240,128]{1,0:T(8,128)(2,1)S(1)}, bf16[240,128]{1,0:T(8,128)(2,1)S(1)}) custom-call(bf16[400,128]{1,0:T(8,128)(2,1)S(1)} %get-tuple-element.17.refs_0_, bf16[400,128]{1,0:T(8,128)(2,1)S(1)} %collective-permute-done.refs_1_, ...), custom_call_target="tpu_custom_call" | custom-call | flops 35999997952 | bytes 1048576 | tf_op jit(solution)/shard_map/lattice/pallas_call | solution.py:372
  53.2 0.1 pad_maximum_fusion.refs_0_
  53.3 1.6 %collective-permute-start.8 = (bf16[2,4,6144]{2,1,0:T(4,128)(2,1)S(1)}, bf16[2,4,6144]{2,1,0:T(4,128)(2,1)S(1)}, u32[]{:S(2)}, u32[]{:S(2)}) collective-permute-start(bf16[2,4,6144]{2,1,0:T(4,128)(2,1)S(1)} %pad_maximum_fusion.refs_0_), channel_id=1, source_target_pairs={{0,2},{1,3},{2,0},{3,1},{4,6},{5,7},{6,4},{7,5},{8,10},{9,11},{10,... | collective-permute-start | bytes 294920 | tf_op jit(solution)/shard_map/ppermute | solution.py:535
  54.9 0.1 copy.18
  55.0 0.1 copy.19
  55.1 0.1 broadcast_multiply_fusion.1
  55.3 0.1 mul.37
  55.4 0.1 mul.40
  55.5 0.1 collective-permute-start.3
  55.6 0.8 %collective-permute-start.4 = (bf16[240,128]{1,0:T(8,128)(2,1)S(1)}, bf16[240,128]{1,0:T(8,128)(2,1)S(1)}, u32[]{:S(2)}, u32[]{:S(2)}) collective-permute-start(bf16[240,128]{1,0:T(8,128)(2,1)S(1)} %get-tuple-element.21), channel_id=1, source_target_pairs={{0,16},{8,24},{16,0},{24,8},{1,17},{9,25},{17,1},{25,9},{2,18},{10... | collective-permute-start | bytes 184328 | tf_op jit(solution)/shard_map/ppermute | solution.py:535
  56.4 1.1 %collective-permute-start.5 = (bf16[240,128]{1,0:T(8,128)(2,1)S(1)}, bf16[240,128]{1,0:T(8,128)(2,1)S(1)}, u32[]{:S(2)}, u32[]{:S(2)}) collective-permute-start(bf16[240,128]{1,0:T(8,128)(2,1)S(1)} %get-tuple-element.22), channel_id=1, source_target_pairs={{0,24},{8,16},{16,8},{24,0},{1,25},{9,17},{17,9},{25,1},{2,26},{10... | collective-permute-start | bytes 184328 | tf_op jit(solution)/shard_map/ppermute | solution.py:535
  57.5 0.0 copy-start.4
  57.5 0.7 %collective-permute-done.8.refs_1_ = bf16[2,4,6144]{2,1,0:T(4,128)(2,1)S(1)} collective-permute-done((bf16[2,4,6144]{2,1,0:T(4,128)(2,1)S(1)}, bf16[2,4,6144]{2,1,0:T(4,128)(2,1)S(1)}, u32[]{:S(2)}, u32[]{:S(2)}) %collective-permute-start.8) | collective-permute-done | bytes 98336 | tf_op jit(solution)/shard_map/ppermute | solution.py:535
  58.2 1.2 %project.3.refs_0_ = f32[16,128]{1,0:T(8,128)S(1)} custom-call(bf16[2,4,6144]{2,1,0:T(4,128)(2,1)S(1)} %pad_maximum_fusion.refs_0_, bf16[2,4,6144]{2,1,0:T(4,128)(2,1)S(1)} %collective-permute-done.8.refs_1_, bf16[2,72,6144]{2,1,0:T(8,128)(2,1)S(1)} %copy-done.2), custom_call_target="tpu_custom_call" | custom-call | flops 1200000000 | bytes 1048576 | tf_op jit(solution)/shard_map/project/pallas_call | solution.py:422
  59.5 0.8 %collective-permute-start.10 = (f32[16,128]{1,0:T(8,128)S(1)}, f32[16,128]{1,0:T(8,128)S(1)}, u32[]{:S(2)}, u32[]{:S(2)}) collective-permute-start(f32[16,128]{1,0:T(8,128)S(1)} %project.3.refs_0_), channel_id=1, source_target_pairs={{0,16},{8,24},{16,0},{24,8},{1,17},{9,25},{17,1},{25,9},{2,18},{10... | collective-permute-start | bytes 24584 | tf_op jit(solution)/shard_map/ppermute | solution.py:535
  60.3 0.2 collective-permute-start.11
  60.5 1.2 %collective-permute-start.9 = (f32[16,128]{1,0:T(8,128)S(1)}, f32[16,128]{1,0:T(8,128)S(1)}, u32[]{:S(2)}, u32[]{:S(2)}) collective-permute-start(f32[16,128]{1,0:T(8,128)S(1)} %project.3.refs_0_), channel_id=1, source_target_pairs={{0,8},{8,0},{16,24},{24,16},{1,9},{9,1},{17,25},{25,17},{2,10},{10... | collective-permute-start | bytes 24584 | tf_op jit(solution)/shard_map/ppermute | solution.py:535
  61.7 2.1 %finish.1 = (bf16[2,6144]{1,0:T(2,128)(2,1)}, bf16[2,6144]{1,0:T(2,128)(2,1)}) custom-call(bf16[240,128]{1,0:T(8,128)(2,1)S(1)} %get-tuple-element.19.refs_0_, bf16[240,128]{1,0:T(8,128)(2,1)S(1)} %collective-permute-done.3.refs_1_, bf16[240,128]{1,0:T(8,128)(2,1)S(1)} %collective-permute-done.4.refs_2_, ...), custom_call_target="tpu_custom_call" | custom-call | flops 2100000000 | bytes 1048576 | tf_op jit(solution)/shard_map/finish/pallas_call | solution.py:482
  63.8 0.8 %gram_row.1 = f32[2,8]{1,0:T(2,128)} custom-call(f32[16,128]{1,0:T(8,128)S(1)} %project.3.refs_0_, f32[16,128]{1,0:T(8,128)S(1)} %collective-permute-done.9.refs_1_, f32[16,128]{1,0:T(8,128)S(1)} %collective-permute-done.10.refs_2_, f32[16,128]{1,0:T(8,128)S(1)} %collective-permute-done.11.refs_3_, f32[128,256]{1,0:T(8,128)S(1)} %select_maximum_fusion.refs_8_.refs_4_), custom_call_target="tpu_custom_call" | custom-call | flops 700000000 | bytes 1048576 | tf_op jit(solution)/shard_map/gram_row/pallas_call | solution.py:524
  (26 shorter events, 0.2 us)
Async XLA Ops:
  0.6 0.7 %copy-start = (bf16[2,1,6144]{2,0,1:T(2,128)(2,1)S(1)}, bf16[2,1,6144]{2,0,1:T(2,128)(2,1)}, u32[]{:S(2)}) copy-start(bf16[2,1,6144]{2,0,1:T(2,128)(2,1)} %param.7) | copy-start | bytes 73732
  1.4 0.7 %copy-start.3 = (s32[6144]{0:T(1024)S(1)}, s32[6144]{0:T(1024)}, u32[]{:S(2)}) copy-start(s32[6144]{0:T(1024)} %param.8) | copy-start | bytes 73732
  2.1 8.0 %copy-start.2 = (bf16[2,72,6144]{2,1,0:T(8,128)(2,1)S(1)}, bf16[2,72,6144]{2,1,0:T(8,128)(2,1)}, u32[]{:S(2)}) copy-start(bf16[2,72,6144]{2,1,0:T(8,128)(2,1)} %refs_2_.1) | copy-start | bytes 5308420
  5.5 6.9 %collective-permute-start.1 = (bf16[400,128]{1,0:T(8,128)(2,1)S(1)}, bf16[400,128]{1,0:T(8,128)(2,1)S(1)}, u32[]{:S(2)}, u32[]{:S(2)}) collective-permute-start(bf16[400,128]{1,0:T(8,128)(2,1)S(1)} %get-tuple-element.17.refs_0_), channel_id=1, source_target_pairs={{0,16},{8,24},{16,0},{24,8},{1,17},{9,25},{17,1},{25,9},{2,18},{10... | collective-permute-start | bytes 307208 | tf_op jit(solution)/shard_map/ppermute | solution.py:535
  8.6 6.8 %collective-permute-start = (bf16[400,128]{1,0:T(8,128)(2,1)S(1)}, bf16[400,128]{1,0:T(8,128)(2,1)S(1)}, u32[]{:S(2)}, u32[]{:S(2)}) collective-permute-start(bf16[400,128]{1,0:T(8,128)(2,1)S(1)} %get-tuple-element.17.refs_0_), channel_id=1, source_target_pairs={{0,8},{8,0},{16,24},{24,16},{1,9},{9,1},{17,25},{25,17},{2,10},{10... | collective-permute-start | bytes 307208 | tf_op jit(solution)/shard_map/ppermute | solution.py:535
  8.6 3.8 %collective-permute-start.6 = (bf16[2,6144]{1,0:T(2,128)(2,1)S(1)}, bf16[2,6144]{1,0:T(2,128)(2,1)S(1)}, u32[]{:S(2)}, u32[]{:S(2)}) collective-permute-start(bf16[2,6144]{1,0:T(2,128)(2,1)S(1)} %bitcast.12), channel_id=1, source_target_pairs={{0,1},{1,0},{2,3},{3,2},{4,5},{5,4},{6,7},{7,6},{8,9},{9,8},{10,11... | collective-permute-start | bytes 73736 | tf_op jit(solution)/shard_map/ppermute | solution.py:535
  10.1 5.2 %copy-start.5 = (bf16[2176,256]{1,0:T(8,128)(2,1)S(1)}, bf16[2176,256]{1,0:T(8,128)(2,1)}, u32[]{:S(2)}) copy-start(bf16[2176,256]{1,0:T(8,128)(2,1)} %constant.5.clone.refs_6_) | copy-start | bytes 3342340
  12.5 2.9 %collective-permute-start.2 = (bf16[400,128]{1,0:T(8,128)(2,1)S(1)}, bf16[400,128]{1,0:T(8,128)(2,1)S(1)}, u32[]{:S(2)}, u32[]{:S(2)}) collective-permute-start(bf16[400,128]{1,0:T(8,128)(2,1)S(1)} %collective-permute-done.1.refs_2_), channel_id=1, source_target_pairs={{0,8},{8,0},{16,24},{24,16},{1,9},{9,1},{17,25},{25,17},{2,10},{10... | collective-permute-start | bytes 307208 | tf_op jit(solution)/shard_map/ppermute | solution.py:535
  12.7 42.3 %copy-start.6 = (f32[4,18,18]{2,0,1:T(4,128)S(1)}, f32[4,18,18]{2,0,1:T(4,128)}, u32[]{:S(2)}) copy-start(f32[4,18,18]{2,0,1:T(4,128)} %param.11) | copy-start | bytes 15556
  12.7 42.4 %copy-start.7 = (f32[4,18,18]{2,0,1:T(4,128)S(1)}, f32[4,18,18]{2,0,1:T(4,128)}, u32[]{:S(2)}) copy-start(f32[4,18,18]{2,0,1:T(4,128)} %param.12) | copy-start | bytes 15556
  12.7 40.5 %collective-permute-start.7 = (bf16[2,2,6144]{2,1,0:T(2,128)(2,1)S(1)}, bf16[2,2,6144]{2,1,0:T(2,128)(2,1)S(1)}, u32[]{:S(2)}, u32[]{:S(2)}) collective-permute-start(bf16[2,2,6144]{2,1,0:T(2,128)(2,1)S(1)} %pad_maximum_fusion.1), channel_id=1, source_target_pairs={{0,4},{1,5},{2,6},{3,7},{4,0},{5,1},{6,2},{7,3},{8,12},{9,13},{10,... | collective-permute-start | bytes 147464 | tf_op jit(solution)/shard_map/ppermute | solution.py:535
  53.3 5.0 %collective-permute-start.8 = (bf16[2,4,6144]{2,1,0:T(4,128)(2,1)S(1)}, bf16[2,4,6144]{2,1,0:T(4,128)(2,1)S(1)}, u32[]{:S(2)}, u32[]{:S(2)}) collective-permute-start(bf16[2,4,6144]{2,1,0:T(4,128)(2,1)S(1)} %pad_maximum_fusion.refs_0_), channel_id=1, source_target_pairs={{0,2},{1,3},{2,0},{3,1},{4,6},{5,7},{6,4},{7,5},{8,10},{9,11},{10,... | collective-permute-start | bytes 294920 | tf_op jit(solution)/shard_map/ppermute | solution.py:535
  55.5 5.0 %collective-permute-start.3 = (bf16[240,128]{1,0:T(8,128)(2,1)S(1)}, bf16[240,128]{1,0:T(8,128)(2,1)S(1)}, u32[]{:S(2)}, u32[]{:S(2)}) collective-permute-start(bf16[240,128]{1,0:T(8,128)(2,1)S(1)} %get-tuple-element.20), channel_id=1, source_target_pairs={{0,8},{8,0},{16,24},{24,16},{1,9},{9,1},{17,25},{25,17},{2,10},{10... | collective-permute-start | bytes 184328 | tf_op jit(solution)/shard_map/ppermute | solution.py:535
  55.6 6.1 %collective-permute-start.4 = (bf16[240,128]{1,0:T(8,128)(2,1)S(1)}, bf16[240,128]{1,0:T(8,128)(2,1)S(1)}, u32[]{:S(2)}, u32[]{:S(2)}) collective-permute-start(bf16[240,128]{1,0:T(8,128)(2,1)S(1)} %get-tuple-element.21), channel_id=1, source_target_pairs={{0,16},{8,24},{16,0},{24,8},{1,17},{9,25},{17,1},{25,9},{2,18},{10... | collective-permute-start | bytes 184328 | tf_op jit(solution)/shard_map/ppermute | solution.py:535
  56.4 5.3 %collective-permute-start.5 = (bf16[240,128]{1,0:T(8,128)(2,1)S(1)}, bf16[240,128]{1,0:T(8,128)(2,1)S(1)}, u32[]{:S(2)}, u32[]{:S(2)}) collective-permute-start(bf16[240,128]{1,0:T(8,128)(2,1)S(1)} %get-tuple-element.22), channel_id=1, source_target_pairs={{0,24},{8,16},{16,8},{24,0},{1,25},{9,17},{17,9},{25,1},{2,26},{10... | collective-permute-start | bytes 184328 | tf_op jit(solution)/shard_map/ppermute | solution.py:535
  57.5 4.2 %copy-start.1 = (bf16[2,1,6144]{2,0,1:T(2,128)(2,1)S(1)}, bf16[2,1,6144]{2,0,1:T(2,128)(2,1)}, u32[]{:S(2)}) copy-start(bf16[2,1,6144]{2,0,1:T(2,128)(2,1)} %param.7) | copy-start | bytes 73732
  57.5 4.2 %copy-start.4 = (s32[6144]{0:T(1024)S(1)}, s32[6144]{0:T(1024)}, u32[]{:S(2)}) copy-start(s32[6144]{0:T(1024)} %param.8) | copy-start | bytes 73732
  59.5 4.4 %collective-permute-start.10 = (f32[16,128]{1,0:T(8,128)S(1)}, f32[16,128]{1,0:T(8,128)S(1)}, u32[]{:S(2)}, u32[]{:S(2)}) collective-permute-start(f32[16,128]{1,0:T(8,128)S(1)} %project.3.refs_0_), channel_id=1, source_target_pairs={{0,16},{8,24},{16,0},{24,8},{1,17},{9,25},{17,1},{25,9},{2,18},{10... | collective-permute-start | bytes 24584 | tf_op jit(solution)/shard_map/ppermute | solution.py:535
  60.3 3.6 %collective-permute-start.11 = (f32[16,128]{1,0:T(8,128)S(1)}, f32[16,128]{1,0:T(8,128)S(1)}, u32[]{:S(2)}, u32[]{:S(2)}) collective-permute-start(f32[16,128]{1,0:T(8,128)S(1)} %project.3.refs_0_), channel_id=1, source_target_pairs={{0,24},{8,16},{16,8},{24,0},{1,25},{9,17},{17,9},{25,1},{2,26},{10... | collective-permute-start | bytes 24584 | tf_op jit(solution)/shard_map/ppermute | solution.py:535
  60.5 3.3 %collective-permute-start.9 = (f32[16,128]{1,0:T(8,128)S(1)}, f32[16,128]{1,0:T(8,128)S(1)}, u32[]{:S(2)}, u32[]{:S(2)}) collective-permute-start(f32[16,128]{1,0:T(8,128)S(1)} %project.3.refs_0_), channel_id=1, source_target_pairs={{0,8},{8,0},{16,24},{24,16},{1,9},{9,1},{17,25},{25,17},{2,10},{10... | collective-permute-start | bytes 24584 | tf_op jit(solution)/shard_map/ppermute | solution.py:535

commit v6 on v5

--- a/solution.py
+++ b/solution.py
@@ -217,7 +217,7 @@
     level_y = level[:length]
     group = 4 if blocks % 4 == 0 else 1
     ahead = 8 if blocks == group else 1
-    batch = 16 if planes % 16 == 0 else 1
+    batch = 24 if planes % 24 == 0 else 1
     turns = (used + ahead - 1) // ahead
 
     def place(s, c):
@@ -355,13 +355,14 @@
     rest = sums_ref[...]
     pieces = []
     for _ in range(3):
-        pieces.append(rest.astype(jnp.bfloat16))
-        rest = rest - pieces[-1].astype(jnp.float32)
-    size = sums_ref.shape[0]
+        pieces.append(rest.astype(jnp.bfloat16).astype(jnp.float32))
+        rest = rest - pieces[-1]
+    blank = jnp.zeros((5, LANES), jnp.float32)
+    packed = [piece[:1] for piece in pieces] + [blank] + [piece[8:9] for piece in pieces] + [blank]
+    packed = jnp.concatenate(packed, axis=0).astype(jnp.bfloat16)
     for s in range(blocks):
         outs[s][0 : 2 * chunks, :] = result[s * 2 * chunks : (s + 1) * 2 * chunks, :].astype(jnp.bfloat16)
-        for n, piece in enumerate(pieces):
-            outs[s][2 * chunks + n * size : 2 * chunks + (n + 1) * size, :] = piece
+        outs[s][2 * chunks :, :] = packed
 
 
 def lattice(pays, sums, vloc, length, planes, chunks):
@@ -371,7 +372,7 @@
     vmem = pl.BlockSpec(memory_space=pltpu.VMEM)
     return pl.pallas_call(
         functools.partial(lattice_kernel, length, planes, chunks, blocks),
-        out_shape=[jax.ShapeDtypeStruct((2 * chunks + 3 * sums.shape[0], LANES), jnp.bfloat16)] * blocks,
+        out_shape=[jax.ShapeDtypeStruct((2 * chunks + sums.shape[0], LANES), jnp.bfloat16)] * blocks,
         in_specs=[vmem] * (blocks + 1) + [pl.BlockSpec(memory_space=pl.ANY), vmem],
         out_specs=[vmem] * blocks,
         scratch_shapes=[
@@ -438,10 +439,13 @@
     total = parts[0][...].astype(jnp.float32)
     for part in parts[1:]:
         total = total + part[...].astype(jnp.float32)
-    size = (total.shape[0] - 2 * chunks) // 3
-    half_size = size // 2
-    sums = [total[2 * chunks + n * size : 2 * chunks + (n + 1) * size] for n in range(3)]
-    sums = sums[0] + (sums[1] + sums[2])
+    packed = total[2 * chunks :]
+    half_size = packed.shape[0] // 2
+    blank = jnp.zeros((half_size - 1, LANES), jnp.float32)
+    sums = []
+    for at in (0, half_size):
+        sums += [packed[at : at + 1] + (packed[at + 1 : at + 2] + packed[at + 2 : at + 3]), blank]
+    sums = jnp.concatenate(sums, axis=0)
     coef = jnp.dot(sums, atoms_ref[...], precision=lax.Precision.HIGHEST, preferred_element_type=jnp.float32)
     coef = coef.astype(jnp.bfloat16).astype(jnp.float32)
     d_re, d_im = coef[:1, :count], coef[half_size : half_size + 1, :count]

time: 64.9 us -> 63.7 us (0.982); the launches traced: 64.6 us -> 62.5 us
  Pallas kernels: 46.6 us -> 44.5 us
    pallas_call x1, Pallas kernels: 37.8 us -> 35.7 us  [lattice(): pl.pallas_call(functools.partial(lattice_kernel, length, planes, chunks,...]
  transfers between devices with their start and end apart: 12 -> 12, of which waited for: 2 -> 2; matrix products, arithmetic and copies ran while one was open for 1% -> 1% of each run, Pallas kernels for 65% -> 64%
where the time goes in v6:
time: 63.7 us; the launch traced here: 62.5 us
  Pallas kernels  44.5 us (70%)
  starting transfers between devices  13 us (20%)
  local copies, waits for them, and re-layouts  2.1 us (3%)
  waiting for transfers between devices  1.76 us (3%)
  between operations  0.84 us (1%)
    pallas_call x1, Pallas kernels, lattice(): pl.pallas_call(functools.partial(lattice_kernel, length, planes, chunks,...  35.7 us
    ppermute x12, starting transfers between devices, swap(): return lax.ppermute(value, axis, [(k, k ^ step) for k in range(size)])  13 us
    pallas_call x1, Pallas kernels, group_waves(): pl.pallas_call(functools.partial(group_kernel, length, planes, chunks), o...  3.43 us
    pallas_call x2, Pallas kernels, project(): pl.pallas_call(functools.partial(project_kernel, bands), out_shape=jax.Sh...  2.39 us
    pallas_call x1, Pallas kernels, finish(): pl.pallas_call(functools.partial(finish_kernel, length, planes, chunks, b...  2.12 us
    ppermute x12, waiting for transfers between devices, swap(): return lax.ppermute(value, axis, [(k, k ^ step) for k in range(size)])  1.76 us
    unnamed x17, local copies, waits for them, and re-layouts  1.54 us
  transfers between devices with their start and end apart: 12, of which 2 were waited for; matrix products, arithmetic and copies ran while one was open for 1% of the time, Pallas kernels for 64%

profile of v6, /device:TPU:0, one launch (start us, length us, event | category | flops | bytes accessed | tf_op | source)
XLA Modules:
  0.0 62.5 jit_solution(12337333022033546599)
XLA Ops:
  0.6 0.0 copy-start
  0.6 0.7 %copy-done = bf16[2,1,6144]{2,0,1:T(2,128)(2,1)S(1)} copy-done((bf16[2,1,6144]{2,0,1:T(2,128)(2,1)S(1)}, bf16[2,1,6144]{2,0,1:T(2,128)(2,1)}, u32[]{:S(2)}) %copy-start) | copy-done | bytes 24600
  1.4 0.7 %copy-done.3 = s32[6144]{0:T(1024)S(1)} copy-done((s32[6144]{0:T(1024)S(1)}, s32[6144]{0:T(1024)}, u32[]{:S(2)}) %copy-start.3) | copy-done | bytes 24600
  2.1 3.4 %group_waves.1 = (bf16[400,128]{1,0:T(8,128)(2,1)S(1)}, f32[1,6144]{1,0:T(1,128)S(1)}) custom-call(s32[1,6144]{1,0:T(1,128)S(1)} %bitcast.14, bf16[2,6144]{1,0:T(2,128)(2,1)S(1)} %bitcast.11), custom_call_target="tpu_custom_call" | custom-call | flops 3400000000 | bytes 1048576 | tf_op jit(solution)/shard_map/group_waves/pallas_call | solution.py:159
  5.5 3.0 %collective-permute-start.1 = (bf16[400,128]{1,0:T(8,128)(2,1)S(1)}, bf16[400,128]{1,0:T(8,128)(2,1)S(1)}, u32[]{:S(2)}, u32[]{:S(2)}) collective-permute-start(bf16[400,128]{1,0:T(8,128)(2,1)S(1)} %get-tuple-element.17.refs_0_), channel_id=1, source_target_pairs={{0,16},{8,24},{16,0},{24,8},{1,17},{9,25},{17,1},{25,9},{2,18},{10... | collective-permute-start | bytes 307208 | tf_op jit(solution)/shard_map/ppermute | solution.py:539
  8.6 1.5 %collective-permute-start.6 = (bf16[2,6144]{1,0:T(2,128)(2,1)S(1)}, bf16[2,6144]{1,0:T(2,128)(2,1)S(1)}, u32[]{:S(2)}, u32[]{:S(2)}) collective-permute-start(bf16[2,6144]{1,0:T(2,128)(2,1)S(1)} %bitcast.12), channel_id=1, source_target_pairs={{0,1},{1,0},{2,3},{3,2},{4,5},{5,4},{6,7},{7,6},{8,9},{9,8},{10,11... | collective-permute-start | bytes 73736 | tf_op jit(solution)/shard_map/ppermute | solution.py:539
  10.1 0.0 copy-start.5
  10.1 1.2 %project.2.refs_4_ = f32[16,128]{1,0:T(8,128)S(1)} custom-call(bf16[2,1,6144]{2,1,0:T(2,128)(2,1)S(1)} %copy.15.refs_0_, bf16[2,72,6144]{2,1,0:T(8,128)(2,1)S(1)} %copy-done.2), custom_call_target="tpu_custom_call" | custom-call | flops 1200000000 | bytes 1048576 | tf_op jit(solution)/shard_map/project/pallas_call | solution.py:423
  11.4 1.0 %collective-permute-done.6 = bf16[2,6144]{1,0:T(2,128)(2,1)S(1)} collective-permute-done((bf16[2,6144]{1,0:T(2,128)(2,1)S(1)}, bf16[2,6144]{1,0:T(2,128)(2,1)S(1)}, u32[]{:S(2)}, u32[]{:S(2)}) %collective-permute-start.6) | collective-permute-done | bytes 24608 | tf_op jit(solution)/shard_map/ppermute | solution.py:539
  12.5 0.1 collective-permute-start.2
  12.5 0.1 pad_maximum_fusion.1
  12.7 0.0 copy-start.6
  12.7 0.0 copy-start.7
  12.7 2.7 %collective-permute-start.7 = (bf16[2,2,6144]{2,1,0:T(2,128)(2,1)S(1)}, bf16[2,2,6144]{2,1,0:T(2,128)(2,1)S(1)}, u32[]{:S(2)}, u32[]{:S(2)}) collective-permute-start(bf16[2,2,6144]{2,1,0:T(2,128)(2,1)S(1)} %pad_maximum_fusion.1), channel_id=1, source_target_pairs={{0,4},{1,5},{2,6},{3,7},{4,0},{5,1},{6,2},{7,3},{8,12},{9,13},{10,... | collective-permute-start | bytes 147464 | tf_op jit(solution)/shard_map/ppermute | solution.py:539
  15.4 35.7 %lattice.1 = (bf16[208,128]{1,0:T(8,128)(2,1)S(1)}, bf16[208,128]{1,0:T(8,128)(2,1)S(1)}, bf16[208,128]{1,0:T(8,128)(2,1)S(1)}, bf16[208,128]{1,0:T(8,128)(2,1)S(1)}) custom-call(bf16[400,128]{1,0:T(8,128)(2,1)S(1)} %get-tuple-element.17.refs_0_, bf16[400,128]{1,0:T(8,128)(2,1)S(1)} %collective-permute-done.refs_1_, ...), custom_call_target="tpu_custom_call" | custom-call | flops 35999997952 | bytes 1048576 | tf_op jit(solution)/shard_map/lattice/pallas_call | solution.py:373
  51.1 0.1 pad_maximum_fusion.refs_0_
  51.2 1.6 %collective-permute-start.8 = (bf16[2,4,6144]{2,1,0:T(4,128)(2,1)S(1)}, bf16[2,4,6144]{2,1,0:T(4,128)(2,1)S(1)}, u32[]{:S(2)}, u32[]{:S(2)}) collective-permute-start(bf16[2,4,6144]{2,1,0:T(4,128)(2,1)S(1)} %pad_maximum_fusion.refs_0_), channel_id=1, source_target_pairs={{0,2},{1,3},{2,0},{3,1},{4,6},{5,7},{6,4},{7,5},{8,10},{9,11},{10,... | collective-permute-start | bytes 294920 | tf_op jit(solution)/shard_map/ppermute | solution.py:539
  52.8 0.1 copy.18
  53.0 0.1 copy.19
  53.1 0.1 broadcast_multiply_fusion.1
  53.2 0.1 mul.37
  53.3 0.1 mul.40
  53.4 0.1 collective-permute-start.3
  53.5 0.7 %collective-permute-start.4 = (bf16[208,128]{1,0:T(8,128)(2,1)S(1)}, bf16[208,128]{1,0:T(8,128)(2,1)S(1)}, u32[]{:S(2)}, u32[]{:S(2)}) collective-permute-start(bf16[208,128]{1,0:T(8,128)(2,1)S(1)} %get-tuple-element.21), channel_id=1, source_target_pairs={{0,16},{8,24},{16,0},{24,8},{1,17},{9,25},{17,1},{25,9},{2,18},{10... | collective-permute-start | bytes 159752 | tf_op jit(solution)/shard_map/ppermute | solution.py:539
  54.3 1.1 %collective-permute-start.5 = (bf16[208,128]{1,0:T(8,128)(2,1)S(1)}, bf16[208,128]{1,0:T(8,128)(2,1)S(1)}, u32[]{:S(2)}, u32[]{:S(2)}) collective-permute-start(bf16[208,128]{1,0:T(8,128)(2,1)S(1)} %get-tuple-element.22), channel_id=1, source_target_pairs={{0,24},{8,16},{16,8},{24,0},{1,25},{9,17},{17,9},{25,1},{2,26},{10... | collective-permute-start | bytes 159752 | tf_op jit(solution)/shard_map/ppermute | solution.py:539
  55.4 0.7 %collective-permute-done.8.refs_1_ = bf16[2,4,6144]{2,1,0:T(4,128)(2,1)S(1)} collective-permute-done((bf16[2,4,6144]{2,1,0:T(4,128)(2,1)S(1)}, bf16[2,4,6144]{2,1,0:T(4,128)(2,1)S(1)}, u32[]{:S(2)}, u32[]{:S(2)}) %collective-permute-start.8) | collective-permute-done | bytes 98336 | tf_op jit(solution)/shard_map/ppermute | solution.py:539
  56.1 1.2 %project.3.refs_0_ = f32[16,128]{1,0:T(8,128)S(1)} custom-call(bf16[2,4,6144]{2,1,0:T(4,128)(2,1)S(1)} %pad_maximum_fusion.refs_0_, bf16[2,4,6144]{2,1,0:T(4,128)(2,1)S(1)} %collective-permute-done.8.refs_1_, bf16[2,72,6144]{2,1,0:T(8,128)(2,1)S(1)} %copy-done.2), custom_call_target="tpu_custom_call" | custom-call | flops 1200000000 | bytes 1048576 | tf_op jit(solution)/shard_map/project/pallas_call | solution.py:423
  57.3 0.8 %collective-permute-start.10 = (f32[16,128]{1,0:T(8,128)S(1)}, f32[16,128]{1,0:T(8,128)S(1)}, u32[]{:S(2)}, u32[]{:S(2)}) collective-permute-start(f32[16,128]{1,0:T(8,128)S(1)} %project.3.refs_0_), channel_id=1, source_target_pairs={{0,16},{8,24},{16,0},{24,8},{1,17},{9,25},{17,1},{25,9},{2,18},{10... | collective-permute-start | bytes 24584 | tf_op jit(solution)/shard_map/ppermute | solution.py:539
  58.2 0.2 collective-permute-start.11
  58.4 1.2 %collective-permute-start.9 = (f32[16,128]{1,0:T(8,128)S(1)}, f32[16,128]{1,0:T(8,128)S(1)}, u32[]{:S(2)}, u32[]{:S(2)}) collective-permute-start(f32[16,128]{1,0:T(8,128)S(1)} %project.3.refs_0_), channel_id=1, source_target_pairs={{0,8},{8,0},{16,24},{24,16},{1,9},{9,1},{17,25},{25,17},{2,10},{10... | collective-permute-start | bytes 24584 | tf_op jit(solution)/shard_map/ppermute | solution.py:539
  59.6 2.1 %finish.1 = (bf16[2,6144]{1,0:T(2,128)(2,1)}, bf16[2,6144]{1,0:T(2,128)(2,1)}) custom-call(bf16[208,128]{1,0:T(8,128)(2,1)S(1)} %get-tuple-element.19.refs_0_, bf16[208,128]{1,0:T(8,128)(2,1)S(1)} %collective-permute-done.3.refs_1_, bf16[208,128]{1,0:T(8,128)(2,1)S(1)} %collective-permute-done.4.refs_2_, ...), custom_call_target="tpu_custom_call" | custom-call | flops 2100000000 | bytes 1048576 | tf_op jit(solution)/shard_map/finish/pallas_call | solution.py:486
  61.7 0.8 %gram_row.1 = f32[2,8]{1,0:T(2,128)} custom-call(f32[16,128]{1,0:T(8,128)S(1)} %project.3.refs_0_, f32[16,128]{1,0:T(8,128)S(1)} %collective-permute-done.9.refs_1_, f32[16,128]{1,0:T(8,128)S(1)} %collective-permute-done.10.refs_2_, f32[16,128]{1,0:T(8,128)S(1)} %collective-permute-done.11.refs_3_, f32[128,256]{1,0:T(8,128)S(1)} %select_maximum_fusion.refs_8_.refs_4_), custom_call_target="tpu_custom_call" | custom-call | flops 700000000 | bytes 1048576 | tf_op jit(solution)/shard_map/gram_row/pallas_call | solution.py:528
  (26 shorter events, 0.2 us)
Async XLA Ops:
  0.6 0.7 %copy-start = (bf16[2,1,6144]{2,0,1:T(2,128)(2,1)S(1)}, bf16[2,1,6144]{2,0,1:T(2,128)(2,1)}, u32[]{:S(2)}) copy-start(bf16[2,1,6144]{2,0,1:T(2,128)(2,1)} %param.7) | copy-start | bytes 73732
  1.4 0.7 %copy-start.3 = (s32[6144]{0:T(1024)S(1)}, s32[6144]{0:T(1024)}, u32[]{:S(2)}) copy-start(s32[6144]{0:T(1024)} %param.8) | copy-start | bytes 73732
  2.1 8.0 %copy-start.2 = (bf16[2,72,6144]{2,1,0:T(8,128)(2,1)S(1)}, bf16[2,72,6144]{2,1,0:T(8,128)(2,1)}, u32[]{:S(2)}) copy-start(bf16[2,72,6144]{2,1,0:T(8,128)(2,1)} %refs_2_.1) | copy-start | bytes 5308420
  5.5 6.9 %collective-permute-start.1 = (bf16[400,128]{1,0:T(8,128)(2,1)S(1)}, bf16[400,128]{1,0:T(8,128)(2,1)S(1)}, u32[]{:S(2)}, u32[]{:S(2)}) collective-permute-start(bf16[400,128]{1,0:T(8,128)(2,1)S(1)} %get-tuple-element.17.refs_0_), channel_id=1, source_target_pairs={{0,16},{8,24},{16,0},{24,8},{1,17},{9,25},{17,1},{25,9},{2,18},{10... | collective-permute-start | bytes 307208 | tf_op jit(solution)/shard_map/ppermute | solution.py:539
  8.6 6.8 %collective-permute-start = (bf16[400,128]{1,0:T(8,128)(2,1)S(1)}, bf16[400,128]{1,0:T(8,128)(2,1)S(1)}, u32[]{:S(2)}, u32[]{:S(2)}) collective-permute-start(bf16[400,128]{1,0:T(8,128)(2,1)S(1)} %get-tuple-element.17.refs_0_), channel_id=1, source_target_pairs={{0,8},{8,0},{16,24},{24,16},{1,9},{9,1},{17,25},{25,17},{2,10},{10... | collective-permute-start | bytes 307208 | tf_op jit(solution)/shard_map/ppermute | solution.py:539
  8.6 3.8 %collective-permute-start.6 = (bf16[2,6144]{1,0:T(2,128)(2,1)S(1)}, bf16[2,6144]{1,0:T(2,128)(2,1)S(1)}, u32[]{:S(2)}, u32[]{:S(2)}) collective-permute-start(bf16[2,6144]{1,0:T(2,128)(2,1)S(1)} %bitcast.12), channel_id=1, source_target_pairs={{0,1},{1,0},{2,3},{3,2},{4,5},{5,4},{6,7},{7,6},{8,9},{9,8},{10,11... | collective-permute-start | bytes 73736 | tf_op jit(solution)/shard_map/ppermute | solution.py:539
  10.1 5.2 %copy-start.5 = (bf16[2176,256]{1,0:T(8,128)(2,1)S(1)}, bf16[2176,256]{1,0:T(8,128)(2,1)}, u32[]{:S(2)}) copy-start(bf16[2176,256]{1,0:T(8,128)(2,1)} %constant.5.clone.refs_6_) | copy-start | bytes 3342340
  12.5 2.9 %collective-permute-start.2 = (bf16[400,128]{1,0:T(8,128)(2,1)S(1)}, bf16[400,128]{1,0:T(8,128)(2,1)S(1)}, u32[]{:S(2)}, u32[]{:S(2)}) collective-permute-start(bf16[400,128]{1,0:T(8,128)(2,1)S(1)} %collective-permute-done.1.refs_2_), channel_id=1, source_target_pairs={{0,8},{8,0},{16,24},{24,16},{1,9},{9,1},{17,25},{25,17},{2,10},{10... | collective-permute-start | bytes 307208 | tf_op jit(solution)/shard_map/ppermute | solution.py:539
  12.7 40.2 %copy-start.6 = (f32[4,18,18]{2,0,1:T(4,128)S(1)}, f32[4,18,18]{2,0,1:T(4,128)}, u32[]{:S(2)}) copy-start(f32[4,18,18]{2,0,1:T(4,128)} %param.11) | copy-start | bytes 15556
  12.7 40.3 %copy-start.7 = (f32[4,18,18]{2,0,1:T(4,128)S(1)}, f32[4,18,18]{2,0,1:T(4,128)}, u32[]{:S(2)}) copy-start(f32[4,18,18]{2,0,1:T(4,128)} %param.12) | copy-start | bytes 15556
  12.7 38.4 %collective-permute-start.7 = (bf16[2,2,6144]{2,1,0:T(2,128)(2,1)S(1)}, bf16[2,2,6144]{2,1,0:T(2,128)(2,1)S(1)}, u32[]{:S(2)}, u32[]{:S(2)}) collective-permute-start(bf16[2,2,6144]{2,1,0:T(2,128)(2,1)S(1)} %pad_maximum_fusion.1), channel_id=1, source_target_pairs={{0,4},{1,5},{2,6},{3,7},{4,0},{5,1},{6,2},{7,3},{8,12},{9,13},{10,... | collective-permute-start | bytes 147464 | tf_op jit(solution)/shard_map/ppermute | solution.py:539
  51.2 4.9 %collective-permute-start.8 = (bf16[2,4,6144]{2,1,0:T(4,128)(2,1)S(1)}, bf16[2,4,6144]{2,1,0:T(4,128)(2,1)S(1)}, u32[]{:S(2)}, u32[]{:S(2)}) collective-permute-start(bf16[2,4,6144]{2,1,0:T(4,128)(2,1)S(1)} %pad_maximum_fusion.refs_0_), channel_id=1, source_target_pairs={{0,2},{1,3},{2,0},{3,1},{4,6},{5,7},{6,4},{7,5},{8,10},{9,11},{10,... | collective-permute-start | bytes 294920 | tf_op jit(solution)/shard_map/ppermute | solution.py:539
  53.4 5.0 %collective-permute-start.3 = (bf16[208,128]{1,0:T(8,128)(2,1)S(1)}, bf16[208,128]{1,0:T(8,128)(2,1)S(1)}, u32[]{:S(2)}, u32[]{:S(2)}) collective-permute-start(bf16[208,128]{1,0:T(8,128)(2,1)S(1)} %get-tuple-element.20), channel_id=1, source_target_pairs={{0,8},{8,0},{16,24},{24,16},{1,9},{9,1},{17,25},{25,17},{2,10},{10... | collective-permute-start | bytes 159752 | tf_op jit(solution)/shard_map/ppermute | solution.py:539
  53.5 6.0 %collective-permute-start.4 = (bf16[208,128]{1,0:T(8,128)(2,1)S(1)}, bf16[208,128]{1,0:T(8,128)(2,1)S(1)}, u32[]{:S(2)}, u32[]{:S(2)}) collective-permute-start(bf16[208,128]{1,0:T(8,128)(2,1)S(1)} %get-tuple-element.21), channel_id=1, source_target_pairs={{0,16},{8,24},{16,0},{24,8},{1,17},{9,25},{17,1},{25,9},{2,18},{10... | collective-permute-start | bytes 159752 | tf_op jit(solution)/shard_map/ppermute | solution.py:539
  54.3 5.3 %collective-permute-start.5 = (bf16[208,128]{1,0:T(8,128)(2,1)S(1)}, bf16[208,128]{1,0:T(8,128)(2,1)S(1)}, u32[]{:S(2)}, u32[]{:S(2)}) collective-permute-start(bf16[208,128]{1,0:T(8,128)(2,1)S(1)} %get-tuple-element.22), channel_id=1, source_target_pairs={{0,24},{8,16},{16,8},{24,0},{1,25},{9,17},{17,9},{25,1},{2,26},{10... | collective-permute-start | bytes 159752 | tf_op jit(solution)/shard_map/ppermute | solution.py:539
  55.4 4.2 %copy-start.1 = (bf16[2,1,6144]{2,0,1:T(2,128)(2,1)S(1)}, bf16[2,1,6144]{2,0,1:T(2,128)(2,1)}, u32[]{:S(2)}) copy-start(bf16[2,1,6144]{2,0,1:T(2,128)(2,1)} %param.7) | copy-start | bytes 73732
  55.4 4.2 %copy-start.4 = (s32[6144]{0:T(1024)S(1)}, s32[6144]{0:T(1024)}, u32[]{:S(2)}) copy-start(s32[6144]{0:T(1024)} %param.8) | copy-start | bytes 73732
  57.3 4.4 %collective-permute-start.10 = (f32[16,128]{1,0:T(8,128)S(1)}, f32[16,128]{1,0:T(8,128)S(1)}, u32[]{:S(2)}, u32[]{:S(2)}) collective-permute-start(f32[16,128]{1,0:T(8,128)S(1)} %project.3.refs_0_), channel_id=1, source_target_pairs={{0,16},{8,24},{16,0},{24,8},{1,17},{9,25},{17,1},{25,9},{2,18},{10... | collective-permute-start | bytes 24584 | tf_op jit(solution)/shard_map/ppermute | solution.py:539
  58.2 3.5 %collective-permute-start.11 = (f32[16,128]{1,0:T(8,128)S(1)}, f32[16,128]{1,0:T(8,128)S(1)}, u32[]{:S(2)}, u32[]{:S(2)}) collective-permute-start(f32[16,128]{1,0:T(8,128)S(1)} %project.3.refs_0_), channel_id=1, source_target_pairs={{0,24},{8,16},{16,8},{24,0},{1,25},{9,17},{17,9},{25,1},{2,26},{10... | collective-permute-start | bytes 24584 | tf_op jit(solution)/shard_map/ppermute | solution.py:539
  58.4 3.3 %collective-permute-start.9 = (f32[16,128]{1,0:T(8,128)S(1)}, f32[16,128]{1,0:T(8,128)S(1)}, u32[]{:S(2)}, u32[]{:S(2)}) collective-permute-start(f32[16,128]{1,0:T(8,128)S(1)} %project.3.refs_0_), channel_id=1, source_target_pairs={{0,8},{8,0},{16,24},{24,16},{1,9},{9,1},{17,25},{25,17},{2,10},{10... | collective-permute-start | bytes 24584 | tf_op jit(solution)/shard_map/ppermute | solution.py:539
